TPU v7x, 32 devices: a whole 2x2x4 slice. The times are simulated.
32 devices in a mesh: dp: 8 (over y, x, core), ctx: 4 (over z).
Axes of the slice: x: 2, y: 2, z: 4, core: 2. Of those that a mesh axis runs over, the one named last changes fastest.
Arguments:
- layer_input: bfloat16 [8, 512, 1024], P('dp', 'ctx'), may hold values from -6 to 6
- projected: bfloat16 [8, 512, 3072], P('dp', 'ctx'), may hold values from -6 to 6
- grad_output: bfloat16 [8, 512, 1024], P('dp', 'ctx'), may hold values from -12 to 12
- w_qkv: bfloat16 [1024, 3072], P('dp', 'ctx'), may hold values from -0.1875 to 0.1875
- lengths: int32 [8, 8], P('dp'), may hold values from 1 to 256, 512 in all within a row
- block_perm: int32 [8, 4], P('dp'), may hold values from 0 to 3, each once within a row
Outputs:
- grad_input: bfloat16 [8, 512, 1024], P('dp', 'ctx')
- grad_weight: float32 [1024, 3072], P('dp', 'ctx')
Inputs may be any that keep to these rules, and one draw needn't show every extreme that they name: Every row of lengths sums to 512 and has an entry equal to 256. Every row of block_perm names each of the 4 blocks once; slot block s holds packed positions block_perm[g, s] * 128 to block_perm[g, s] * 128 + 127.
All inputs are finite; a program needn't handle non-finite values.
Results may differ from a plain program's by a relative error of at most 0.0065.
Values may be sent and summed in bfloat16 or wider, within the bound.
No kernel may reach another device: no remote copies, remote signals or barrier semaphores. Data moves between devices by JAX's collectives and lax.ppermute only.
A program may use at most 64 MiB of HBM per device.

v0:
```python
import jax
import jax.numpy as jnp
from jax import lax
from jax.sharding import PartitionSpec as P

DH = 64


def silu_slope(value):
    sigma = jax.nn.sigmoid(value)
    return sigma * (1.0 + value * (1.0 - sigma))


def slot_positions(slot_blocks, rows, block_size):
    slots = jnp.arange(rows, dtype=jnp.int32)
    owner = (slots // block_size)[:, None] == jnp.arange(slot_blocks.shape[0], dtype=jnp.int32)[
        None, :
    ]
    placed = jnp.sum(jnp.where(owner, slot_blocks[None, :], 0), axis=1)
    return placed * block_size + slots % block_size


def user_layout(user_lengths, position):
    ends = jnp.cumsum(user_lengths)
    segment = jnp.sum((position[:, None] >= ends[None, :]).astype(jnp.int32), axis=1)
    member = segment[:, None] == jnp.arange(user_lengths.shape[0], dtype=jnp.int32)[None, :]
    user_len = jnp.sum(jnp.where(member, user_lengths[None, :], 0), axis=1)
    first_row = jnp.sum(jnp.where(member, (ends - user_lengths)[None, :], 0), axis=1)
    row_scale = lax.rsqrt(user_len.astype(jnp.float32))
    return (segment, row_scale, first_row)


def tile_grads(
    query_block,
    grad_block,
    position_block,
    segment_block,
    scale_block,
    key_block,
    value_block,
    key_position,
    key_segment,
):
    scale = DH ** (-0.5)
    contract = (((1,), (1,)), ((), ()))
    across = (((0,), (0,)), ((), ()))
    scores = (
        lax.dot_general(query_block, key_block, contract, preferred_element_type=jnp.float32)
        * scale
    )
    visible = (segment_block[:, None] == key_segment[None, :]) & (
        key_position[None, :] <= position_block[:, None]
    )
    sigma = jax.nn.sigmoid(scores)
    weights = jnp.where(visible, scores * sigma * scale_block[:, None], 0.0).astype(jnp.bfloat16)
    grad_weights = lax.dot_general(
        grad_block, value_block, contract, preferred_element_type=jnp.float32
    )
    slope = grad_weights * sigma * (1.0 + scores * (1.0 - sigma)) * (scale_block[:, None] * scale)
    grad_scores = jnp.where(visible, slope, 0.0).astype(jnp.bfloat16)
    grad_query = jnp.dot(grad_scores, key_block, preferred_element_type=jnp.float32)
    grad_key = lax.dot_general(grad_scores, query_block, across, preferred_element_type=jnp.float32)
    grad_value = lax.dot_general(weights, grad_block, across, preferred_element_type=jnp.float32)
    return (grad_query, grad_key, grad_value)


def dense_grads(
    query_rows, key_rows, value_rows, grad_rows, position, segment, row_scale, block_rows
):
    whole = query_rows.shape[0]
    count = whole // block_rows

    def blocked(array):
        return array.reshape((count, block_rows) + array.shape[1:])

    def step(carry, block_item):
        query_block, grad_block, position_block, segment_block, scale_block = block_item
        grad_query, grad_key, grad_value = tile_grads(
            query_block,
            grad_block,
            position_block,
            segment_block,
            scale_block,
            key_rows,
            value_rows,
            position,
            segment,
        )
        return ((carry[0] + grad_key, carry[1] + grad_value), grad_query)

    empty = jnp.zeros((whole, DH), jnp.float32)
    sums, grad_query = lax.scan(
        step,
        (empty, empty),
        (
            blocked(query_rows),
            blocked(grad_rows),
            blocked(position),
            blocked(segment),
            blocked(row_scale),
        ),
    )
    return (grad_query.reshape(whole, DH), sums[0], sums[1])


def body(layer_input, projected, grad_output, w_qkv, lengths, block_perm):
    tokens_dev = layer_input.shape[1]
    width = layer_input.shape[2]
    ctx_count = lax.axis_size("ctx")
    data_count = lax.axis_size("dp")
    whole = tokens_dev * ctx_count
    local_heads = width // DH // ctx_count
    columns = local_heads * 3 * DH
    user_lengths = lengths[0]
    slot_blocks = block_perm[0]
    block_size = whole // slot_blocks.shape[0]
    block_rows = min(512, whole)
    position = slot_positions(slot_blocks, whole, block_size)
    segment, row_scale, first_row = user_layout(user_lengths, position)
    contract_cols = (((1,), (1,)), ((), ()))

    def one_head(pre_head, grad_head):
        active = jax.nn.silu(pre_head.astype(jnp.float32)).astype(jnp.bfloat16)
        query_rows = active[:, :DH]
        key_rows = active[:, DH : 2 * DH]
        value_rows = active[:, 2 * DH :]
        grad_query, grad_key, grad_value = dense_grads(
            query_rows, key_rows, value_rows, grad_head, position, segment, row_scale, block_rows
        )
        grads = jnp.concatenate([grad_query, grad_key, grad_value], axis=1)
        return (grads * silu_slope(pre_head.astype(jnp.float32))).astype(jnp.bfloat16)

    pre_split = projected[0].reshape(tokens_dev, ctx_count, local_heads, 3 * DH)
    grad_split = grad_output[0].reshape(tokens_dev, ctx_count, local_heads, DH)
    pre_pieces = lax.all_to_all(pre_split, "ctx", split_axis=1, concat_axis=0, tiled=True)
    grad_pieces = lax.all_to_all(grad_split, "ctx", split_axis=1, concat_axis=0, tiled=True)
    grad_pre = jax.vmap(one_head, in_axes=(1, 1), out_axes=1)(pre_pieces[:, 0], grad_pieces[:, 0])
    flat_grad = grad_pre.reshape(whole, columns)
    weight_local = lax.dot_general(
        lax.all_gather(layer_input, "ctx", axis=1, tiled=True)[0],
        flat_grad,
        (((0,), (0,)), ((), ())),
        preferred_element_type=jnp.float32,
    )
    grad_weight = lax.psum_scatter(weight_local, "dp", scatter_dimension=0, tiled=True) * (
        1.0 / data_count
    )
    head_band = lax.all_gather(w_qkv, "dp", axis=0, tiled=True)
    partial_rows = lax.dot_general(
        flat_grad, head_band, contract_cols, preferred_element_type=jnp.float32
    ).astype(jnp.bfloat16)
    arrived = lax.all_to_all(
        partial_rows.reshape(ctx_count, tokens_dev, width),
        "ctx",
        split_axis=0,
        concat_axis=0,
        tiled=True,
    )
    input_grad = jnp.sum(arrived.astype(jnp.float32), axis=0)
    return (input_grad.astype(jnp.bfloat16)[None], grad_weight)


def solution(mesh):
    return jax.shard_map(
        body,
        mesh=mesh,
        in_specs=(
            P("dp", "ctx", None),
            P("dp", "ctx", None),
            P("dp", "ctx", None),
            P("dp", "ctx"),
            P("dp", None),
            P("dp", None),
        ),
        out_specs=(P("dp", "ctx", None), P("dp", "ctx")),
        check_vma=False,
    )
```

profile of v0, /device:TPU:18, one launch (start us, length us, event | category | flops | bytes accessed | tf_op | source)
XLA Modules:
  0.0 136.9 jit_solution(15091118931478296629)
XLA Ops:
  7.2 0.0 all-gather.5.cloned.1.call-start
  7.2 0.7 all-gather.5.cloned.1.call-update
  7.9 0.0 copy-start.2
  7.9 0.0 copy-start.1
  7.9 1.8 %copy.26 = bf16[1,128,1024]{1,2,0:T(8,128)(2,1)} copy(bf16[1,128,1024]{2,1,0:T(8,128)(2,1)} %param.8) | data formatting | bytes 524288 | tf_op args[2]
  9.7 5.2 %all-to-all-start.1 = ((bf16[128,4,4,64]{0,3,2,1:T(8,128)(2,1)}), bf16[128,4,4,64]{0,3,2,1:T(8,128)(2,1)S(1)}, u32[]{:S(2)}, u32[]{:S(2)}) async-start(bf16[128,4,4,64]{0,3,2,1:T(8,128)(2,1)} %bitcast.7), calls=%async_computation.1 | async-start | bytes 524288 | tf_op jit(solution)/shard_map/all_to_all | solution.py:136
  14.9 2.3 %copy.24 = bf16[1,128,3072]{1,2,0:T(8,128)(2,1)} copy(bf16[1,128,3072]{2,1,0:T(8,128)(2,1)} %param.7) | data formatting | bytes 1572864 | tf_op args[1]
  17.2 6.5 %all-to-all-done.1 = bf16[128,4,4,64]{0,3,2,1:T(8,128)(2,1)S(1)} async-done(((bf16[128,4,4,64]{0,3,2,1:T(8,128)(2,1)}), bf16[128,4,4,64]{0,3,2,1:T(8,128)(2,1)S(1)}, u32[]{:S(2)}, u32[]{:S(2)}) %all-to-all-start.1) | async-done | bytes 262176 | tf_op jit(solution)/shard_map/all_to_all | solution.py:136
  23.7 8.7 %all-to-all-start = ((bf16[128,4,4,192]{0,3,2,1:T(8,128)(2,1)}), bf16[128,4,4,192]{0,3,2,1:T(8,128)(2,1)S(1)}, u32[]{:S(2)}, u32[]{:S(2)}) async-start(bf16[128,4,4,192]{0,3,2,1:T(8,128)(2,1)} %bitcast.3), calls=%async_computation | async-start | bytes 1572864 | tf_op jit(solution)/shard_map/all_to_all | solution.py:135
  32.4 0.0 all-gather.3.cloned.1.call-start
  32.4 0.7 all-gather.3.cloned.1.call-update
  33.2 0.0 reduce-scatter.2.cloned.1.call-start
  33.2 0.0 copy-done.2
  33.2 0.2 reduce-window.8
  33.4 0.0 copy-done.1
  33.4 0.1 select_reduce_fusion.1
  33.5 0.1 convert_reduce_fusion
  33.6 0.1 select_reduce_fusion
  33.7 0.3 compare_and_fusion
  34.0 0.2 copy.27
  34.2 0.8 squeeze.25
  35.0 19.3 %all-to-all-done = bf16[128,4,4,192]{0,3,2,1:T(8,128)(2,1)S(1)} async-done(((bf16[128,4,4,192]{0,3,2,1:T(8,128)(2,1)}), bf16[128,4,4,192]{0,3,2,1:T(8,128)(2,1)S(1)}, u32[]{:S(2)}, u32[]{:S(2)}) %all-to-all-start) | async-done | bytes 786464 | tf_op jit(solution)/shard_map/all_to_all | solution.py:135
  54.3 0.1 convert_bitcast_fusion
  54.4 1.0 copy.25
  55.4 0.6 reshape.115
  56.1 0.4 multiply_convert_fusion
  56.5 0.0 copy-start
  56.5 0.8 fusion.10
  57.3 0.2 copy-done
  57.5 2.5 %fusion.3 = bf16[4,512,512]{1,2,0:T(8,128)(2,1)S(1)} fusion(f32[4,512,512]{1,2,0:T(8,128)S(1)} %fusion.10, f32[512]{0:T(512)S(1)} %get-tuple-element.34, pred[512,512]{0,1:T(8,128)(4,1)S(1)} %compare_and_fusion, bf16[512,4,192]{0,2,1:T(8,128)(2,1)S(1)} %multiply_convert_fusion, bf16[512,4,64]{0,2,1:T(8,128)(2,1)S(1)} %copy-done), kind=kOutput, calls=%fused_computation.4 | convolution fusion | flops 146800640 | bytes 7079936 | tf_op jit(solution)/shard_map/vmap()/while/body/eval_jaxpr/dot_general | solution.py:56
  59.9 0.7 fusion.11
  60.7 0.5 fusion.9
  61.2 1.5 %fusion.4 = f32[4,512,64]{1,2,0:T(8,128)S(1)} fusion(f32[4,512,512]{1,2,0:T(8,128)S(1)} %fusion.10, f32[512]{0:T(512)S(1)} %get-tuple-element.35, pred[512,512]{0,1:T(8,128)(4,1)S(1)} %compare_and_fusion, bf16[512,4,64]{0,2,1:T(8,128)(2,1)S(1)} %copy-done), kind=kOutput, calls=%fused_computation.7 | convolution fusion | flops 142606336 | bytes 5244928 | tf_op jit(solution)/shard_map/vmap()/while/body/eval_jaxpr/dot_general | solution.py:63
  62.7 0.6 fusion.5
  63.3 0.0 all-gather.5.cloned.1.call-done
  63.3 3.9 %convolution_bitcast_fusion = f32[1024,768]{0,1:T(8,128)} fusion(bf16[512,768]{0,1:T(8,128)(2,1)S(1)} %bitcast.61, bf16[1,512,1024]{2,1,0:T(8,128)(2,1)} %all-gather.5.cloned.1.call-done), kind=kOutput, calls=%fused_computation.8 | convolution fusion | flops 805306368 | bytes 4980736 | tf_op jit(solution)/shard_map/dot_general | solution.py:139
  67.2 0.0 reduce-scatter.2.cloned.1.call-update
  67.2 11.6 %all-gather.3.cloned.1.call-done = bf16[1024,768]{1,0:T(8,128)(2,1)} async-done(((bf16[128,768]{1,0:T(8,128)(2,1)}), bf16[1024,768]{1,0:T(8,128)(2,1)}) %all-gather.3.cloned.1.call-update) | async-done | bytes 1572880 | tf_op jit(solution)/shard_map/all_gather | solution.py:148
  78.8 2.4 %convolution_convert_fusion = bf16[512,1024]{1,0:T(8,128)(2,1)S(1)} fusion(bf16[512,768]{0,1:T(8,128)(2,1)S(1)} %bitcast.62, bf16[1024,768]{1,0:T(8,128)(2,1)} %all-gather.3.cloned.1.call-done), kind=kOutput, calls=%fused_computation.14 | convolution fusion | flops 805830656 | bytes 3407872 | tf_op jit(solution)/shard_map/dot_general | solution.py:149
  81.3 28.4 %all_to_all.29 = bf16[4,128,1024]{2,1,0:T(8,128)(2,1)S(1)} all-to-all(bf16[4,128,1024]{2,1,0:T(8,128)(2,1)S(1)} %bitcast.63), channel_id=1, replica_groups=mesh['dp'=8,'ctx'=4] {'ctx'}, dimensions={0} | all-to-all | bytes 2097152 | tf_op jit(solution)/shard_map/all_to_all | solution.py:152
  109.6 0.9 reduce_sum.42
  110.6 17.9 %reduce-scatter.2.cloned.1.call-done = f32[128,768]{0,1:T(8,128)} async-done(((f32[1024,768]{0,1:T(8,128)}), f32[128,768]{0,1:T(8,128)}) %reduce-scatter.2.cloned.1.call-update) | async-done | bytes 393232 | tf_op jit(solution)/shard_map/reduce_scatter | solution.py:145
  128.4 1.0 broadcast_multiply_fusion
  129.5 0.9 copy.32
  (3 shorter events, 0.0 us)
Async XLA Ops:
  7.2 56.2 %all-gather.5.cloned.1.call-start = ((), (), s32[]{:S(2)}) async-start(), calls=%async_computation.5 | async-start | bytes 1310720 | tf_op jit(solution)/shard_map/all_gather | solution.py:140
  7.9 25.3 %copy-start.2 = (s32[1,8]{1,0:T(1,128)S(1)}, s32[1,8]{1,0:T(1,128)}, u32[]{:S(2)}) copy-start(s32[1,8]{1,0:T(1,128)} %param.10) | copy-start | bytes 100
  7.9 25.5 %copy-start.1 = (s32[1,4]{1,0:T(1,128)S(1)}, s32[1,4]{1,0:T(1,128)}, u32[]{:S(2)}) copy-start(s32[1,4]{1,0:T(1,128)} %param.11) | copy-start | bytes 52
  9.7 14.0 %all-to-all-start.1 = ((bf16[128,4,4,64]{0,3,2,1:T(8,128)(2,1)}), bf16[128,4,4,64]{0,3,2,1:T(8,128)(2,1)S(1)}, u32[]{:S(2)}, u32[]{:S(2)}) async-start(bf16[128,4,4,64]{0,3,2,1:T(8,128)(2,1)} %bitcast.7), calls=%async_computation.1 | async-start | bytes 524288 | tf_op jit(solution)/shard_map/all_to_all | solution.py:136
  23.7 30.5 %all-to-all-start = ((bf16[128,4,4,192]{0,3,2,1:T(8,128)(2,1)}), bf16[128,4,4,192]{0,3,2,1:T(8,128)(2,1)S(1)}, u32[]{:S(2)}, u32[]{:S(2)}) async-start(bf16[128,4,4,192]{0,3,2,1:T(8,128)(2,1)} %bitcast.3), calls=%async_computation | async-start | bytes 1572864 | tf_op jit(solution)/shard_map/all_to_all | solution.py:135
  32.4 46.4 %all-gather.3.cloned.1.call-start = ((), (), s32[]{:S(2)}) async-start(), calls=%async_computation.4 | async-start | bytes 1769472 | tf_op jit(solution)/shard_map/all_gather | solution.py:148
  33.2 95.3 %reduce-scatter.2.cloned.1.call-start = ((), (), s32[]{:S(2)}) async-start(), calls=%async_computation.6 | async-start | bytes 3538944 | tf_op jit(solution)/shard_map/reduce_scatter | solution.py:145
  56.5 1.0 copy-start
Sparse Core Ops, SparseCore 0:
  9.6 37.6 all-gather.4
  49.1 29.6 all-gather.2
  82.2 46.1 reduce-scatter.1
where the time goes:
time: 139 us; the launch traced here: 137 us
  waiting for transfers between devices  56.7 us (41%)
  blocking collectives  28.4 us (20%)
  starting transfers between devices  14 us (10%)
  between operations  13.9 us (10%)
  matrix products  12.3 us (9%)
  local copies, waits for them, and re-layouts  7.85 us (6%)
  other arithmetic  3.85 us (3%)
    all_to_all x1, blocking collectives, body(): lax.all_to_all(partial_rows.reshape(ctx_count, tokens_dev, width), 'ctx',...  28.4 us
    all_to_all x1, waiting for transfers between devices, body(): lax.all_to_all(pre_split, 'ctx', split_axis=1, concat_axis=0, tiled=True)  19.3 us
    reduce_scatter x1, waiting for transfers between devices, body(): lax.psum_scatter(weight_local, 'dp', scatter_dimension=0, tiled=True)  17.9 us
    all_gather x1, waiting for transfers between devices, body(): head_band = lax.all_gather(w_qkv, 'dp', axis=0, tiled=True)  11.6 us
    all_to_all x1, starting transfers between devices, body(): lax.all_to_all(pre_split, 'ctx', split_axis=1, concat_axis=0, tiled=True)  8.7 us
    all_to_all x1, waiting for transfers between devices, body(): lax.all_to_all(grad_split, 'ctx', split_axis=1, concat_axis=0, tiled=True)  6.53 us
    all_to_all x1, starting transfers between devices, body(): lax.all_to_all(grad_split, 'ctx', split_axis=1, concat_axis=0, tiled=True)  5.2 us
    unnamed x9, local copies, waits for them, and re-layouts  5.19 us
  transfers between devices with their start and end apart: 5, of which 4 were waited for; matrix products, arithmetic and copies ran while one was open for 16% of the time, Pallas kernels for 0%

commit v1 on v0

v1 whole, which is shorter than its diff:
```python
import jax
import jax.numpy as jnp
from jax import lax
from jax.experimental import pallas as pl
from jax.experimental.pallas import tpu as pltpu
from jax.sharding import PartitionSpec as P

DH = 64
VMEM_BYTES = 48 * 1024 * 1024
BY_ROWS = (((0,), (0,)), ((), ()))
BY_COLS = (((1,), (1,)), ((), ()))


def dot(a, b, dims):
    return lax.dot_general(a, b, dims, preferred_element_type=jnp.float32)


def in_vmem():
    return pl.BlockSpec(memory_space=pltpu.VMEM)


def in_smem():
    return pl.BlockSpec(memory_space=pltpu.SMEM)


def call(kernel, scalars, arrays, outs, scratch=(), flops=0):
    size = sum(a.size * a.dtype.itemsize for a in arrays) + sum(
        o.size * o.dtype.itemsize for o in outs
    )
    return pl.pallas_call(
        kernel,
        out_shape=list(outs),
        in_specs=[in_smem()] * len(scalars) + [in_vmem()] * len(arrays),
        out_specs=[in_vmem()] * len(outs),
        scratch_shapes=list(scratch),
        compiler_params=pltpu.CompilerParams(vmem_limit_bytes=VMEM_BYTES),
        cost_estimate=pl.CostEstimate(flops=flops, bytes_accessed=size, transcendentals=0),
    )(*scalars, *arrays)


def bf16(*shape):
    return jax.ShapeDtypeStruct(shape, jnp.bfloat16)


def f32(*shape):
    return jax.ShapeDtypeStruct(shape, jnp.float32)


def swap(array, axis, mask):
    count = lax.axis_size(axis)
    return lax.ppermute(array, axis, [(i, i ^ mask) for i in range(count)])


def gather(array, axis):
    held, mask = {0: array}, lax.axis_size(axis) // 2
    while mask:
        for near in sorted(held):
            held[near ^ mask] = swap(held[near], axis, mask)
        mask //= 2
    return [held[r] for r in sorted(held)]


def pack(ctx_index, pre, grad, ctx_count, parts, heads):
    rows = pre.shape[0]
    wide, narrow = heads * 3 * DH, heads * DH
    if wide % 128 or narrow % 128:
        both = jnp.concatenate(
            [
                pre.reshape(rows, ctx_count, parts, wide),
                grad.reshape(rows, ctx_count, parts, narrow),
            ],
            axis=3,
        ).transpose(1, 2, 0, 3)
        owners = [lax.dynamic_index_in_dim(both, ctx_index ^ r, 0, False) for r in range(ctx_count)]
        return [[owner[part] for owner in owners] for part in range(parts)]

    def kernel(me_ref, pre_ref, grad_ref, *out_refs):
        for part in range(parts):
            for r in range(ctx_count):
                owner = (me_ref[0] ^ r) * parts + part
                out = out_refs[part * ctx_count + r]
                out[:, :wide] = pre_ref[:, pl.ds(pl.multiple_of(owner * wide, 128), wide)]
                out[:, wide:] = grad_ref[:, pl.ds(pl.multiple_of(owner * narrow, 128), narrow)]

    outs = call(
        kernel,
        [ctx_index[None]],
        [pre, grad],
        [bf16(rows, wide + narrow)] * (parts * ctx_count),
    )
    return [outs[part * ctx_count : (part + 1) * ctx_count] for part in range(parts)]


def head_grads(lengths_ref, act, pre, out_ref, heads, rows, blocks, column):
    whole = rows * blocks
    place = lax.broadcasted_iota(jnp.int32, (8, whole), 1)
    first = jnp.zeros((8, whole), jnp.int32)
    length = jnp.zeros((8, whole), jnp.int32)
    start = jnp.int32(0)
    for user in range(lengths_ref.shape[1]):
        inside = place >= start
        first = jnp.where(inside, start, first)
        length = jnp.where(inside, lengths_ref[0, user], length)
        start = start + lengths_ref[0, user]
    scale = lax.rsqrt(length.astype(jnp.float32))[:1]
    first = first[:1]
    grad_q = [[None] * blocks for _ in range(heads)]
    for j in range(blocks):
        lo = j * rows
        count = whole - lo
        key_place = lax.broadcasted_iota(jnp.int32, (rows, count), 0)
        query_place = lax.broadcasted_iota(jnp.int32, (rows, count), 1)
        visible = (query_place >= key_place) & (key_place + lo >= first[:, lo:])
        scales = jnp.where(visible, scale[:, lo:], 0.0)
        for h in range(heads):
            base = h * 3 * DH
            query = act[lo:, base : base + DH]
            key = act[lo : lo + rows, base + DH : base + 2 * DH]
            value = act[lo : lo + rows, base + 2 * DH : base + 3 * DH]
            grad = act[lo:, heads * 3 * DH + h * DH : heads * 3 * DH + (h + 1) * DH]
            u = dot(key, query, BY_COLS)
            gw = dot(value, grad, BY_COLS)
            t = jnp.tanh(u)
            a = scales + scales * t
            weights = (u * a).astype(jnp.bfloat16)
            slope = (gw * a * (1.0 + (u - u * t))).astype(jnp.bfloat16)
            grad_v = dot(weights, grad, (((1,), (0,)), ((), ())))
            grad_k = dot(slope, query, (((1,), (0,)), ((), ())))
            add_q = dot(slope, key, BY_ROWS)
            for i in range(j, blocks):
                term = add_q[(i - j) * rows : (i - j + 1) * rows]
                grad_q[h][i] = term if j == 0 else grad_q[h][i] + term
            for part, value_grad in ((1, grad_k), (2, grad_v), (0, grad_q[h][j])):
                at = base + part * DH
                z = pre[lo : lo + rows, at : at + DH].astype(jnp.float32)
                s = 0.5 + 0.5 * jnp.tanh(0.5 * z)
                factor = s * (1.0 + z * (1.0 - s))
                if part == 0:
                    factor = factor * 0.0625
                out_ref[lo : lo + rows, column + at : column + at + DH] = (
                    value_grad * factor
                ).astype(jnp.bfloat16)


def load_pieces(perm_ref, me, piece_refs, pre, act, heads, rows):
    wide = heads * 3 * DH
    for r, piece in enumerate(piece_refs):
        at = pl.ds(pl.multiple_of(perm_ref[0, me ^ r] * rows, rows), rows)
        value = piece[...]
        pre[at, :] = value[:, :wide]
        z = value[:, :wide].astype(jnp.float32)
        active = (z * (0.5 + 0.5 * jnp.tanh(0.5 * z))).astype(jnp.bfloat16)
        column = lax.broadcasted_iota(jnp.int32, active.shape, 1) % (3 * DH)
        act[at, :wide] = jnp.where(column < DH, active * jnp.bfloat16(0.0625), active)
        act[at, wide:] = value[:, wide:]


def body(layer_input, projected, grad_output, w_qkv, lengths, block_perm):
    rows, width = layer_input.shape[1:]
    ctx_count, dp_count = lax.axis_size("ctx"), lax.axis_size("dp")
    me_ctx, me_dp = lax.axis_index("ctx"), lax.axis_index("dp")
    whole = rows * ctx_count
    local_heads = width // DH // ctx_count
    parts = 2 if local_heads % 4 == 0 else 1
    heads = local_heads // parts
    wide = heads * 3 * DH
    columns = parts * wide
    w_rows = w_qkv.shape[0]
    part_flops = 10 * heads * whole * whole * DH
    product_flops = 2 * whole * columns * width

    pieces = pack(me_ctx, projected[0], grad_output[0], ctx_count, parts, heads)
    arrived = [
        [pieces[part][0]]
        + [swap(pieces[part][r], "ctx", r) for r in range(1, ctx_count)]
        for part in range(parts)
    ]
    weights = gather(w_qkv, "dp")
    tokens = gather(layer_input[0], "ctx")

    scratch = [
        pltpu.VMEM((whole, wide), jnp.bfloat16),
        pltpu.VMEM((whole, wide + heads * DH), jnp.bfloat16),
    ]

    def attention(lengths_ref, perm_ref, me_ref, *refs):
        piece_refs, (out, pre, act) = refs[:ctx_count], refs[ctx_count:]
        load_pieces(perm_ref, me_ref[0], piece_refs, pre, act, heads, rows)
        head_grads(lengths_ref, act, pre, out, heads, rows, ctx_count, 0)

    scalars = [lengths, block_perm, jnp.stack([me_ctx, me_dp])]
    grad_pre = [
        call(attention, scalars, arrived[part], [bf16(whole, wide)], scratch, part_flops)[0]
        for part in range(parts)
    ]

    def input_terms(perm_ref, me_ref, *refs):
        grads = refs[:parts]
        bands = refs[parts : parts + dp_count]
        outs = refs[parts + dp_count : parts + dp_count + ctx_count]
        band = refs[-1]
        for r in range(dp_count):
            band[pl.ds(pl.multiple_of((me_ref[1] ^ r) * w_rows, w_rows), w_rows), :] = bands[r][...]
        for r in range(ctx_count):
            at = pl.ds(pl.multiple_of(perm_ref[0, me_ref[0] ^ r] * rows, rows), rows)
            total = None
            for part in range(parts):
                term = dot(grads[part][at, :], band[:, part * wide : (part + 1) * wide], BY_COLS)
                total = term if total is None else total + term
            outs[r][...] = total.astype(jnp.bfloat16)

    terms = call(
        input_terms,
        scalars[1:],
        grad_pre + weights,
        [bf16(rows, width)] * ctx_count,
        [pltpu.VMEM((width, columns), jnp.bfloat16)],
        product_flops,
    )
    returned = [terms[0]] + [swap(terms[r], "ctx", r) for r in range(1, ctx_count)]

    def weight_terms(perm_ref, me_ref, *refs):
        grads = refs[:parts]
        token_refs = refs[parts : parts + ctx_count]
        keep, send, held = refs[parts + ctx_count :]
        for r in range(ctx_count):
            at = pl.ds(pl.multiple_of(perm_ref[0, me_ref[0] ^ r] * rows, rows), rows)
            held[at, :] = token_refs[r][...]
        for part in range(parts):
            total = dot(held[...], grads[part][...], BY_ROWS)
            keep[:, part * wide : (part + 1) * wide] = total
        for r in range(0, dp_count, 2):
            at = pl.ds(pl.multiple_of((me_ref[1] ^ r ^ 1) * w_rows, w_rows), w_rows)
            send[r // 2] = keep[at, :].astype(jnp.bfloat16)

    keep, send = call(
        weight_terms,
        scalars[1:],
        grad_pre + tokens,
        [f32(width, columns), bf16(dp_count // 2, w_rows, columns)],
        [pltpu.VMEM((whole, width), jnp.bfloat16)],
        product_flops,
    )
    other = swap(send, "dp", 1)

    def chip_terms(me_ref, keep_ref, other_ref, own, *outs):
        for r in range(0, dp_count, 2):
            at = pl.ds(pl.multiple_of((me_ref[1] ^ r) * w_rows, w_rows), w_rows)
            total = keep_ref[at, :] + other_ref[r // 2].astype(jnp.float32)
            if r == 0:
                own[...] = total
            else:
                outs[r // 2 - 1][...] = total.astype(jnp.bfloat16)

    own, *outgoing = call(
        chip_terms,
        scalars[2:],
        [keep, other],
        [f32(w_rows, columns)] + [bf16(w_rows, columns)] * (dp_count // 2 - 1),
    )
    incoming = [swap(block, "dp", 2 * (i + 1)) for i, block in enumerate(outgoing)]
    total = own
    for block in incoming:
        total = total + block.astype(jnp.float32)
    grad_weight = total * (1.0 / dp_count)
    input_grad = returned[0].astype(jnp.float32)
    for block in returned[1:]:
        input_grad = input_grad + block.astype(jnp.float32)
    return (input_grad.astype(jnp.bfloat16)[None], grad_weight)


def solution(mesh):
    return jax.shard_map(
        body,
        mesh=mesh,
        in_specs=(
            P("dp", "ctx", None),
            P("dp", "ctx", None),
            P("dp", "ctx", None),
            P("dp", "ctx"),
            P("dp", None),
            P("dp", None),
        ),
        out_specs=(P("dp", "ctx", None), P("dp", "ctx")),
        check_vma=False,
    )
```

time: 139 us -> 88.3 us (0.64); the launches traced: 137 us -> 88.1 us
  blocking collectives: 28.4 us -> 0 us
  between operations: 13.9 us -> 0.76 us
  matrix products: 12.3 us -> 0 us
  Pallas kernels: 0 us -> 12.2 us
  waiting for transfers between devices: 56.7 us -> 45.9 us
  starting transfers between devices: 14 us -> 24.1 us
  local copies, waits for them, and re-layouts: 7.85 us -> 3.41 us
  other arithmetic: 3.85 us -> 1.8 us
    ppermute x0 -> x23, waiting for transfers between devices: none -> 45.9 us  [swap(): return lax.ppermute(array, axis, [(i, i ^ mask) for i in range(count)])]
    all_to_all x1 -> x0, blocking collectives: 28.4 us -> none  [body(): lax.all_to_all(partial_rows.reshape(ctx_count, tokens_dev, width), 'ctx',...]
    all_to_all x2 -> x0, waiting for transfers between devices: 25.8 us -> none  [the longest x1 19.3 us: body(): lax.all_to_all(pre_split, 'ctx', split_axis=1, concat_axis=0, tiled=True)]
    ppermute x0 -> x23, starting transfers between devices: none -> 24.1 us  [swap(): return lax.ppermute(array, axis, [(i, i ^ mask) for i in range(count)])]
    reduce_scatter x1 -> x0, waiting for transfers between devices: 17.9 us -> none  [body(): lax.psum_scatter(weight_local, 'dp', scatter_dimension=0, tiled=True)]
    all_to_all x2 -> x0, starting transfers between devices: 13.9 us -> none  [the longest x1 8.7 us: body(): lax.all_to_all(pre_split, 'ctx', split_axis=1, concat_axis=0, tiled=True)]
    dot_general x7 -> x0, matrix products: 12.3 us -> none  [the longest x1 3.87 us: body(): lax.dot_general(lax.all_gather(layer_input, 'ctx', axis=1, tiled=True)[0]...]
    pallas_call x0 -> x6, Pallas kernels: none -> 12.2 us  [call(): pl.pallas_call(kernel, out_shape=list(outs), in_specs=[in_smem()] * len(s...]
  transfers between devices with their start and end apart: 5 -> 23, of which waited for: 4 -> 11; matrix products, arithmetic and copies ran while one was open for 16% -> 1% of each run, Pallas kernels for 0% -> 14%
where the time goes in v1:
time: 88.3 us; the launch traced here: 88.1 us
  waiting for transfers between devices  45.9 us (52%)
  starting transfers between devices  24.1 us (27%)
  Pallas kernels  12.2 us (14%)
  local copies, waits for them, and re-layouts  3.41 us (4%)
  other arithmetic  1.8 us (2%)
    ppermute x23, waiting for transfers between devices, swap(): return lax.ppermute(array, axis, [(i, i ^ mask) for i in range(count)])  45.9 us
    ppermute x23, starting transfers between devices, swap(): return lax.ppermute(array, axis, [(i, i ^ mask) for i in range(count)])  24.1 us
    pallas_call x6, Pallas kernels, call(): pl.pallas_call(kernel, out_shape=list(outs), in_specs=[in_smem()] * len(s...  12.2 us
    unnamed x14, local copies, waits for them, and re-layouts  3.41 us
  transfers between devices with their start and end apart: 23, of which 11 were waited for; matrix products, arithmetic and copies ran while one was open for 1% of the time, Pallas kernels for 14%

profile of v1, /device:TPU:18, one launch (start us, length us, event | category | flops | bytes accessed | tf_op | source)
XLA Modules:
  0.0 88.1 jit_solution(3971611717778346020)
XLA Ops:
  0.6 0.0 copy-start.6
  0.6 0.4 collective-permute-start.17
  1.0 1.1 %copy-done = bf16[1,128,3072]{2,1,0:T(8,128)(2,1)S(1)} copy-done((bf16[1,128,3072]{2,1,0:T(8,128)(2,1)S(1)}, bf16[1,128,3072]{2,1,0:T(8,128)(2,1)}, u32[]{:S(2)}) %copy-start) | copy-done | bytes 786456
  2.2 0.9 %copy-done.1 = bf16[1,128,1024]{2,1,0:T(8,128)(2,1)S(1)} copy-done((bf16[1,128,1024]{2,1,0:T(8,128)(2,1)S(1)}, bf16[1,128,1024]{2,1,0:T(8,128)(2,1)}, u32[]{:S(2)}) %copy-start.1) | copy-done | bytes 262168
  3.1 0.2 shard_map.77
  3.3 1.6 %collective-permute-start.3 = (bf16[128,512]{1,0:T(8,128)(2,1)S(1)}, bf16[128,512]{1,0:T(8,128)(2,1)S(1)}, u32[]{:S(2)}, u32[]{:S(2)}) collective-permute-start(bf16[128,512]{1,0:T(8,128)(2,1)S(1)} %get-tuple-element.25), channel_id=1, source_target_pairs={{0,1},{1,0},{2,3},{3,2},{4,5},{5,4},{6,7},{7,6},{8,9},{9,8},{10,11... | collective-permute-start | bytes 393224 | tf_op jit(solution)/shard_map/ppermute | solution.py:51
  4.9 2.6 %collective-permute-start.4 = (bf16[128,512]{1,0:T(8,128)(2,1)S(1)}, bf16[128,512]{1,0:T(8,128)(2,1)S(1)}, u32[]{:S(2)}, u32[]{:S(2)}) collective-permute-start(bf16[128,512]{1,0:T(8,128)(2,1)S(1)} %get-tuple-element.26), channel_id=1, source_target_pairs={{0,2},{1,3},{2,0},{3,1},{4,6},{5,7},{6,4},{7,5},{8,10},{9,11},{10,... | collective-permute-start | bytes 393224 | tf_op jit(solution)/shard_map/ppermute | solution.py:51
  7.5 1.8 %collective-permute-start = (bf16[128,512]{1,0:T(8,128)(2,1)S(1)}, bf16[128,512]{1,0:T(8,128)(2,1)S(1)}, u32[]{:S(2)}, u32[]{:S(2)}) collective-permute-start(bf16[128,512]{1,0:T(8,128)(2,1)S(1)} %get-tuple-element.21), channel_id=1, source_target_pairs={{0,1},{1,0},{2,3},{3,2},{4,5},{5,4},{6,7},{7,6},{8,9},{9,8},{10,11... | collective-permute-start | bytes 393224 | tf_op jit(solution)/shard_map/ppermute | solution.py:51
  9.3 3.5 %collective-permute-done.3.refs_1_ = bf16[128,512]{1,0:T(8,128)(2,1)S(1)} collective-permute-done((bf16[128,512]{1,0:T(8,128)(2,1)S(1)}, bf16[128,512]{1,0:T(8,128)(2,1)S(1)}, u32[]{:S(2)}, u32[]{:S(2)}) %collective-permute-start.3) | collective-permute-done | bytes 131104 | tf_op jit(solution)/shard_map/ppermute | solution.py:51
  12.8 0.0 collective-permute-start.16
  12.8 6.5 %collective-permute-done.17.refs_4_ = bf16[128,1024]{1,0:T(8,128)(2,1)S(1)} collective-permute-done((bf16[128,1024]{1,0:T(8,128)(2,1)}, bf16[128,1024]{1,0:T(8,128)(2,1)S(1)}, u32[]{:S(2)}, u32[]{:S(2)}) %collective-permute-start.17) | collective-permute-done | bytes 262176 | tf_op jit(solution)/shard_map/ppermute | solution.py:51
  19.3 3.4 %collective-permute-start.18 = (bf16[128,1024]{1,0:T(8,128)(2,1)S(1)}, bf16[128,1024]{1,0:T(8,128)(2,1)S(1)}, u32[]{:S(2)}, u32[]{:S(2)}) collective-permute-start(bf16[128,1024]{1,0:T(8,128)(2,1)S(1)} %collective-permute-done.17.refs_4_), channel_id=1, source_target_pairs={{0,1},{1,0},{2,3},{3,2},{4,5},{5,4},{6,7},{7,6},{8,9},{9,8},{10,11... | collective-permute-start | bytes 786440 | tf_op jit(solution)/shard_map/ppermute | solution.py:51
  22.8 0.0 collective-permute-done.4.refs_2_
  22.8 2.7 %collective-permute-start.1 = (bf16[128,512]{1,0:T(8,128)(2,1)S(1)}, bf16[128,512]{1,0:T(8,128)(2,1)S(1)}, u32[]{:S(2)}, u32[]{:S(2)}) collective-permute-start(bf16[128,512]{1,0:T(8,128)(2,1)S(1)} %get-tuple-element.22), channel_id=1, source_target_pairs={{0,2},{1,3},{2,0},{3,1},{4,6},{5,7},{6,4},{7,5},{8,10},{9,11},{10,... | collective-permute-start | bytes 393224 | tf_op jit(solution)/shard_map/ppermute | solution.py:51
  25.4 1.3 %collective-permute-done.5.refs_3_ = bf16[128,512]{1,0:T(8,128)(2,1)S(1)} collective-permute-done((bf16[128,512]{1,0:T(8,128)(2,1)S(1)}, bf16[128,512]{1,0:T(8,128)(2,1)S(1)}, u32[]{:S(2)}, u32[]{:S(2)}) %collective-permute-start.5) | collective-permute-done | bytes 131104 | tf_op jit(solution)/shard_map/ppermute | solution.py:51
  26.8 0.2 collective-permute-start.2
  27.0 0.0 collective-permute-done.refs_1_
  27.0 1.5 %collective-permute-start.9 = (bf16[128,768]{1,0:T(8,128)(2,1)}, bf16[128,768]{1,0:T(8,128)(2,1)S(1)}, u32[]{:S(2)}, u32[]{:S(2)}) collective-permute-start(bf16[128,768]{1,0:T(8,128)(2,1)} %refs_2_.1), channel_id=1, source_target_pairs={{0,16},{4,20},{8,24},{12,28},{16,0},{20,4},{24,8},{28,12},{1,17},{... | collective-permute-start | bytes 589832 | tf_op jit(solution)/shard_map/ppermute | solution.py:51
  28.5 0.1 pad_add_fusion.me_ref
  28.6 0.7 copy-done.4
  29.2 0.7 copy-done.5
  29.9 3.3 %shard_map.79.refs_1_ = bf16[512,384]{1,0:T(8,128)(2,1)S(1)} custom-call(s32[1,8]{1,0:T(1,128)S(1)} %copy-done.4, s32[1,4]{1,0:T(1,128)S(1)} %copy-done.5, s32[2]{0:T(128)S(1)} %pad_add_fusion.me_ref, bf16[128,512]{1,0:T(8,128)(2,1)S(1)} %get-tuple-element.24.refs_0_, bf16[128,512]{1,0:T(8,128)(2,1)S(1)} %collective-permute-done.3.refs_1_, ...), custom_call_target="tpu_custom_call" | custom-call | flops 335544320 | bytes 917504 | tf_op jit(solution)/shard_map/pallas_call | solution.py:30
  33.2 3.3 %collective-permute-done.1.refs_2_ = bf16[128,512]{1,0:T(8,128)(2,1)S(1)} collective-permute-done((bf16[128,512]{1,0:T(8,128)(2,1)S(1)}, bf16[128,512]{1,0:T(8,128)(2,1)S(1)}, u32[]{:S(2)}, u32[]{:S(2)}) %collective-permute-start.1) | collective-permute-done | bytes 131104 | tf_op jit(solution)/shard_map/ppermute | solution.py:51
  36.5 2.3 %collective-permute-done.2.refs_3_ = bf16[128,512]{1,0:T(8,128)(2,1)S(1)} collective-permute-done((bf16[128,512]{1,0:T(8,128)(2,1)S(1)}, bf16[128,512]{1,0:T(8,128)(2,1)S(1)}, u32[]{:S(2)}, u32[]{:S(2)}) %collective-permute-start.2) | collective-permute-done | bytes 131104 | tf_op jit(solution)/shard_map/ppermute | solution.py:51
  38.7 3.3 %shard_map.78.refs_0_ = bf16[512,384]{1,0:T(8,128)(2,1)S(1)} custom-call(s32[1,8]{1,0:T(1,128)S(1)} %copy-done.4, s32[1,4]{1,0:T(1,128)S(1)} %copy-done.5, s32[2]{0:T(128)S(1)} %pad_add_fusion.me_ref, bf16[128,512]{1,0:T(8,128)(2,1)S(1)} %get-tuple-element.20.refs_0_, bf16[128,512]{1,0:T(8,128)(2,1)S(1)} %collective-permute-done.refs_1_, ...), custom_call_target="tpu_custom_call" | custom-call | flops 335544320 | bytes 917504 | tf_op jit(solution)/shard_map/pallas_call | solution.py:30
  42.1 2.0 %shard_map.81 = (f32[1024,768]{1,0:T(8,128)S(1)}, bf16[4,128,768]{2,1,0:T(8,128)(2,1)S(1)}) custom-call(s32[1,4]{1,0:T(1,128)S(1)} %copy-done.6, s32[2]{0:T(128)S(1)} %pad_add_fusion.me_ref, bf16[512,384]{1,0:T(8,128)(2,1)S(1)} %shard_map.78.refs_0_, bf16[512,384]{1,0:T(8,128)(2,1)S(1)} %shard_map.79.refs_1_, bf16[128,1024]{1,0:T(8,128)(2,1)S(1)} %bitcast.11, ...), custom_call_target="tpu_custom_call" | custom-call | flops 805306368 | bytes 5767168 | tf_op jit(solution)/shard_map/pallas_call | solution.py:30
  44.1 0.1 collective-permute-start.19
  44.2 0.6 collective-permute-start.7
  44.8 1.5 %collective-permute-start.11 = (bf16[128,768]{1,0:T(8,128)(2,1)S(1)}, bf16[128,768]{1,0:T(8,128)(2,1)S(1)}, u32[]{:S(2)}, u32[]{:S(2)}) collective-permute-start(bf16[128,768]{1,0:T(8,128)(2,1)S(1)} %collective-permute-done.9.refs_6_), channel_id=1, source_target_pairs={{0,8},{4,12},{8,0},{12,4},{16,24},{20,28},{24,16},{28,20},{1,9},{5... | collective-permute-start | bytes 589832 | tf_op jit(solution)/shard_map/ppermute | solution.py:51
  46.3 0.0 collective-permute-start.6
  46.3 0.5 collective-permute-start.10
  46.8 5.2 %collective-permute-done.7.refs_4_ = bf16[128,768]{1,0:T(8,128)(2,1)S(1)} collective-permute-done((bf16[128,768]{1,0:T(8,128)(2,1)S(1)}, bf16[128,768]{1,0:T(8,128)(2,1)S(1)}, u32[]{:S(2)}, u32[]{:S(2)}) %collective-permute-start.7) | collective-permute-done | bytes 196640 | tf_op jit(solution)/shard_map/ppermute | solution.py:51
  52.0 3.7 %collective-permute-done.11.refs_8_ = bf16[128,768]{1,0:T(8,128)(2,1)S(1)} collective-permute-done((bf16[128,768]{1,0:T(8,128)(2,1)S(1)}, bf16[128,768]{1,0:T(8,128)(2,1)S(1)}, u32[]{:S(2)}, u32[]{:S(2)}) %collective-permute-start.11) | collective-permute-done | bytes 196640 | tf_op jit(solution)/shard_map/ppermute | solution.py:51
  55.7 0.0 collective-permute-start.12
  55.7 1.4 %collective-permute-done.12.refs_9_ = bf16[128,768]{1,0:T(8,128)(2,1)S(1)} collective-permute-done((bf16[128,768]{1,0:T(8,128)(2,1)S(1)}, bf16[128,768]{1,0:T(8,128)(2,1)S(1)}, u32[]{:S(2)}, u32[]{:S(2)}) %collective-permute-start.12) | collective-permute-done | bytes 196640 | tf_op jit(solution)/shard_map/ppermute | solution.py:51
  57.2 2.7 %shard_map.80 = (bf16[128,1024]{1,0:T(8,128)(2,1)S(1)}, bf16[128,1024]{1,0:T(8,128)(2,1)S(1)}, bf16[128,1024]{1,0:T(8,128)(2,1)S(1)}, bf16[128,1024]{1,0:T(8,128)(2,1)S(1)}) custom-call(s32[1,4]{1,0:T(1,128)S(1)} %copy-done.6, s32[2]{0:T(128)S(1)} %pad_add_fusion.me_ref, bf16[512,384]{1,0:T(8,128)(2,1)S(1)} %shard_map.78.refs_0_, ...), custom_call_target="tpu_custom_call" | custom-call | flops 805306368 | bytes 3407872 | tf_op jit(solution)/shard_map/pallas_call | solution.py:30
  59.9 1.0 %collective-permute-start.13 = (bf16[128,1024]{1,0:T(8,128)(2,1)S(1)}, bf16[128,1024]{1,0:T(8,128)(2,1)S(1)}, u32[]{:S(2)}, u32[]{:S(2)}) collective-permute-start(bf16[128,1024]{1,0:T(8,128)(2,1)S(1)} %get-tuple-element.29), channel_id=1, source_target_pairs={{0,1},{1,0},{2,3},{3,2},{4,5},{5,4},{6,7},{7,6},{8,9},{9,8},{10,11... | collective-permute-start | bytes 786440 | tf_op jit(solution)/shard_map/ppermute | solution.py:51
  60.9 0.6 collective-permute-start.14
  61.5 2.0 %collective-permute-start.15 = (bf16[128,1024]{1,0:T(8,128)(2,1)S(1)}, bf16[128,1024]{1,0:T(8,128)(2,1)S(1)}, u32[]{:S(2)}, u32[]{:S(2)}) collective-permute-start(bf16[128,1024]{1,0:T(8,128)(2,1)S(1)} %get-tuple-element.31), channel_id=1, source_target_pairs={{0,3},{1,2},{2,1},{3,0},{4,7},{5,6},{6,5},{7,4},{8,11},{9,10},{10,... | collective-permute-start | bytes 786440 | tf_op jit(solution)/shard_map/ppermute | solution.py:51
  63.5 0.7 shard_map.82
  64.2 0.6 collective-permute-start.20
  64.8 1.5 %collective-permute-start.21 = (bf16[128,768]{1,0:T(8,128)(2,1)S(1)}, bf16[128,768]{1,0:T(8,128)(2,1)S(1)}, u32[]{:S(2)}, u32[]{:S(2)}) collective-permute-start(bf16[128,768]{1,0:T(8,128)(2,1)S(1)} %get-tuple-element.36), channel_id=1, source_target_pairs={{0,16},{4,20},{8,24},{12,28},{16,0},{20,4},{24,8},{28,12},{1,17},{... | collective-permute-start | bytes 589832 | tf_op jit(solution)/shard_map/ppermute | solution.py:51
  66.3 4.5 %collective-permute-done.13 = bf16[128,1024]{1,0:T(8,128)(2,1)S(1)} collective-permute-done((bf16[128,1024]{1,0:T(8,128)(2,1)S(1)}, bf16[128,1024]{1,0:T(8,128)(2,1)S(1)}, u32[]{:S(2)}, u32[]{:S(2)}) %collective-permute-start.13) | collective-permute-done | bytes 262176 | tf_op jit(solution)/shard_map/ppermute | solution.py:51
  70.8 1.5 %collective-permute-start.22 = (bf16[128,768]{1,0:T(8,128)(2,1)S(1)}, bf16[128,768]{1,0:T(8,128)(2,1)S(1)}, u32[]{:S(2)}, u32[]{:S(2)}) collective-permute-start(bf16[128,768]{1,0:T(8,128)(2,1)S(1)} %get-tuple-element.37), channel_id=1, source_target_pairs={{0,24},{4,28},{8,16},{12,20},{16,8},{20,12},{24,0},{28,4},{1,25},{... | collective-permute-start | bytes 589832 | tf_op jit(solution)/shard_map/ppermute | solution.py:51
  72.3 7.2 %collective-permute-done.14 = bf16[128,1024]{1,0:T(8,128)(2,1)S(1)} collective-permute-done((bf16[128,1024]{1,0:T(8,128)(2,1)S(1)}, bf16[128,1024]{1,0:T(8,128)(2,1)S(1)}, u32[]{:S(2)}, u32[]{:S(2)}) %collective-permute-start.14) | collective-permute-done | bytes 262176 | tf_op jit(solution)/shard_map/ppermute | solution.py:51
  79.4 7.0 %collective-permute-done.15 = bf16[128,1024]{1,0:T(8,128)(2,1)S(1)} collective-permute-done((bf16[128,1024]{1,0:T(8,128)(2,1)S(1)}, bf16[128,1024]{1,0:T(8,128)(2,1)S(1)}, u32[]{:S(2)}, u32[]{:S(2)}) %collective-permute-start.15) | collective-permute-done | bytes 262176 | tf_op jit(solution)/shard_map/ppermute | solution.py:51
  86.4 0.9 fusion
  87.3 0.8 add_multiply_fusion
  (21 shorter events, 0.0 us)
Async XLA Ops:
  0.6 41.5 %copy-start.6 = (s32[1,4]{1,0:T(1,128)S(1)}, s32[1,4]{1,0:T(1,128)}, u32[]{:S(2)}) copy-start(s32[1,4]{1,0:T(1,128)} %perm_ref.7) | copy-start | bytes 52
  0.6 18.7 %collective-permute-start.17 = (bf16[128,1024]{1,0:T(8,128)(2,1)}, bf16[128,1024]{1,0:T(8,128)(2,1)S(1)}, u32[]{:S(2)}, u32[]{:S(2)}) collective-permute-start(bf16[128,1024]{1,0:T(8,128)(2,1)} %bitcast.9), channel_id=1, source_target_pairs={{0,2},{1,3},{2,0},{3,1},{4,6},{5,7},{6,4},{7,5},{8,10},{9,11},{10,... | collective-permute-start | bytes 786440 | tf_op jit(solution)/shard_map/ppermute | solution.py:51
  1.0 1.1 %copy-start = (bf16[1,128,3072]{2,1,0:T(8,128)(2,1)S(1)}, bf16[1,128,3072]{2,1,0:T(8,128)(2,1)}, u32[]{:S(2)}) copy-start(bf16[1,128,3072]{2,1,0:T(8,128)(2,1)} %param.7) | copy-start | bytes 2359300
  2.2 0.9 %copy-start.1 = (bf16[1,128,1024]{2,1,0:T(8,128)(2,1)S(1)}, bf16[1,128,1024]{2,1,0:T(8,128)(2,1)}, u32[]{:S(2)}) copy-start(bf16[1,128,1024]{2,1,0:T(8,128)(2,1)} %param.8) | copy-start | bytes 786436
  3.1 39.0 %copy-start.2 = (bf16[1,128,1024]{2,1,0:T(8,128)(2,1)S(1)}, bf16[1,128,1024]{2,1,0:T(8,128)(2,1)}, u32[]{:S(2)}) copy-start(bf16[1,128,1024]{2,1,0:T(8,128)(2,1)} %param.6) | copy-start | bytes 786436
  3.1 41.1 %copy-start.3 = (bf16[128,768]{1,0:T(8,128)(2,1)S(1)}, bf16[128,768]{1,0:T(8,128)(2,1)}, u32[]{:S(2)}) copy-start(bf16[128,768]{1,0:T(8,128)(2,1)} %refs_2_.1) | copy-start | bytes 589828
  3.3 9.5 %collective-permute-start.3 = (bf16[128,512]{1,0:T(8,128)(2,1)S(1)}, bf16[128,512]{1,0:T(8,128)(2,1)S(1)}, u32[]{:S(2)}, u32[]{:S(2)}) collective-permute-start(bf16[128,512]{1,0:T(8,128)(2,1)S(1)} %get-tuple-element.25), channel_id=1, source_target_pairs={{0,1},{1,0},{2,3},{3,2},{4,5},{5,4},{6,7},{7,6},{8,9},{9,8},{10,11... | collective-permute-start | bytes 393224 | tf_op jit(solution)/shard_map/ppermute | solution.py:51
  4.9 17.8 %collective-permute-start.4 = (bf16[128,512]{1,0:T(8,128)(2,1)S(1)}, bf16[128,512]{1,0:T(8,128)(2,1)S(1)}, u32[]{:S(2)}, u32[]{:S(2)}) collective-permute-start(bf16[128,512]{1,0:T(8,128)(2,1)S(1)} %get-tuple-element.26), channel_id=1, source_target_pairs={{0,2},{1,3},{2,0},{3,1},{4,6},{5,7},{6,4},{7,5},{8,10},{9,11},{10,... | collective-permute-start | bytes 393224 | tf_op jit(solution)/shard_map/ppermute | solution.py:51
  7.5 19.3 %collective-permute-start.5 = (bf16[128,512]{1,0:T(8,128)(2,1)S(1)}, bf16[128,512]{1,0:T(8,128)(2,1)S(1)}, u32[]{:S(2)}, u32[]{:S(2)}) collective-permute-start(bf16[128,512]{1,0:T(8,128)(2,1)S(1)} %get-tuple-element.27), channel_id=1, source_target_pairs={{0,3},{1,2},{2,1},{3,0},{4,7},{5,6},{6,5},{7,4},{8,11},{9,10},{10,... | collective-permute-start | bytes 393224 | tf_op jit(solution)/shard_map/ppermute | solution.py:51
  7.5 19.5 %collective-permute-start = (bf16[128,512]{1,0:T(8,128)(2,1)S(1)}, bf16[128,512]{1,0:T(8,128)(2,1)S(1)}, u32[]{:S(2)}, u32[]{:S(2)}) collective-permute-start(bf16[128,512]{1,0:T(8,128)(2,1)S(1)} %get-tuple-element.21), channel_id=1, source_target_pairs={{0,1},{1,0},{2,3},{3,2},{4,5},{5,4},{6,7},{7,6},{8,9},{9,8},{10,11... | collective-permute-start | bytes 393224 | tf_op jit(solution)/shard_map/ppermute | solution.py:51
  12.8 29.3 %collective-permute-start.16 = (bf16[128,1024]{1,0:T(8,128)(2,1)}, bf16[128,1024]{1,0:T(8,128)(2,1)S(1)}, u32[]{:S(2)}, u32[]{:S(2)}) collective-permute-start(bf16[128,1024]{1,0:T(8,128)(2,1)} %bitcast.10), channel_id=1, source_target_pairs={{0,1},{1,0},{2,3},{3,2},{4,5},{5,4},{6,7},{7,6},{8,9},{9,8},{10,11... | collective-permute-start | bytes 786440 | tf_op jit(solution)/shard_map/ppermute | solution.py:51
  19.3 22.7 %collective-permute-start.18 = (bf16[128,1024]{1,0:T(8,128)(2,1)S(1)}, bf16[128,1024]{1,0:T(8,128)(2,1)S(1)}, u32[]{:S(2)}, u32[]{:S(2)}) collective-permute-start(bf16[128,1024]{1,0:T(8,128)(2,1)S(1)} %collective-permute-done.17.refs_4_), channel_id=1, source_target_pairs={{0,1},{1,0},{2,3},{3,2},{4,5},{5,4},{6,7},{7,6},{8,9},{9,8},{10,11... | collective-permute-start | bytes 786440 | tf_op jit(solution)/shard_map/ppermute | solution.py:51
  22.8 13.7 %collective-permute-start.1 = (bf16[128,512]{1,0:T(8,128)(2,1)S(1)}, bf16[128,512]{1,0:T(8,128)(2,1)S(1)}, u32[]{:S(2)}, u32[]{:S(2)}) collective-permute-start(bf16[128,512]{1,0:T(8,128)(2,1)S(1)} %get-tuple-element.22), channel_id=1, source_target_pairs={{0,2},{1,3},{2,0},{3,1},{4,6},{5,7},{6,4},{7,5},{8,10},{9,11},{10,... | collective-permute-start | bytes 393224 | tf_op jit(solution)/shard_map/ppermute | solution.py:51
  26.8 12.0 %collective-permute-start.2 = (bf16[128,512]{1,0:T(8,128)(2,1)S(1)}, bf16[128,512]{1,0:T(8,128)(2,1)S(1)}, u32[]{:S(2)}, u32[]{:S(2)}) collective-permute-start(bf16[128,512]{1,0:T(8,128)(2,1)S(1)} %get-tuple-element.23), channel_id=1, source_target_pairs={{0,3},{1,2},{2,1},{3,0},{4,7},{5,6},{6,5},{7,4},{8,11},{9,10},{10,... | collective-permute-start | bytes 393224 | tf_op jit(solution)/shard_map/ppermute | solution.py:51
  27.0 17.8 %collective-permute-start.9 = (bf16[128,768]{1,0:T(8,128)(2,1)}, bf16[128,768]{1,0:T(8,128)(2,1)S(1)}, u32[]{:S(2)}, u32[]{:S(2)}) collective-permute-start(bf16[128,768]{1,0:T(8,128)(2,1)} %refs_2_.1), channel_id=1, source_target_pairs={{0,16},{4,20},{8,24},{12,28},{16,0},{20,4},{24,8},{28,12},{1,17},{... | collective-permute-start | bytes 589832 | tf_op jit(solution)/shard_map/ppermute | solution.py:51
  28.6 0.7 copy-start.4
  29.2 0.7 copy-start.5
  44.1 19.4 %collective-permute-start.19 = (bf16[4,128,768]{2,1,0:T(8,128)(2,1)S(1)}, bf16[4,128,768]{2,1,0:T(8,128)(2,1)S(1)}, u32[]{:S(2)}, u32[]{:S(2)}) collective-permute-start(bf16[4,128,768]{2,1,0:T(8,128)(2,1)S(1)} %get-tuple-element.33), channel_id=1, source_target_pairs={{0,4},{4,0},{8,12},{12,8},{16,20},{20,16},{24,28},{28,24},{1,5},{5... | collective-permute-start | bytes 2359304 | tf_op jit(solution)/shard_map/ppermute | solution.py:51
  44.2 7.8 %collective-permute-start.7 = (bf16[128,768]{1,0:T(8,128)(2,1)S(1)}, bf16[128,768]{1,0:T(8,128)(2,1)S(1)}, u32[]{:S(2)}, u32[]{:S(2)}) collective-permute-start(bf16[128,768]{1,0:T(8,128)(2,1)S(1)} %copy-done.3), channel_id=1, source_target_pairs={{0,8},{4,12},{8,0},{12,4},{16,24},{20,28},{24,16},{28,20},{1,9},{5... | collective-permute-start | bytes 589832 | tf_op jit(solution)/shard_map/ppermute | solution.py:51
  44.8 10.9 %collective-permute-start.11 = (bf16[128,768]{1,0:T(8,128)(2,1)S(1)}, bf16[128,768]{1,0:T(8,128)(2,1)S(1)}, u32[]{:S(2)}, u32[]{:S(2)}) collective-permute-start(bf16[128,768]{1,0:T(8,128)(2,1)S(1)} %collective-permute-done.9.refs_6_), channel_id=1, source_target_pairs={{0,8},{4,12},{8,0},{12,4},{16,24},{20,28},{24,16},{28,20},{1,9},{5... | collective-permute-start | bytes 589832 | tf_op jit(solution)/shard_map/ppermute | solution.py:51
  46.3 9.4 %collective-permute-start.6 = (bf16[128,768]{1,0:T(8,128)(2,1)S(1)}, bf16[128,768]{1,0:T(8,128)(2,1)S(1)}, u32[]{:S(2)}, u32[]{:S(2)}) collective-permute-start(bf16[128,768]{1,0:T(8,128)(2,1)S(1)} %copy-done.3), channel_id=1, source_target_pairs={{0,4},{4,0},{8,12},{12,8},{16,20},{20,16},{24,28},{28,24},{1,5},{5... | collective-permute-start | bytes 589832 | tf_op jit(solution)/shard_map/ppermute | solution.py:51
  46.3 9.4 %collective-permute-start.10 = (bf16[128,768]{1,0:T(8,128)(2,1)S(1)}, bf16[128,768]{1,0:T(8,128)(2,1)S(1)}, u32[]{:S(2)}, u32[]{:S(2)}) collective-permute-start(bf16[128,768]{1,0:T(8,128)(2,1)S(1)} %collective-permute-done.9.refs_6_), channel_id=1, source_target_pairs={{0,4},{4,0},{8,12},{12,8},{16,20},{20,16},{24,28},{28,24},{1,5},{5... | collective-permute-start | bytes 589832 | tf_op jit(solution)/shard_map/ppermute | solution.py:51
  52.0 3.8 %collective-permute-start.8 = (bf16[128,768]{1,0:T(8,128)(2,1)S(1)}, bf16[128,768]{1,0:T(8,128)(2,1)S(1)}, u32[]{:S(2)}, u32[]{:S(2)}) collective-permute-start(bf16[128,768]{1,0:T(8,128)(2,1)S(1)} %collective-permute-done.7.refs_4_), channel_id=1, source_target_pairs={{0,4},{4,0},{8,12},{12,8},{16,20},{20,16},{24,28},{28,24},{1,5},{5... | collective-permute-start | bytes 589832 | tf_op jit(solution)/shard_map/ppermute | solution.py:51
  55.7 1.4 %collective-permute-start.12 = (bf16[128,768]{1,0:T(8,128)(2,1)S(1)}, bf16[128,768]{1,0:T(8,128)(2,1)S(1)}, u32[]{:S(2)}, u32[]{:S(2)}) collective-permute-start(bf16[128,768]{1,0:T(8,128)(2,1)S(1)} %collective-permute-done.11.refs_8_), channel_id=1, source_target_pairs={{0,4},{4,0},{8,12},{12,8},{16,20},{20,16},{24,28},{28,24},{1,5},{5... | collective-permute-start | bytes 589832 | tf_op jit(solution)/shard_map/ppermute | solution.py:51
  59.9 10.9 %collective-permute-start.13 = (bf16[128,1024]{1,0:T(8,128)(2,1)S(1)}, bf16[128,1024]{1,0:T(8,128)(2,1)S(1)}, u32[]{:S(2)}, u32[]{:S(2)}) collective-permute-start(bf16[128,1024]{1,0:T(8,128)(2,1)S(1)} %get-tuple-element.29), channel_id=1, source_target_pairs={{0,1},{1,0},{2,3},{3,2},{4,5},{5,4},{6,7},{7,6},{8,9},{9,8},{10,11... | collective-permute-start | bytes 786440 | tf_op jit(solution)/shard_map/ppermute | solution.py:51
  60.9 18.5 %collective-permute-start.14 = (bf16[128,1024]{1,0:T(8,128)(2,1)S(1)}, bf16[128,1024]{1,0:T(8,128)(2,1)S(1)}, u32[]{:S(2)}, u32[]{:S(2)}) collective-permute-start(bf16[128,1024]{1,0:T(8,128)(2,1)S(1)} %get-tuple-element.30), channel_id=1, source_target_pairs={{0,2},{1,3},{2,0},{3,1},{4,6},{5,7},{6,4},{7,5},{8,10},{9,11},{10,... | collective-permute-start | bytes 786440 | tf_op jit(solution)/shard_map/ppermute | solution.py:51
  61.5 24.9 %collective-permute-start.15 = (bf16[128,1024]{1,0:T(8,128)(2,1)S(1)}, bf16[128,1024]{1,0:T(8,128)(2,1)S(1)}, u32[]{:S(2)}, u32[]{:S(2)}) collective-permute-start(bf16[128,1024]{1,0:T(8,128)(2,1)S(1)} %get-tuple-element.31), channel_id=1, source_target_pairs={{0,3},{1,2},{2,1},{3,0},{4,7},{5,6},{6,5},{7,4},{8,11},{9,10},{10,... | collective-permute-start | bytes 786440 | tf_op jit(solution)/shard_map/ppermute | solution.py:51
  64.2 23.1 %collective-permute-start.20 = (bf16[128,768]{1,0:T(8,128)(2,1)S(1)}, bf16[128,768]{1,0:T(8,128)(2,1)S(1)}, u32[]{:S(2)}, u32[]{:S(2)}) collective-permute-start(bf16[128,768]{1,0:T(8,128)(2,1)S(1)} %get-tuple-element.35), channel_id=1, source_target_pairs={{0,8},{4,12},{8,0},{12,4},{16,24},{20,28},{24,16},{28,20},{1,9},{5... | collective-permute-start | bytes 589832 | tf_op jit(solution)/shard_map/ppermute | solution.py:51
  64.8 22.5 %collective-permute-start.21 = (bf16[128,768]{1,0:T(8,128)(2,1)S(1)}, bf16[128,768]{1,0:T(8,128)(2,1)S(1)}, u32[]{:S(2)}, u32[]{:S(2)}) collective-permute-start(bf16[128,768]{1,0:T(8,128)(2,1)S(1)} %get-tuple-element.36), channel_id=1, source_target_pairs={{0,16},{4,20},{8,24},{12,28},{16,0},{20,4},{24,8},{28,12},{1,17},{... | collective-permute-start | bytes 589832 | tf_op jit(solution)/shard_map/ppermute | solution.py:51
  70.8 16.5 %collective-permute-start.22 = (bf16[128,768]{1,0:T(8,128)(2,1)S(1)}, bf16[128,768]{1,0:T(8,128)(2,1)S(1)}, u32[]{:S(2)}, u32[]{:S(2)}) collective-permute-start(bf16[128,768]{1,0:T(8,128)(2,1)S(1)} %get-tuple-element.37), channel_id=1, source_target_pairs={{0,24},{4,28},{8,16},{12,20},{16,8},{20,12},{24,0},{28,4},{1,25},{... | collective-permute-start | bytes 589832 | tf_op jit(solution)/shard_map/ppermute | solution.py:51

commit v2 on v1

v2 whole, which is shorter than its diff:
```python
import jax
import jax.numpy as jnp
from jax import lax
from jax.experimental import pallas as pl
from jax.experimental.pallas import tpu as pltpu
from jax.sharding import PartitionSpec as P

DH = 64
LANES = 128
VMEM_BYTES = 48 * 1024 * 1024
PLAIN = (((1,), (0,)), ((), ()))
BY_ROWS = (((0,), (0,)), ((), ()))
BY_COLS = (((1,), (1,)), ((), ()))


def dot(a, b, dims=PLAIN):
    return lax.dot_general(a, b, dims, preferred_element_type=jnp.float32)


def call(kernel, scalars, arrays, outs, scratch=(), flops=0, place=pltpu.VMEM):
    size = sum(a.size * a.dtype.itemsize for a in arrays) + sum(
        o.size * o.dtype.itemsize for o in outs
    )
    return pl.pallas_call(
        kernel,
        out_shape=list(outs),
        in_specs=[pl.BlockSpec(memory_space=pltpu.SMEM)] * len(scalars)
        + [pl.BlockSpec(memory_space=place)] * len(arrays),
        out_specs=[pl.BlockSpec(memory_space=pltpu.VMEM)] * len(outs),
        scratch_shapes=list(scratch),
        compiler_params=pltpu.CompilerParams(vmem_limit_bytes=VMEM_BYTES),
        cost_estimate=pl.CostEstimate(flops=flops, bytes_accessed=size, transcendentals=0),
    )(*scalars, *arrays)


def bf16(*shape):
    return jax.ShapeDtypeStruct(shape, jnp.bfloat16)


def f32(*shape):
    return jax.ShapeDtypeStruct(shape, jnp.float32)


def after(values, *others):
    return lax.optimization_barrier((values, others))[0]


def swap(array, axis, mask):
    count = lax.axis_size(axis)
    return lax.ppermute(array, axis, [(i, i ^ mask) for i in range(count)])


def row_block(index, rows):
    return pl.ds(pl.multiple_of(index * rows, rows), rows)


def pack(me, pre, grad, count):
    rows = pre.shape[0]
    wide, narrow = pre.shape[1] // count, grad.shape[1] // count
    if wide % LANES or narrow % LANES:
        both = jnp.concatenate(
            [pre.reshape(rows, count, wide), grad.reshape(rows, count, narrow)], axis=2
        ).transpose(1, 0, 2)
        return [lax.dynamic_index_in_dim(both, me ^ r, 0, False) for r in range(count)]

    def kernel(me_ref, pre_ref, grad_ref, *refs):
        outs, sems = refs[:count], refs[count]
        copies = []
        for r in range(count):
            owner = me_ref[0] ^ r
            for i, (ref, at, size) in enumerate(((pre_ref, 0, wide), (grad_ref, wide, narrow))):
                copies.append(
                    pltpu.make_async_copy(
                        ref.at[:, pl.ds(pl.multiple_of(owner * size, LANES), size)],
                        outs[r].at[:, pl.ds(at, size)],
                        sems.at[2 * r + i],
                    )
                )
        for copy in copies:
            copy.start()
        for copy in copies:
            copy.wait()

    return call(
        kernel,
        [me[None]],
        [pre, grad],
        [bf16(rows, wide + narrow)] * count,
        [pltpu.SemaphoreType.DMA((2 * count,))],
        place=pltpu.HBM,
    )


def pair_rows(me, own, other):
    rows = own.shape[0]

    def kernel(me_ref, own_ref, other_ref, out):
        core = me_ref[0] & 1
        out[row_block(core, rows), :] = own_ref[...]
        out[row_block(1 - core, rows), :] = other_ref[...]

    return call(kernel, [me[None]], [own, other], [bf16(2 * rows, own.shape[1])])[0]


def half_columns(me, tokens, count):
    rows, width = tokens.shape
    size = width // count
    if size % LANES:
        blocks = tokens.reshape(rows, count, size)
        return [
            jnp.concatenate(
                [lax.dynamic_index_in_dim(blocks, me ^ r, 1, False) for r in range(i, count, 2)],
                axis=1,
            )
            for i in range(2)
        ]

    def kernel(me_ref, tokens_ref, *outs):
        for r in range(count):
            owner = pl.multiple_of((me_ref[0] ^ r) * size, LANES)
            outs[r % 2][:, r // 2 * size : (r // 2 + 1) * size] = tokens_ref[:, pl.ds(owner, size)]

    return call(kernel, [me[None]], [tokens], [bf16(rows, width // 2)] * 2)


def user_rows(lengths, whole):
    place = lax.broadcasted_iota(jnp.int32, (8, whole), 1)
    first = jnp.zeros((8, whole), jnp.int32)
    length = jnp.zeros((8, whole), jnp.int32)
    start = jnp.int32(0)
    for size in lengths:
        inside = place >= start
        first = jnp.where(inside, start, first)
        length = jnp.where(inside, size, length)
        start = start + size
    return first[:1], lax.rsqrt(length.astype(jnp.float32))[:1]


def attention(perm, lengths, pieces, grad_pre, refs, heads, rows):
    blocks = len(pieces)
    whole = rows * blocks
    wide = heads * 3 * DH
    query_ref, key_ref, value_ref, grad_ref, factor_ref = refs
    for r, piece in enumerate(pieces):
        at = row_block(perm[r], rows)
        z = piece[:, :wide].astype(jnp.float32)
        s = 0.5 + 0.5 * jnp.tanh(0.5 * z)
        active = z * s
        factor_ref[r * rows : (r + 1) * rows, :] = s + active * (1.0 - s)
        active = active.astype(jnp.bfloat16)
        for h in range(heads):
            base = 3 * DH * h
            key = active[:, base + DH : base + 2 * DH]
            query_ref[h, at, :] = active[:, base : base + DH] * jnp.bfloat16(0.0625)
            key_ref[h, at, :] = key
            value_ref[h, at, :] = active[:, base + 2 * DH : base + 3 * DH]
            grad_ref[h, at, :] = piece[:, wide + h * DH : wide + (h + 1) * DH]
    first, scale = user_rows(lengths, whole)
    grad_q = [None] * heads
    for j in range(blocks):
        lo = j * rows
        count = whole - lo
        key_place = lax.broadcasted_iota(jnp.int32, (rows, count), 0)
        query_place = lax.broadcasted_iota(jnp.int32, (rows, count), 1)
        visible = (query_place >= key_place) & (key_place + lo >= first[:, lo:])
        scales = jnp.where(visible, scale[:, lo:], 0.0)
        slot = sum([jnp.where(perm[r] == j, r, 0) for r in range(blocks)])
        done = []
        for h in range(heads):
            query, grad = query_ref[h, lo:, :], grad_ref[h, lo:, :]
            u = dot(key_ref[h, lo : lo + rows, :], query, BY_COLS)
            gw = dot(value_ref[h, lo : lo + rows, :], grad, BY_COLS)
            t = jnp.tanh(u)
            a = scales + scales * t
            weights = (u * a).astype(jnp.bfloat16)
            slope = (gw * a * (1.0 + (u - u * t))).astype(jnp.bfloat16)
            add_q = dot(key_ref[h, lo : lo + rows, :].T, slope)
            total_q = add_q if j == 0 else grad_q[h] + add_q
            grad_q[h] = total_q[:, rows:]
            done += [total_q[:, :rows].T * 0.0625, dot(slope, query), dot(weights, grad)]
        at = row_block(slot, rows)
        grad_pre[at, :] = (jnp.concatenate(done, axis=1) * factor_ref[at, :]).astype(jnp.bfloat16)


def attention_scratch(heads, rows, blocks):
    whole = rows * blocks
    return [pltpu.VMEM((heads, whole, DH), jnp.bfloat16)] * 4 + [
        pltpu.VMEM((whole, heads * 3 * DH), jnp.float32),
    ]


def body(layer_input, projected, grad_output, w_qkv, lengths, block_perm):
    rows, width = layer_input.shape[1:]
    ctx_count, dp_count = lax.axis_size("ctx"), lax.axis_size("dp")
    me_ctx, me_dp = lax.axis_index("ctx"), lax.axis_index("dp")
    whole = rows * ctx_count
    heads = width // DH // ctx_count
    wide = heads * 3 * DH
    users = lengths.shape[1]
    w_rows = w_qkv.shape[0]
    chips = dp_count // 2
    product_flops = 2 * whole * wide * width

    pieces = pack(me_ctx, projected[0], grad_output[0], ctx_count)
    arrived = [pieces[0]] + [None] * (ctx_count - 1)
    for r in range(ctx_count - 1, 0, -1):
        arrived[r] = swap(pieces[r], "ctx", r)

    scalars = jnp.concatenate([me_ctx[None], me_dp[None], lengths[0], block_perm[0]])

    def perm_of(s_ref):
        return [s_ref[2 + users + (s_ref[0] ^ r)] for r in range(ctx_count)]

    pair = pair_rows(me_dp, w_qkv, swap(w_qkv, "dp", 1))
    pair = after(pair, pieces)
    pairs = [pair] + [swap(pair, "dp", 2 * r) for r in range(1, chips)]

    def main(s_ref, *refs):
        attention(
            perm_of(s_ref),
            [s_ref[2 + i] for i in range(users)],
            refs[:ctx_count],
            refs[ctx_count],
            refs[ctx_count + 1 :],
            heads,
            rows,
        )

    grad_pre = call(
        main,
        [scalars],
        arrived,
        [bf16(whole, wide)],
        attention_scratch(heads, rows, ctx_count),
        12 * product_flops,
    )[0]

    kept, sent = half_columns(me_dp, layer_input[0], dp_count)
    sent = after(sent, pieces)
    tokens, mask = {0: jnp.stack([kept, swap(sent, "dp", 1)])}, ctx_count // 2
    tokens[0] = after(tokens[0], arrived[1])
    while mask:
        for r in sorted(tokens):
            tokens[r ^ mask] = swap(after(tokens[r], grad_pre) if r else tokens[r], "ctx", mask)
        mask //= 2
    tokens = [tokens[r] for r in range(ctx_count)]

    grad_pair = swap(grad_pre, "dp", 1)

    def input_terms(s_ref, grad_ref, *refs):
        pair_refs, terms, band = refs[:chips], refs[chips:-1], refs[-1]
        for r in range(chips):
            band[row_block((s_ref[1] >> 1) ^ r, 2 * w_rows), :] = pair_refs[r][...]
        step = min(256, width)
        for at in range(0, width, step):
            product = dot(grad_ref[...], band[at : at + step, :], BY_COLS).astype(jnp.bfloat16)
            for r in range(ctx_count):
                terms[r][:, at : at + step] = product[r * rows : (r + 1) * rows]

    terms = call(
        input_terms,
        [scalars],
        [grad_pre] + pairs,
        [bf16(rows, width)] * ctx_count,
        [pltpu.VMEM((width, wide), jnp.bfloat16)],
        50 * product_flops,
    )
    returned = [terms[0]] + [None] * (ctx_count - 1)
    for r in range(ctx_count - 1, 0, -1):
        returned[r] = swap(terms[r], "ctx", r)

    def weight_terms(own_ref, pair_ref, *refs):
        token_refs = refs[:ctx_count]
        outs, (held, grads) = refs[ctx_count:-2], refs[-2:]
        for r in range(ctx_count):
            for i in range(2):
                at = i * whole + r * rows
                held[at : at + rows, :] = token_refs[r][i]
        grads[:whole, :] = own_ref[...]
        grads[whole:, :] = pair_ref[...]
        product = dot(held[...], grads[...], BY_ROWS)
        for r in range(chips):
            outs[r][...] = product[r * w_rows : (r + 1) * w_rows].astype(outs[r].dtype)

    own, *outgoing = call(
        weight_terms,
        [],
        [grad_pre, grad_pair] + tokens,
        [f32(w_rows, wide)] + [bf16(w_rows, wide)] * (chips - 1),
        [pltpu.VMEM((2 * whole, width // 2), jnp.bfloat16), pltpu.VMEM((2 * whole, wide), jnp.bfloat16)],
        product_flops,
    )
    total = own
    for r in range(1, chips):
        total = total + swap(outgoing[r - 1], "dp", 2 * r).astype(jnp.float32)
    grad_weight = total * (1.0 / dp_count)
    input_grad = returned[0].astype(jnp.float32)
    for block in returned[1:]:
        input_grad = input_grad + block.astype(jnp.float32)
    return (input_grad.astype(jnp.bfloat16)[None], grad_weight)


def solution(mesh):
    return jax.shard_map(
        body,
        mesh=mesh,
        in_specs=(
            P("dp", "ctx", None),
            P("dp", "ctx", None),
            P("dp", "ctx", None),
            P("dp", "ctx"),
            P("dp", None),
            P("dp", None),
        ),
        out_specs=(P("dp", "ctx", None), P("dp", "ctx")),
        check_vma=False,
    )
```

time: 88.3 us -> 75.7 us (0.86); the launches traced: 88.1 us -> 74.7 us
  waiting for transfers between devices: 45.9 us -> 41.1 us
  starting transfers between devices: 24.1 us -> 19.4 us
  Pallas kernels: 12.2 us -> 8.8 us
    ppermute x23 -> x18, waiting for transfers between devices: 45.9 us -> 41.1 us  [swap(): return lax.ppermute(array, axis, [(i, i ^ mask) for i in range(count)])]
    ppermute x23 -> x18, starting transfers between devices: 24.1 us -> 19.4 us  [swap(): return lax.ppermute(array, axis, [(i, i ^ mask) for i in range(count)])]
    pallas_call x6, Pallas kernels: 12.2 us -> 8.8 us  [call(): pl.pallas_call(kernel, out_shape=list(outs), in_specs=[pl.BlockSpec(memor...]
    unnamed x14 -> x12, local copies, waits for them, and re-layouts: 3.41 us -> 2.76 us
  transfers between devices with their start and end apart: 23 -> 18, of which waited for: 11 -> 9; matrix products, arithmetic and copies ran while one was open for 1% -> 1% of each run, Pallas kernels for 14% -> 11%
where the time goes in v2:
time: 75.7 us; the launch traced here: 74.7 us
  waiting for transfers between devices  41.1 us (54%)
  starting transfers between devices  19.4 us (26%)
  Pallas kernels  8.8 us (12%)
  local copies, waits for them, and re-layouts  2.76 us (4%)
  other arithmetic  1.81 us (2%)
    ppermute x18, waiting for transfers between devices, swap(): return lax.ppermute(array, axis, [(i, i ^ mask) for i in range(count)])  41.1 us
    ppermute x18, starting transfers between devices, swap(): return lax.ppermute(array, axis, [(i, i ^ mask) for i in range(count)])  19.4 us
    pallas_call x6, Pallas kernels, call(): pl.pallas_call(kernel, out_shape=list(outs), in_specs=[pl.BlockSpec(memor...  8.8 us
    unnamed x12, local copies, waits for them, and re-layouts  2.76 us
  transfers between devices with their start and end apart: 18, of which 9 were waited for; matrix products, arithmetic and copies ran while one was open for 1% of the time, Pallas kernels for 11%

profile of v2, /device:TPU:18, one launch (start us, length us, event | category | flops | bytes accessed | tf_op | source)
XLA Modules:
  0.0 74.7 jit_solution(12441579743489352290)
XLA Ops:
  0.6 1.1 %copy-done = bf16[1,128,3072]{2,1,0:T(8,128)(2,1)S(1)} copy-done((bf16[1,128,3072]{2,1,0:T(8,128)(2,1)S(1)}, bf16[1,128,3072]{2,1,0:T(8,128)(2,1)}, u32[]{:S(2)}) %copy-start) | copy-done | bytes 786456
  1.8 0.9 %copy-done.2 = bf16[1,128,1024]{2,1,0:T(8,128)(2,1)S(1)} copy-done((bf16[1,128,1024]{2,1,0:T(8,128)(2,1)S(1)}, bf16[1,128,1024]{2,1,0:T(8,128)(2,1)}, u32[]{:S(2)}) %copy-start.2) | copy-done | bytes 262168
  2.7 0.2 shard_map.77
  3.0 0.0 copy-start.3
  3.0 1.6 %collective-permute-start = (bf16[128,1024]{1,0:T(8,128)(2,1)S(1)}, bf16[128,1024]{1,0:T(8,128)(2,1)S(1)}, u32[]{:S(2)}, u32[]{:S(2)}) collective-permute-start(bf16[128,1024]{1,0:T(8,128)(2,1)S(1)} %get-tuple-element.21), channel_id=1, source_target_pairs={{0,1},{1,0},{2,3},{3,2},{4,5},{5,4},{6,7},{7,6},{8,9},{9,8},{10,11... | collective-permute-start | bytes 786440 | tf_op jit(solution)/shard_map/ppermute | solution.py:50
  4.6 0.3 collective-permute-start.1
  5.0 1.6 %collective-permute-start.2 = (bf16[128,1024]{1,0:T(8,128)(2,1)S(1)}, bf16[128,1024]{1,0:T(8,128)(2,1)S(1)}, u32[]{:S(2)}, u32[]{:S(2)}) collective-permute-start(bf16[128,1024]{1,0:T(8,128)(2,1)S(1)} %get-tuple-element.23), channel_id=1, source_target_pairs={{0,3},{1,2},{2,1},{3,0},{4,7},{5,6},{6,5},{7,4},{8,11},{9,10},{10,... | collective-permute-start | bytes 786440 | tf_op jit(solution)/shard_map/ppermute | solution.py:50
  6.5 0.1 shard_map.81
  6.6 0.1 collective-permute-start.11
  6.7 0.5 collective-permute-start.3
  7.2 0.7 copy-done.4
  7.8 0.0 copy-done.5
  7.9 0.1 pad_add_fusion.s_ref
  7.9 0.1 collective-permute-done.11
  8.1 0.3 collective-permute-done.3.other_ref
  8.3 1.6 %collective-permute-start.6 = (bf16[256,768]{1,0:T(8,128)(2,1)S(1)}, bf16[256,768]{1,0:T(8,128)(2,1)S(1)}, u32[]{:S(2)}, u32[]{:S(2)}) collective-permute-start(bf16[256,768]{1,0:T(8,128)(2,1)S(1)} %shard_map.79.refs_0_), channel_id=1, source_target_pairs={{0,24},{4,28},{8,16},{12,20},{16,8},{20,12},{24,0},{28,4},{1,25},{... | collective-permute-start | bytes 1179656 | tf_op jit(solution)/shard_map/ppermute | solution.py:50
  9.9 0.5 collective-permute-start.5
  10.4 4.1 %collective-permute-done.refs_1_ = bf16[128,1024]{1,0:T(8,128)(2,1)S(1)} collective-permute-done((bf16[128,1024]{1,0:T(8,128)(2,1)S(1)}, bf16[128,1024]{1,0:T(8,128)(2,1)S(1)}, u32[]{:S(2)}, u32[]{:S(2)}) %collective-permute-start) | collective-permute-done | bytes 262176 | tf_op jit(solution)/shard_map/ppermute | solution.py:50
  14.5 0.5 collective-permute-start.4
  15.0 10.7 %collective-permute-done.1.refs_2_ = bf16[128,1024]{1,0:T(8,128)(2,1)S(1)} collective-permute-done((bf16[128,1024]{1,0:T(8,128)(2,1)S(1)}, bf16[128,1024]{1,0:T(8,128)(2,1)S(1)}, u32[]{:S(2)}, u32[]{:S(2)}) %collective-permute-start.1) | collective-permute-done | bytes 262176 | tf_op jit(solution)/shard_map/ppermute | solution.py:50
  25.8 3.4 %collective-permute-start.13 = (bf16[2,128,512]{2,1,0:T(8,128)(2,1)S(1)}, bf16[2,128,512]{2,1,0:T(8,128)(2,1)S(1)}, u32[]{:S(2)}, u32[]{:S(2)}) collective-permute-start(bf16[2,128,512]{2,1,0:T(8,128)(2,1)S(1)} %pad_maximum_fusion.refs_0_), channel_id=1, source_target_pairs={{0,2},{1,3},{2,0},{3,1},{4,6},{5,7},{6,4},{7,5},{8,10},{9,11},{10,... | collective-permute-start | bytes 786440 | tf_op jit(solution)/shard_map/ppermute | solution.py:50
  29.1 7.1 %collective-permute-done.2.refs_3_ = bf16[128,1024]{1,0:T(8,128)(2,1)S(1)} collective-permute-done((bf16[128,1024]{1,0:T(8,128)(2,1)S(1)}, bf16[128,1024]{1,0:T(8,128)(2,1)S(1)}, u32[]{:S(2)}, u32[]{:S(2)}) %collective-permute-start.2) | collective-permute-done | bytes 262176 | tf_op jit(solution)/shard_map/ppermute | solution.py:50
  36.2 0.0 collective-permute-start.12
  36.2 5.8 %shard_map.78.grad_ref.own_ref = bf16[512,768]{1,0:T(8,128)(2,1)S(1)} custom-call(s32[14]{0:T(128)S(1)} %pad_add_fusion.s_ref, bf16[128,1024]{1,0:T(8,128)(2,1)S(1)} %get-tuple-element.20.refs_0_, bf16[128,1024]{1,0:T(8,128)(2,1)S(1)} %collective-permute-done.refs_1_, bf16[128,1024]{1,0:T(8,128)(2,1)S(1)} %collective-permute-done.1.refs_2_, ...), custom_call_target="tpu_custom_call" | custom-call | flops 9663676416 | bytes 1835008 | tf_op jit(solution)/shard_map/pallas_call | solution.py:24
  42.0 0.0 collective-permute-done.13.refs_2_
  42.0 0.1 collective-permute-start.10
  42.1 0.0 collective-permute-done.6.refs_3_
  42.1 2.1 %collective-permute-start.14 = (bf16[2,128,512]{2,1,0:T(8,128)(2,1)S(1)}, bf16[2,128,512]{2,1,0:T(8,128)(2,1)S(1)}, u32[]{:S(2)}, u32[]{:S(2)}) collective-permute-start(bf16[2,128,512]{2,1,0:T(8,128)(2,1)S(1)} %collective-permute-done.13.refs_2_), channel_id=1, source_target_pairs={{0,1},{1,0},{2,3},{3,2},{4,5},{5,4},{6,7},{7,6},{8,9},{9,8},{10,11... | collective-permute-start | bytes 786440 | tf_op jit(solution)/shard_map/ppermute | solution.py:50
  44.2 0.0 collective-permute-done.5.refs_2_
  44.2 0.0 collective-permute-done.4.refs_1_
  44.2 1.7 %shard_map.80 = (bf16[128,1024]{1,0:T(8,128)(2,1)S(1)}, bf16[128,1024]{1,0:T(8,128)(2,1)S(1)}, bf16[128,1024]{1,0:T(8,128)(2,1)S(1)}, bf16[128,1024]{1,0:T(8,128)(2,1)S(1)}) custom-call(s32[14]{0:T(128)S(1)} %pad_add_fusion.s_ref, bf16[512,768]{1,0:T(8,128)(2,1)S(1)} %shard_map.78.grad_ref.own_ref, bf16[256,768]{1,0:T(8,128)(2,1)S(1)} %shard_map.79.refs_0_, ...), custom_call_target="tpu_custom_call" | custom-call | flops 40265318400 | bytes 3407872 | tf_op jit(solution)/shard_map/pallas_call | solution.py:24
  45.9 0.1 collective-permute-start.7
  46.0 1.9 %collective-permute-start.8 = (bf16[128,1024]{1,0:T(8,128)(2,1)S(1)}, bf16[128,1024]{1,0:T(8,128)(2,1)S(1)}, u32[]{:S(2)}, u32[]{:S(2)}) collective-permute-start(bf16[128,1024]{1,0:T(8,128)(2,1)S(1)} %get-tuple-element.27), channel_id=1, source_target_pairs={{0,2},{1,3},{2,0},{3,1},{4,6},{5,7},{6,4},{7,5},{8,10},{9,11},{10,... | collective-permute-start | bytes 786440 | tf_op jit(solution)/shard_map/ppermute | solution.py:50
  47.8 0.0 collective-permute-done.12.refs_1_
  47.8 1.6 %collective-permute-start.9 = (bf16[128,1024]{1,0:T(8,128)(2,1)S(1)}, bf16[128,1024]{1,0:T(8,128)(2,1)S(1)}, u32[]{:S(2)}, u32[]{:S(2)}) collective-permute-start(bf16[128,1024]{1,0:T(8,128)(2,1)S(1)} %get-tuple-element.28), channel_id=1, source_target_pairs={{0,3},{1,2},{2,1},{3,0},{4,7},{5,6},{6,5},{7,4},{8,11},{9,10},{10,... | collective-permute-start | bytes 786440 | tf_op jit(solution)/shard_map/ppermute | solution.py:50
  49.4 6.9 %collective-permute-done.14.refs_3_ = bf16[2,128,512]{2,1,0:T(8,128)(2,1)S(1)} collective-permute-done((bf16[2,128,512]{2,1,0:T(8,128)(2,1)S(1)}, bf16[2,128,512]{2,1,0:T(8,128)(2,1)S(1)}, u32[]{:S(2)}, u32[]{:S(2)}) %collective-permute-start.14) | collective-permute-done | bytes 262176 | tf_op jit(solution)/shard_map/ppermute | solution.py:50
  56.3 0.0 collective-permute-done.10.pair_ref
  56.3 1.0 %shard_map.82 = (f32[128,768]{1,0:T(8,128)S(1)}, bf16[128,768]{1,0:T(8,128)(2,1)S(1)}, bf16[128,768]{1,0:T(8,128)(2,1)S(1)}, bf16[128,768]{1,0:T(8,128)(2,1)S(1)}) custom-call(bf16[512,768]{1,0:T(8,128)(2,1)S(1)} %shard_map.78.grad_ref.own_ref, bf16[512,768]{1,0:T(8,128)(2,1)S(1)} %collective-permute-done.10.pair_ref, ...), custom_call_target="tpu_custom_call" | custom-call | flops 805306368 | bytes 3604480 | tf_op jit(solution)/shard_map/pallas_call | solution.py:24
  57.3 0.6 collective-permute-start.15
  57.9 1.5 %collective-permute-start.16 = (bf16[128,768]{1,0:T(8,128)(2,1)S(1)}, bf16[128,768]{1,0:T(8,128)(2,1)S(1)}, u32[]{:S(2)}, u32[]{:S(2)}) collective-permute-start(bf16[128,768]{1,0:T(8,128)(2,1)S(1)} %get-tuple-element.36), channel_id=1, source_target_pairs={{0,16},{4,20},{8,24},{12,28},{16,0},{20,4},{24,8},{28,12},{1,17},{... | collective-permute-start | bytes 589832 | tf_op jit(solution)/shard_map/ppermute | solution.py:50
  59.4 7.8 %collective-permute-done.7 = bf16[128,1024]{1,0:T(8,128)(2,1)S(1)} collective-permute-done((bf16[128,1024]{1,0:T(8,128)(2,1)S(1)}, bf16[128,1024]{1,0:T(8,128)(2,1)S(1)}, u32[]{:S(2)}, u32[]{:S(2)}) %collective-permute-start.7) | collective-permute-done | bytes 262176 | tf_op jit(solution)/shard_map/ppermute | solution.py:50
  67.2 1.5 %collective-permute-start.17 = (bf16[128,768]{1,0:T(8,128)(2,1)S(1)}, bf16[128,768]{1,0:T(8,128)(2,1)S(1)}, u32[]{:S(2)}, u32[]{:S(2)}) collective-permute-start(bf16[128,768]{1,0:T(8,128)(2,1)S(1)} %get-tuple-element.37), channel_id=1, source_target_pairs={{0,24},{4,28},{8,16},{12,20},{16,8},{20,12},{24,0},{28,4},{1,25},{... | collective-permute-start | bytes 589832 | tf_op jit(solution)/shard_map/ppermute | solution.py:50
  68.7 0.0 collective-permute-done.8
  68.7 3.7 %collective-permute-done.9 = bf16[128,1024]{1,0:T(8,128)(2,1)S(1)} collective-permute-done((bf16[128,1024]{1,0:T(8,128)(2,1)S(1)}, bf16[128,1024]{1,0:T(8,128)(2,1)S(1)}, u32[]{:S(2)}, u32[]{:S(2)}) %collective-permute-start.9) | collective-permute-done | bytes 262176 | tf_op jit(solution)/shard_map/ppermute | solution.py:50
  72.4 0.9 %fusion = bf16[1,128,1024]{2,1,0:T(8,128)(2,1)} fusion(bf16[128,1024]{1,0:T(8,128)(2,1)S(1)} %collective-permute-done.9, bf16[128,1024]{1,0:T(8,128)(2,1)S(1)} %collective-permute-done.8, bf16[128,1024]{1,0:T(8,128)(2,1)S(1)} %collective-permute-done.7, bf16[128,1024]{1,0:T(8,128)(2,1)S(1)} %get-tuple-element.25), kind=kLoop, calls=%fused_computation.2 | loop fusion | flops 1048576 | bytes 1310720 | tf_op jit(solution)/shard_map/broadcast_in_dim | solution.py:300
  73.3 0.0 collective-permute-done.15
  73.3 0.6 collective-permute-done.17
  73.8 0.8 %add_multiply_fusion = f32[128,768]{1,0:T(8,128)} fusion(bf16[128,768]{1,0:T(8,128)(2,1)S(1)} %collective-permute-done.17, bf16[128,768]{1,0:T(8,128)(2,1)S(1)} %collective-permute-done.16, f32[128,768]{1,0:T(8,128)S(1)} %get-tuple-element.34, bf16[128,768]{1,0:T(8,128)(2,1)S(1)} %collective-permute-done.15), kind=kLoop, calls=%fused_computation.1 | loop fusion | flops 688128 | bytes 1376256 | tf_op jit(solution)/shard_map/mul | solution.py:296
  (10 shorter events, 0.1 us)
Async XLA Ops:
  0.6 1.1 %copy-start = (bf16[1,128,3072]{2,1,0:T(8,128)(2,1)S(1)}, bf16[1,128,3072]{2,1,0:T(8,128)(2,1)}, u32[]{:S(2)}) copy-start(bf16[1,128,3072]{2,1,0:T(8,128)(2,1)} %param.7) | copy-start | bytes 2359300
  1.8 0.9 %copy-start.2 = (bf16[1,128,1024]{2,1,0:T(8,128)(2,1)S(1)}, bf16[1,128,1024]{2,1,0:T(8,128)(2,1)}, u32[]{:S(2)}) copy-start(bf16[1,128,1024]{2,1,0:T(8,128)(2,1)} %param.8) | copy-start | bytes 786436
  2.7 3.8 %copy-start.1 = (bf16[1,128,1024]{2,1,0:T(8,128)(2,1)S(1)}, bf16[1,128,1024]{2,1,0:T(8,128)(2,1)}, u32[]{:S(2)}) copy-start(bf16[1,128,1024]{2,1,0:T(8,128)(2,1)} %param.6) | copy-start | bytes 786436
  3.0 3.7 %copy-start.3 = (bf16[128,768]{1,0:T(8,128)(2,1)S(1)}, bf16[128,768]{1,0:T(8,128)(2,1)}, u32[]{:S(2)}) copy-start(bf16[128,768]{1,0:T(8,128)(2,1)} %own_ref.1) | copy-start | bytes 589828
  3.0 11.5 %collective-permute-start = (bf16[128,1024]{1,0:T(8,128)(2,1)S(1)}, bf16[128,1024]{1,0:T(8,128)(2,1)S(1)}, u32[]{:S(2)}, u32[]{:S(2)}) collective-permute-start(bf16[128,1024]{1,0:T(8,128)(2,1)S(1)} %get-tuple-element.21), channel_id=1, source_target_pairs={{0,1},{1,0},{2,3},{3,2},{4,5},{5,4},{6,7},{7,6},{8,9},{9,8},{10,11... | collective-permute-start | bytes 786440 | tf_op jit(solution)/shard_map/ppermute | solution.py:50
  4.6 21.1 %collective-permute-start.1 = (bf16[128,1024]{1,0:T(8,128)(2,1)S(1)}, bf16[128,1024]{1,0:T(8,128)(2,1)S(1)}, u32[]{:S(2)}, u32[]{:S(2)}) collective-permute-start(bf16[128,1024]{1,0:T(8,128)(2,1)S(1)} %get-tuple-element.22), channel_id=1, source_target_pairs={{0,2},{1,3},{2,0},{3,1},{4,6},{5,7},{6,4},{7,5},{8,10},{9,11},{10,... | collective-permute-start | bytes 786440 | tf_op jit(solution)/shard_map/ppermute | solution.py:50
  5.0 31.3 %collective-permute-start.2 = (bf16[128,1024]{1,0:T(8,128)(2,1)S(1)}, bf16[128,1024]{1,0:T(8,128)(2,1)S(1)}, u32[]{:S(2)}, u32[]{:S(2)}) collective-permute-start(bf16[128,1024]{1,0:T(8,128)(2,1)S(1)} %get-tuple-element.23), channel_id=1, source_target_pairs={{0,3},{1,2},{2,1},{3,0},{4,7},{5,6},{6,5},{7,4},{8,11},{9,10},{10,... | collective-permute-start | bytes 786440 | tf_op jit(solution)/shard_map/ppermute | solution.py:50
  6.6 1.4 %collective-permute-start.11 = (bf16[128,512]{1,0:T(8,128)(2,1)S(1)}, bf16[128,512]{1,0:T(8,128)(2,1)S(1)}, u32[]{:S(2)}, u32[]{:S(2)}) collective-permute-start(bf16[128,512]{1,0:T(8,128)(2,1)S(1)} %get-tuple-element.31), channel_id=1, source_target_pairs={{0,4},{4,0},{8,12},{12,8},{16,20},{20,16},{24,28},{28,24},{1,5},{5... | collective-permute-start | bytes 393224 | tf_op jit(solution)/shard_map/ppermute | solution.py:50
  6.7 1.6 %collective-permute-start.3 = (bf16[128,768]{1,0:T(8,128)(2,1)S(1)}, bf16[128,768]{1,0:T(8,128)(2,1)S(1)}, u32[]{:S(2)}, u32[]{:S(2)}) collective-permute-start(bf16[128,768]{1,0:T(8,128)(2,1)S(1)} %copy-done.3), channel_id=1, source_target_pairs={{0,4},{4,0},{8,12},{12,8},{16,20},{20,16},{24,28},{28,24},{1,5},{5... | collective-permute-start | bytes 589832 | tf_op jit(solution)/shard_map/ppermute | solution.py:50
  7.2 0.7 copy-start.4
  7.2 0.7 copy-start.5
  8.3 33.8 %collective-permute-start.6 = (bf16[256,768]{1,0:T(8,128)(2,1)S(1)}, bf16[256,768]{1,0:T(8,128)(2,1)S(1)}, u32[]{:S(2)}, u32[]{:S(2)}) collective-permute-start(bf16[256,768]{1,0:T(8,128)(2,1)S(1)} %shard_map.79.refs_0_), channel_id=1, source_target_pairs={{0,24},{4,28},{8,16},{12,20},{16,8},{20,12},{24,0},{28,4},{1,25},{... | collective-permute-start | bytes 1179656 | tf_op jit(solution)/shard_map/ppermute | solution.py:50
  9.9 34.3 %collective-permute-start.5 = (bf16[256,768]{1,0:T(8,128)(2,1)S(1)}, bf16[256,768]{1,0:T(8,128)(2,1)S(1)}, u32[]{:S(2)}, u32[]{:S(2)}) collective-permute-start(bf16[256,768]{1,0:T(8,128)(2,1)S(1)} %shard_map.79.refs_0_), channel_id=1, source_target_pairs={{0,16},{4,20},{8,24},{12,28},{16,0},{20,4},{24,8},{28,12},{1,17},{... | collective-permute-start | bytes 1179656 | tf_op jit(solution)/shard_map/ppermute | solution.py:50
  14.5 29.7 %collective-permute-start.4 = (bf16[256,768]{1,0:T(8,128)(2,1)S(1)}, bf16[256,768]{1,0:T(8,128)(2,1)S(1)}, u32[]{:S(2)}, u32[]{:S(2)}) collective-permute-start(bf16[256,768]{1,0:T(8,128)(2,1)S(1)} %shard_map.79.refs_0_), channel_id=1, source_target_pairs={{0,8},{4,12},{8,0},{12,4},{16,24},{20,28},{24,16},{28,20},{1,9},{5... | collective-permute-start | bytes 1179656 | tf_op jit(solution)/shard_map/ppermute | solution.py:50
  25.8 16.2 %collective-permute-start.13 = (bf16[2,128,512]{2,1,0:T(8,128)(2,1)S(1)}, bf16[2,128,512]{2,1,0:T(8,128)(2,1)S(1)}, u32[]{:S(2)}, u32[]{:S(2)}) collective-permute-start(bf16[2,128,512]{2,1,0:T(8,128)(2,1)S(1)} %pad_maximum_fusion.refs_0_), channel_id=1, source_target_pairs={{0,2},{1,3},{2,0},{3,1},{4,6},{5,7},{6,4},{7,5},{8,10},{9,11},{10,... | collective-permute-start | bytes 786440 | tf_op jit(solution)/shard_map/ppermute | solution.py:50
  36.2 11.6 %collective-permute-start.12 = (bf16[2,128,512]{2,1,0:T(8,128)(2,1)S(1)}, bf16[2,128,512]{2,1,0:T(8,128)(2,1)S(1)}, u32[]{:S(2)}, u32[]{:S(2)}) collective-permute-start(bf16[2,128,512]{2,1,0:T(8,128)(2,1)S(1)} %pad_maximum_fusion.refs_0_), channel_id=1, source_target_pairs={{0,1},{1,0},{2,3},{3,2},{4,5},{5,4},{6,7},{7,6},{8,9},{9,8},{10,11... | collective-permute-start | bytes 786440 | tf_op jit(solution)/shard_map/ppermute | solution.py:50
  42.0 14.3 %collective-permute-start.10 = (bf16[512,768]{1,0:T(8,128)(2,1)S(1)}, bf16[512,768]{1,0:T(8,128)(2,1)S(1)}, u32[]{:S(2)}, u32[]{:S(2)}) collective-permute-start(bf16[512,768]{1,0:T(8,128)(2,1)S(1)} %shard_map.78.grad_ref.own_ref), channel_id=1, source_target_pairs={{0,4},{4,0},{8,12},{12,8},{16,20},{20,16},{24,28},{28,24},{1,5},{5... | collective-permute-start | bytes 2359304 | tf_op jit(solution)/shard_map/ppermute | solution.py:50
  42.1 14.2 %collective-permute-start.14 = (bf16[2,128,512]{2,1,0:T(8,128)(2,1)S(1)}, bf16[2,128,512]{2,1,0:T(8,128)(2,1)S(1)}, u32[]{:S(2)}, u32[]{:S(2)}) collective-permute-start(bf16[2,128,512]{2,1,0:T(8,128)(2,1)S(1)} %collective-permute-done.13.refs_2_), channel_id=1, source_target_pairs={{0,1},{1,0},{2,3},{3,2},{4,5},{5,4},{6,7},{7,6},{8,9},{9,8},{10,11... | collective-permute-start | bytes 786440 | tf_op jit(solution)/shard_map/ppermute | solution.py:50
  45.9 21.4 %collective-permute-start.7 = (bf16[128,1024]{1,0:T(8,128)(2,1)S(1)}, bf16[128,1024]{1,0:T(8,128)(2,1)S(1)}, u32[]{:S(2)}, u32[]{:S(2)}) collective-permute-start(bf16[128,1024]{1,0:T(8,128)(2,1)S(1)} %get-tuple-element.26), channel_id=1, source_target_pairs={{0,1},{1,0},{2,3},{3,2},{4,5},{5,4},{6,7},{7,6},{8,9},{9,8},{10,11... | collective-permute-start | bytes 786440 | tf_op jit(solution)/shard_map/ppermute | solution.py:50
  46.0 22.8 %collective-permute-start.8 = (bf16[128,1024]{1,0:T(8,128)(2,1)S(1)}, bf16[128,1024]{1,0:T(8,128)(2,1)S(1)}, u32[]{:S(2)}, u32[]{:S(2)}) collective-permute-start(bf16[128,1024]{1,0:T(8,128)(2,1)S(1)} %get-tuple-element.27), channel_id=1, source_target_pairs={{0,2},{1,3},{2,0},{3,1},{4,6},{5,7},{6,4},{7,5},{8,10},{9,11},{10,... | collective-permute-start | bytes 786440 | tf_op jit(solution)/shard_map/ppermute | solution.py:50
  47.8 24.5 %collective-permute-start.9 = (bf16[128,1024]{1,0:T(8,128)(2,1)S(1)}, bf16[128,1024]{1,0:T(8,128)(2,1)S(1)}, u32[]{:S(2)}, u32[]{:S(2)}) collective-permute-start(bf16[128,1024]{1,0:T(8,128)(2,1)S(1)} %get-tuple-element.28), channel_id=1, source_target_pairs={{0,3},{1,2},{2,1},{3,0},{4,7},{5,6},{6,5},{7,4},{8,11},{9,10},{10,... | collective-permute-start | bytes 786440 | tf_op jit(solution)/shard_map/ppermute | solution.py:50
  57.3 15.9 %collective-permute-start.15 = (bf16[128,768]{1,0:T(8,128)(2,1)S(1)}, bf16[128,768]{1,0:T(8,128)(2,1)S(1)}, u32[]{:S(2)}, u32[]{:S(2)}) collective-permute-start(bf16[128,768]{1,0:T(8,128)(2,1)S(1)} %get-tuple-element.35), channel_id=1, source_target_pairs={{0,8},{4,12},{8,0},{12,4},{16,24},{20,28},{24,16},{28,20},{1,9},{5... | collective-permute-start | bytes 589832 | tf_op jit(solution)/shard_map/ppermute | solution.py:50
  57.9 15.3 %collective-permute-start.16 = (bf16[128,768]{1,0:T(8,128)(2,1)S(1)}, bf16[128,768]{1,0:T(8,128)(2,1)S(1)}, u32[]{:S(2)}, u32[]{:S(2)}) collective-permute-start(bf16[128,768]{1,0:T(8,128)(2,1)S(1)} %get-tuple-element.36), channel_id=1, source_target_pairs={{0,16},{4,20},{8,24},{12,28},{16,0},{20,4},{24,8},{28,12},{1,17},{... | collective-permute-start | bytes 589832 | tf_op jit(solution)/shard_map/ppermute | solution.py:50
  67.2 6.6 %collective-permute-start.17 = (bf16[128,768]{1,0:T(8,128)(2,1)S(1)}, bf16[128,768]{1,0:T(8,128)(2,1)S(1)}, u32[]{:S(2)}, u32[]{:S(2)}) collective-permute-start(bf16[128,768]{1,0:T(8,128)(2,1)S(1)} %get-tuple-element.37), channel_id=1, source_target_pairs={{0,24},{4,28},{8,16},{12,20},{16,8},{20,12},{24,0},{28,4},{1,25},{... | collective-permute-start | bytes 589832 | tf_op jit(solution)/shard_map/ppermute | solution.py:50

commit v3 on v2

--- a/solution.py
+++ b/solution.py
@@ -17,7 +17,7 @@
     return lax.dot_general(a, b, dims, preferred_element_type=jnp.float32)
 
 
-def call(kernel, scalars, arrays, outs, scratch=(), flops=0, place=pltpu.VMEM):
+def call(kernel, scalars, arrays, outs, scratch=(), flops=0, place=pltpu.VMEM, vmem=VMEM_BYTES):
     size = sum(a.size * a.dtype.itemsize for a in arrays) + sum(
         o.size * o.dtype.itemsize for o in outs
     )
@@ -28,7 +28,7 @@
         + [pl.BlockSpec(memory_space=place)] * len(arrays),
         out_specs=[pl.BlockSpec(memory_space=pltpu.VMEM)] * len(outs),
         scratch_shapes=list(scratch),
-        compiler_params=pltpu.CompilerParams(vmem_limit_bytes=VMEM_BYTES),
+        compiler_params=pltpu.CompilerParams(vmem_limit_bytes=vmem),
         cost_estimate=pl.CostEstimate(flops=flops, bytes_accessed=size, transcendentals=0),
     )(*scalars, *arrays)
 
@@ -102,25 +102,22 @@
     return call(kernel, [me[None]], [own, other], [bf16(2 * rows, own.shape[1])])[0]
 
 
-def half_columns(me, tokens, count):
-    rows, width = tokens.shape
+def half_columns(me, own, other, count):
+    rows, width = own.shape
     size = width // count
     if size % LANES:
-        blocks = tokens.reshape(rows, count, size)
-        return [
-            jnp.concatenate(
-                [lax.dynamic_index_in_dim(blocks, me ^ r, 1, False) for r in range(i, count, 2)],
-                axis=1,
-            )
-            for i in range(2)
-        ]
-
-    def kernel(me_ref, tokens_ref, *outs):
-        for r in range(count):
-            owner = pl.multiple_of((me_ref[0] ^ r) * size, LANES)
-            outs[r % 2][:, r // 2 * size : (r // 2 + 1) * size] = tokens_ref[:, pl.ds(owner, size)]
-
-    return call(kernel, [me[None]], [tokens], [bf16(rows, width // 2)] * 2)
+        both = jnp.stack([own, other]).reshape(2, rows, count, size)
+        blocks = [lax.dynamic_index_in_dim(both, me ^ r, 2, False) for r in range(0, count, 2)]
+        return jnp.concatenate(blocks, axis=2)
+
+    def kernel(me_ref, own_ref, other_ref, out):
+        for r in range(0, count, 2):
+            owner = pl.ds(pl.multiple_of((me_ref[0] ^ r) * size, LANES), size)
+            at = slice(r // 2 * size, (r // 2 + 1) * size)
+            out[0, :, at] = own_ref[:, owner]
+            out[1, :, at] = other_ref[:, owner]
+
+    return call(kernel, [me[None]], [own, other], [bf16(2, rows, width // 2)])[0]
 
 
 def user_rows(lengths, whole):
@@ -156,28 +153,37 @@
             value_ref[h, at, :] = active[:, base + 2 * DH : base + 3 * DH]
             grad_ref[h, at, :] = piece[:, wide + h * DH : wide + (h + 1) * DH]
     first, scale = user_rows(lengths, whole)
-    grad_q = [None] * heads
-    for j in range(blocks):
-        lo = j * rows
-        count = whole - lo
-        key_place = lax.broadcasted_iota(jnp.int32, (rows, count), 0)
-        query_place = lax.broadcasted_iota(jnp.int32, (rows, count), 1)
-        visible = (query_place >= key_place) & (key_place + lo >= first[:, lo:])
-        scales = jnp.where(visible, scale[:, lo:], 0.0)
-        slot = sum([jnp.where(perm[r] == j, r, 0) for r in range(blocks)])
-        done = []
+    step = min(256, whole)
+    grad_k, grad_v, grad_q = ([[] for _ in range(heads)] for _ in range(3))
+    for lo in range(0, whole, step):
+        hi = lo + step
+        key_place = lax.broadcasted_iota(jnp.int32, (hi, step), 0)
+        query_place = lax.broadcasted_iota(jnp.int32, (hi, step), 1) + lo
+        visible = (query_place >= key_place) & (key_place >= first[:, lo:hi])
+        scales = jnp.where(visible, scale[:, lo:hi], 0.0)
         for h in range(heads):
-            query, grad = query_ref[h, lo:, :], grad_ref[h, lo:, :]
-            u = dot(key_ref[h, lo : lo + rows, :], query, BY_COLS)
-            gw = dot(value_ref[h, lo : lo + rows, :], grad, BY_COLS)
+            query, grad = query_ref[h, lo:hi, :], grad_ref[h, lo:hi, :]
+            key = key_ref[h, :hi, :]
+            u = dot(key, query, BY_COLS)
+            gw = dot(value_ref[h, :hi, :], grad, BY_COLS)
             t = jnp.tanh(u)
             a = scales + scales * t
             weights = (u * a).astype(jnp.bfloat16)
             slope = (gw * a * (1.0 + (u - u * t))).astype(jnp.bfloat16)
-            add_q = dot(key_ref[h, lo : lo + rows, :].T, slope)
-            total_q = add_q if j == 0 else grad_q[h] + add_q
-            grad_q[h] = total_q[:, rows:]
-            done += [total_q[:, :rows].T * 0.0625, dot(slope, query), dot(weights, grad)]
+            grad_q[h].append(dot(key.T, slope).T)
+            add_k, add_v = dot(slope, query), dot(weights, grad)
+            if lo == 0:
+                grad_k[h], grad_v[h] = add_k, add_v
+            else:
+                grad_k[h] = jnp.concatenate([grad_k[h] + add_k[:lo], add_k[lo:]], axis=0)
+                grad_v[h] = jnp.concatenate([grad_v[h] + add_v[:lo], add_v[lo:]], axis=0)
+    for j in range(blocks):
+        slot = sum([jnp.where(perm[r] == j, r, 0) for r in range(blocks)])
+        lo, hi = j * rows, (j + 1) * rows
+        done = []
+        for h in range(heads):
+            query = grad_q[h][lo // step]
+            done += [query[lo % step : lo % step + rows] * 0.0625, grad_k[h][lo:hi], grad_v[h][lo:hi]]
         at = row_block(slot, rows)
         grad_pre[at, :] = (jnp.concatenate(done, axis=1) * factor_ref[at, :]).astype(jnp.bfloat16)
 
@@ -220,47 +226,41 @@
             perm_of(s_ref),
             [s_ref[2 + i] for i in range(users)],
             refs[:ctx_count],
-            refs[ctx_count],
-            refs[ctx_count + 1 :],
+            refs[-1],
+            refs[ctx_count + 2 : -1],
             heads,
             rows,
         )
+        size = whole // 2
+        for i in range(2):
+            refs[ctx_count + i][...] = refs[-1][i * size : (i + 1) * size, :]
 
     grad_pre = call(
         main,
         [scalars],
         arrived,
-        [bf16(whole, wide)],
-        attention_scratch(heads, rows, ctx_count),
+        [bf16(whole // 2, wide)] * 2,
+        attention_scratch(heads, rows, ctx_count) + [pltpu.VMEM((whole, wide), jnp.bfloat16)],
         12 * product_flops,
-    )[0]
-
-    kept, sent = half_columns(me_dp, layer_input[0], dp_count)
-    sent = after(sent, pieces)
-    tokens, mask = {0: jnp.stack([kept, swap(sent, "dp", 1)])}, ctx_count // 2
-    tokens[0] = after(tokens[0], arrived[1])
-    while mask:
-        for r in sorted(tokens):
-            tokens[r ^ mask] = swap(after(tokens[r], grad_pre) if r else tokens[r], "ctx", mask)
-        mask //= 2
-    tokens = [tokens[r] for r in range(ctx_count)]
-
-    grad_pair = swap(grad_pre, "dp", 1)
-
-    def input_terms(s_ref, grad_ref, *refs):
-        pair_refs, terms, band = refs[:chips], refs[chips:-1], refs[-1]
+    )
+    grad_pre = list(grad_pre)
+
+    def input_terms(s_ref, *refs):
+        grad_refs, pair_refs, terms, band = refs[:2], refs[2 : 2 + chips], refs[2 + chips : -1], refs[-1]
+        size = ctx_count // 2
         for r in range(chips):
             band[row_block((s_ref[1] >> 1) ^ r, 2 * w_rows), :] = pair_refs[r][...]
         step = min(256, width)
         for at in range(0, width, step):
-            product = dot(grad_ref[...], band[at : at + step, :], BY_COLS).astype(jnp.bfloat16)
-            for r in range(ctx_count):
-                terms[r][:, at : at + step] = product[r * rows : (r + 1) * rows]
+            for i in range(2):
+                product = dot(grad_refs[i][...], band[at : at + step, :], BY_COLS).astype(jnp.bfloat16)
+                for r in range(size):
+                    terms[i * size + r][:, at : at + step] = product[r * rows : (r + 1) * rows]
 
     terms = call(
         input_terms,
         [scalars],
-        [grad_pre] + pairs,
+        grad_pre + pairs,
         [bf16(rows, width)] * ctx_count,
         [pltpu.VMEM((width, wide), jnp.bfloat16)],
         50 * product_flops,
@@ -269,15 +269,31 @@
     for r in range(ctx_count - 1, 0, -1):
         returned[r] = swap(terms[r], "ctx", r)
 
-    def weight_terms(own_ref, pair_ref, *refs):
-        token_refs = refs[:ctx_count]
-        outs, (held, grads) = refs[ctx_count:-2], refs[-2:]
+    tokens = {0: half_columns(me_dp, layer_input[0], swap(layer_input[0], "dp", 1), dp_count)}
+    mask = ctx_count // 2
+    tokens[0] = tokens[0]
+    near = swap(tokens[0], "ctx", 1)
+    tokens[0] = after(tokens[0], near, arrived)
+    while mask > 1:
+        for r in sorted(tokens):
+            tokens[r ^ mask] = swap(tokens[r], "ctx", mask)
+        mask //= 2
+    for r in sorted(tokens):
+        tokens[r ^ 1] = swap(tokens[r], "ctx", 1) if r else near
+    tokens = [tokens[r] for r in range(ctx_count)]
+
+    grad_pair = [swap(part, "dp", 1) for part in grad_pre]
+
+    def weight_terms(*refs):
+        token_refs = refs[2 * 2 : 2 * 2 + ctx_count]
+        outs, (held, grads) = refs[2 * 2 + ctx_count : -2], refs[-2:]
         for r in range(ctx_count):
             for i in range(2):
                 at = i * whole + r * rows
                 held[at : at + rows, :] = token_refs[r][i]
-        grads[:whole, :] = own_ref[...]
-        grads[whole:, :] = pair_ref[...]
+        size = whole // 2
+        for i in range(2 * 2):
+            grads[i * size : (i + 1) * size, :] = refs[i][...]
         product = dot(held[...], grads[...], BY_ROWS)
         for r in range(chips):
             outs[r][...] = product[r * w_rows : (r + 1) * w_rows].astype(outs[r].dtype)
@@ -285,19 +301,29 @@
     own, *outgoing = call(
         weight_terms,
         [],
-        [grad_pre, grad_pair] + tokens,
+        grad_pre + grad_pair + tokens,
         [f32(w_rows, wide)] + [bf16(w_rows, wide)] * (chips - 1),
         [pltpu.VMEM((2 * whole, width // 2), jnp.bfloat16), pltpu.VMEM((2 * whole, wide), jnp.bfloat16)],
         product_flops,
     )
-    total = own
-    for r in range(1, chips):
-        total = total + swap(outgoing[r - 1], "dp", 2 * r).astype(jnp.float32)
-    grad_weight = total * (1.0 / dp_count)
-    input_grad = returned[0].astype(jnp.float32)
-    for block in returned[1:]:
-        input_grad = input_grad + block.astype(jnp.float32)
-    return (input_grad.astype(jnp.bfloat16)[None], grad_weight)
+    incoming = [swap(block, "dp", 2 * (r + 1)) for r, block in enumerate(outgoing)]
+
+    def sums(own_ref, *refs):
+        chip_refs, term_refs = refs[: chips - 1], refs[chips - 1 : chips - 1 + ctx_count]
+        weight_out, input_out = refs[-2:]
+        total = own_ref[...]
+        for ref in chip_refs:
+            total = total + ref[...].astype(jnp.float32)
+        weight_out[...] = total * (1.0 / dp_count)
+        total = term_refs[0][...].astype(jnp.float32)
+        for ref in term_refs[1:]:
+            total = total + ref[...].astype(jnp.float32)
+        input_out[...] = total.astype(jnp.bfloat16)
+
+    grad_weight, input_grad = call(
+        sums, [], [own] + incoming + returned, [f32(w_rows, wide), bf16(rows, width)]
+    )
+    return (input_grad[None], grad_weight)
 
 
 def solution(mesh):

time: 75.7 us -> 73.1 us (0.966)
  waiting for transfers between devices: 41.1 us -> 38.9 us
  starting transfers between devices: 19.4 us -> 21.2 us
  other arithmetic: 1.81 us -> 0.08 us
    ppermute x18 -> x19, waiting for transfers between devices: 41.1 us -> 38.9 us  [swap(): return lax.ppermute(array, axis, [(i, i ^ mask) for i in range(count)])]
    ppermute x18 -> x19, starting transfers between devices: 19.4 us -> 21.2 us  [swap(): return lax.ppermute(array, axis, [(i, i ^ mask) for i in range(count)])]
    broadcast_in_dim x1 -> x0, other arithmetic: 0.87 us -> none  [body(): return (input_grad.astype(jnp.bfloat16)[None], grad_weight)]
    mul x1 -> x0, other arithmetic: 0.84 us -> none  [body(): grad_weight = total * (1.0 / dp_count)]
    pallas_call x6 -> x7, Pallas kernels: 8.8 us -> 8.85 us  [call(): pl.pallas_call(kernel, out_shape=list(outs), in_specs=[pl.BlockSpec(memor...]
  transfers between devices with their start and end apart: 18 -> 19, of which waited for: 9 -> 8; matrix products, arithmetic and copies ran while one was open for 1% -> 0% of each run, Pallas kernels for 11% -> 11%
where the time goes in v3:
time: 73.1 us; the launch traced here: 72.6 us
  waiting for transfers between devices  38.9 us (53%)
  starting transfers between devices  21.2 us (29%)
  Pallas kernels  8.85 us (12%)
  local copies, waits for them, and re-layouts  2.75 us (4%)
  between operations  0.74 us (1%)
    ppermute x19, waiting for transfers between devices, swap(): return lax.ppermute(array, axis, [(i, i ^ mask) for i in range(count)])  38.9 us
    ppermute x19, starting transfers between devices, swap(): return lax.ppermute(array, axis, [(i, i ^ mask) for i in range(count)])  21.2 us
    pallas_call x7, Pallas kernels, call(): pl.pallas_call(kernel, out_shape=list(outs), in_specs=[pl.BlockSpec(memor...  8.85 us
    unnamed x12, local copies, waits for them, and re-layouts  2.75 us
  transfers between devices with their start and end apart: 19, of which 8 were waited for; matrix products, arithmetic and copies ran while one was open for 0% of the time, Pallas kernels for 11%

profile of v3, /device:TPU:18, one launch (start us, length us, event | category | flops | bytes accessed | tf_op | source)
XLA Modules:
  0.0 72.6 jit_solution(2460482174778807500)
XLA Ops:
  0.6 0.1 collective-permute-start.5
  0.7 1.1 %copy-done = bf16[1,128,3072]{2,1,0:T(8,128)(2,1)S(1)} copy-done((bf16[1,128,3072]{2,1,0:T(8,128)(2,1)S(1)}, bf16[1,128,3072]{2,1,0:T(8,128)(2,1)}, u32[]{:S(2)}) %copy-start) | copy-done | bytes 786456
  1.8 0.9 %copy-done.1 = bf16[1,128,1024]{2,1,0:T(8,128)(2,1)S(1)} copy-done((bf16[1,128,1024]{2,1,0:T(8,128)(2,1)S(1)}, bf16[1,128,1024]{2,1,0:T(8,128)(2,1)}, u32[]{:S(2)}) %copy-start.1) | copy-done | bytes 262168
  2.8 0.2 shard_map.77
  3.0 1.6 %collective-permute-start = (bf16[128,1024]{1,0:T(8,128)(2,1)S(1)}, bf16[128,1024]{1,0:T(8,128)(2,1)S(1)}, u32[]{:S(2)}, u32[]{:S(2)}) collective-permute-start(bf16[128,1024]{1,0:T(8,128)(2,1)S(1)} %get-tuple-element.21), channel_id=1, source_target_pairs={{0,1},{1,0},{2,3},{3,2},{4,5},{5,4},{6,7},{7,6},{8,9},{9,8},{10,11... | collective-permute-start | bytes 786440 | tf_op jit(solution)/shard_map/ppermute | solution.py:50
  4.7 0.3 collective-permute-start.1
  5.0 1.6 %collective-permute-start.2 = (bf16[128,1024]{1,0:T(8,128)(2,1)S(1)}, bf16[128,1024]{1,0:T(8,128)(2,1)S(1)}, u32[]{:S(2)}, u32[]{:S(2)}) collective-permute-start(bf16[128,1024]{1,0:T(8,128)(2,1)S(1)} %get-tuple-element.23), channel_id=1, source_target_pairs={{0,3},{1,2},{2,1},{3,0},{4,7},{5,6},{6,5},{7,4},{8,11},{9,10},{10,... | collective-permute-start | bytes 786440 | tf_op jit(solution)/shard_map/ppermute | solution.py:50
  6.6 0.0 collective-permute-done.5.other_ref
  6.6 0.1 shard_map.79.refs_4_
  6.7 2.5 %collective-permute-start.6 = (bf16[2,128,512]{2,1,0:T(8,128)(2,1)S(1)}, bf16[2,128,512]{2,1,0:T(8,128)(2,1)S(1)}, u32[]{:S(2)}, u32[]{:S(2)}) collective-permute-start(bf16[2,128,512]{2,1,0:T(8,128)(2,1)S(1)} %shard_map.79.refs_4_), channel_id=1, source_target_pairs={{0,1},{1,0},{2,3},{3,2},{4,5},{5,4},{6,7},{7,6},{8,9},{9,8},{10,11... | collective-permute-start | bytes 786440 | tf_op jit(solution)/shard_map/ppermute | solution.py:50
  9.2 0.0 collective-permute-start.12
  9.2 0.6 copy-done.4
  9.9 0.0 copy-done.5
  9.9 0.1 pad_add_fusion.s_ref
  10.0 0.7 collective-permute-done.12.other_ref
  10.7 1.6 %collective-permute-start.15 = (bf16[256,768]{1,0:T(8,128)(2,1)S(1)}, bf16[256,768]{1,0:T(8,128)(2,1)S(1)}, u32[]{:S(2)}, u32[]{:S(2)}) collective-permute-start(bf16[256,768]{1,0:T(8,128)(2,1)S(1)} %shard_map.81.refs_2_), channel_id=1, source_target_pairs={{0,24},{4,28},{8,16},{12,20},{16,8},{20,12},{24,0},{28,4},{1,25},{... | collective-permute-start | bytes 1179656 | tf_op jit(solution)/shard_map/ppermute | solution.py:50
  12.3 3.4 %collective-permute-done.refs_1_ = bf16[128,1024]{1,0:T(8,128)(2,1)S(1)} collective-permute-done((bf16[128,1024]{1,0:T(8,128)(2,1)S(1)}, bf16[128,1024]{1,0:T(8,128)(2,1)S(1)}, u32[]{:S(2)}, u32[]{:S(2)}) %collective-permute-start) | collective-permute-done | bytes 262176 | tf_op jit(solution)/shard_map/ppermute | solution.py:50
  15.7 1.5 %collective-permute-start.14 = (bf16[256,768]{1,0:T(8,128)(2,1)S(1)}, bf16[256,768]{1,0:T(8,128)(2,1)S(1)}, u32[]{:S(2)}, u32[]{:S(2)}) collective-permute-start(bf16[256,768]{1,0:T(8,128)(2,1)S(1)} %shard_map.81.refs_2_), channel_id=1, source_target_pairs={{0,16},{4,20},{8,24},{12,28},{16,0},{20,4},{24,8},{28,12},{1,17},{... | collective-permute-start | bytes 1179656 | tf_op jit(solution)/shard_map/ppermute | solution.py:50
  17.2 5.7 %collective-permute-done.1.refs_2_ = bf16[128,1024]{1,0:T(8,128)(2,1)S(1)} collective-permute-done((bf16[128,1024]{1,0:T(8,128)(2,1)S(1)}, bf16[128,1024]{1,0:T(8,128)(2,1)S(1)}, u32[]{:S(2)}, u32[]{:S(2)}) %collective-permute-start.1) | collective-permute-done | bytes 262176 | tf_op jit(solution)/shard_map/ppermute | solution.py:50
  22.9 0.5 collective-permute-start.13
  23.4 6.5 %collective-permute-done.2.refs_3_ = bf16[128,1024]{1,0:T(8,128)(2,1)S(1)} collective-permute-done((bf16[128,1024]{1,0:T(8,128)(2,1)S(1)}, bf16[128,1024]{1,0:T(8,128)(2,1)S(1)}, u32[]{:S(2)}, u32[]{:S(2)}) %collective-permute-start.2) | collective-permute-done | bytes 262176 | tf_op jit(solution)/shard_map/ppermute | solution.py:50
  29.9 0.0 collective-permute-done.6.refs_5_
  29.9 0.0 collective-permute-start.7
  29.9 4.8 %shard_map.78 = (bf16[256,768]{1,0:T(8,128)(2,1)S(1)}, bf16[256,768]{1,0:T(8,128)(2,1)S(1)}) custom-call(s32[14]{0:T(128)S(1)} %pad_add_fusion.s_ref, bf16[128,1024]{1,0:T(8,128)(2,1)S(1)} %get-tuple-element.20.refs_0_, bf16[128,1024]{1,0:T(8,128)(2,1)S(1)} %collective-permute-done.refs_1_, bf16[128,1024]{1,0:T(8,128)(2,1)S(1)} %collective-permute-done.1.refs_2_, ...), custom_call_target="tpu_custom_call" | custom-call | flops 9663676416 | bytes 1835008 | tf_op jit(solution)/shard_map/pallas_call | solution.py:24
  34.8 0.1 collective-permute-start.3
  34.9 0.0 collective-permute-done.15.refs_5_
  34.9 0.5 collective-permute-start.4
  35.4 5.6 %collective-permute-done.7.refs_6_ = bf16[2,128,512]{2,1,0:T(8,128)(2,1)S(1)} collective-permute-done((bf16[2,128,512]{2,1,0:T(8,128)(2,1)S(1)}, bf16[2,128,512]{2,1,0:T(8,128)(2,1)S(1)}, u32[]{:S(2)}, u32[]{:S(2)}) %collective-permute-start.7) | collective-permute-done | bytes 262176 | tf_op jit(solution)/shard_map/ppermute | solution.py:50
  41.0 3.7 %collective-permute-start.8 = (bf16[2,128,512]{2,1,0:T(8,128)(2,1)S(1)}, bf16[2,128,512]{2,1,0:T(8,128)(2,1)S(1)}, u32[]{:S(2)}, u32[]{:S(2)}) collective-permute-start(bf16[2,128,512]{2,1,0:T(8,128)(2,1)S(1)} %collective-permute-done.7.refs_6_), channel_id=1, source_target_pairs={{0,1},{1,0},{2,3},{3,2},{4,5},{5,4},{6,7},{7,6},{8,9},{9,8},{10,11... | collective-permute-start | bytes 786440 | tf_op jit(solution)/shard_map/ppermute | solution.py:50
  44.7 0.0 collective-permute-done.14.refs_4_
  44.7 0.0 collective-permute-done.13.refs_3_
  44.7 1.7 %shard_map.82 = (bf16[128,1024]{1,0:T(8,128)(2,1)S(1)}, bf16[128,1024]{1,0:T(8,128)(2,1)S(1)}, bf16[128,1024]{1,0:T(8,128)(2,1)S(1)}, bf16[128,1024]{1,0:T(8,128)(2,1)S(1)}) custom-call(s32[14]{0:T(128)S(1)} %pad_add_fusion.s_ref, bf16[256,768]{1,0:T(8,128)(2,1)S(1)} %get-tuple-element.24.refs_0_, bf16[256,768]{1,0:T(8,128)(2,1)S(1)} %get-tuple-element.25.refs_1_, ...), custom_call_target="tpu_custom_call" | custom-call | flops 40265318400 | bytes 3407872 | tf_op jit(solution)/shard_map/pallas_call | solution.py:24
  46.4 0.1 collective-permute-start.16
  46.4 1.7 %collective-permute-start.17 = (bf16[128,1024]{1,0:T(8,128)(2,1)S(1)}, bf16[128,1024]{1,0:T(8,128)(2,1)S(1)}, u32[]{:S(2)}, u32[]{:S(2)}) collective-permute-start(bf16[128,1024]{1,0:T(8,128)(2,1)S(1)} %get-tuple-element.34), channel_id=1, source_target_pairs={{0,2},{1,3},{2,0},{3,1},{4,6},{5,7},{6,4},{7,5},{8,10},{9,11},{10,... | collective-permute-start | bytes 786440 | tf_op jit(solution)/shard_map/ppermute | solution.py:50
  48.1 0.0 collective-permute-done.3.refs_2_
  48.1 1.8 %collective-permute-start.18 = (bf16[128,1024]{1,0:T(8,128)(2,1)S(1)}, bf16[128,1024]{1,0:T(8,128)(2,1)S(1)}, u32[]{:S(2)}, u32[]{:S(2)}) collective-permute-start(bf16[128,1024]{1,0:T(8,128)(2,1)S(1)} %get-tuple-element.35), channel_id=1, source_target_pairs={{0,3},{1,2},{2,1},{3,0},{4,7},{5,6},{6,5},{7,4},{8,11},{9,10},{10,... | collective-permute-start | bytes 786440 | tf_op jit(solution)/shard_map/ppermute | solution.py:50
  49.9 0.0 collective-permute-done.4.refs_3_
  49.9 6.0 %collective-permute-done.8.refs_7_ = bf16[2,128,512]{2,1,0:T(8,128)(2,1)S(1)} collective-permute-done((bf16[2,128,512]{2,1,0:T(8,128)(2,1)S(1)}, bf16[2,128,512]{2,1,0:T(8,128)(2,1)S(1)}, u32[]{:S(2)}, u32[]{:S(2)}) %collective-permute-start.8) | collective-permute-done | bytes 262176 | tf_op jit(solution)/shard_map/ppermute | solution.py:50
  55.9 1.0 %shard_map.80 = (f32[128,768]{1,0:T(8,128)S(1)}, bf16[128,768]{1,0:T(8,128)(2,1)S(1)}, bf16[128,768]{1,0:T(8,128)(2,1)S(1)}, bf16[128,768]{1,0:T(8,128)(2,1)S(1)}) custom-call(bf16[256,768]{1,0:T(8,128)(2,1)S(1)} %get-tuple-element.24.refs_0_, bf16[256,768]{1,0:T(8,128)(2,1)S(1)} %get-tuple-element.25.refs_1_, ...), custom_call_target="tpu_custom_call" | custom-call | flops 805306368 | bytes 3604480 | tf_op jit(solution)/shard_map/pallas_call | solution.py:24
  56.9 0.6 collective-permute-start.9
  57.5 1.5 %collective-permute-start.10 = (bf16[128,768]{1,0:T(8,128)(2,1)S(1)}, bf16[128,768]{1,0:T(8,128)(2,1)S(1)}, u32[]{:S(2)}, u32[]{:S(2)}) collective-permute-start(bf16[128,768]{1,0:T(8,128)(2,1)S(1)} %get-tuple-element.29), channel_id=1, source_target_pairs={{0,16},{4,20},{8,24},{12,28},{16,0},{20,4},{24,8},{28,12},{1,17},{... | collective-permute-start | bytes 589832 | tf_op jit(solution)/shard_map/ppermute | solution.py:50
  59.1 2.5 %collective-permute-done.16.refs_4_ = bf16[128,1024]{1,0:T(8,128)(2,1)S(1)} collective-permute-done((bf16[128,1024]{1,0:T(8,128)(2,1)S(1)}, bf16[128,1024]{1,0:T(8,128)(2,1)S(1)}, u32[]{:S(2)}, u32[]{:S(2)}) %collective-permute-start.16) | collective-permute-done | bytes 262176 | tf_op jit(solution)/shard_map/ppermute | solution.py:50
  61.5 1.5 %collective-permute-start.11 = (bf16[128,768]{1,0:T(8,128)(2,1)S(1)}, bf16[128,768]{1,0:T(8,128)(2,1)S(1)}, u32[]{:S(2)}, u32[]{:S(2)}) collective-permute-start(bf16[128,768]{1,0:T(8,128)(2,1)S(1)} %get-tuple-element.30), channel_id=1, source_target_pairs={{0,24},{4,28},{8,16},{12,20},{16,8},{20,12},{24,0},{28,4},{1,25},{... | collective-permute-start | bytes 589832 | tf_op jit(solution)/shard_map/ppermute | solution.py:50
  63.0 0.0 collective-permute-done.17.refs_5_
  63.0 8.6 %collective-permute-done.18.refs_6_ = bf16[128,1024]{1,0:T(8,128)(2,1)S(1)} collective-permute-done((bf16[128,1024]{1,0:T(8,128)(2,1)S(1)}, bf16[128,1024]{1,0:T(8,128)(2,1)S(1)}, u32[]{:S(2)}, u32[]{:S(2)}) %collective-permute-start.18) | collective-permute-done | bytes 262176 | tf_op jit(solution)/shard_map/ppermute | solution.py:50
  71.6 0.0 collective-permute-done.9.refs_0_
  71.6 0.0 collective-permute-done.10.refs_1_
  71.6 1.0 %shard_map.83 = (f32[128,768]{1,0:T(8,128)}, bf16[128,1024]{1,0:T(8,128)(2,1)}) custom-call(f32[128,768]{1,0:T(8,128)S(1)} %get-tuple-element.27.own_ref, bf16[128,768]{1,0:T(8,128)(2,1)S(1)} %collective-permute-done.9.refs_0_, bf16[128,768]{1,0:T(8,128)(2,1)S(1)} %collective-permute-done.10.refs_1_, bf16[128,768]{1,0:T(8,128)(2,1)S(1)} %collective-permute-done.11.refs_2_, ...), custom_call_target="tpu_custom_call" | custom-call | bytes 2686976 | tf_op jit(solution)/shard_map/pallas_call | solution.py:24
  (10 shorter events, 0.0 us)
Async XLA Ops:
  0.6 6.0 %collective-permute-start.5 = (bf16[128,1024]{1,0:T(8,128)(2,1)}, bf16[128,1024]{1,0:T(8,128)(2,1)S(1)}, u32[]{:S(2)}, u32[]{:S(2)}) collective-permute-start(bf16[128,1024]{1,0:T(8,128)(2,1)} %bitcast.10), channel_id=1, source_target_pairs={{0,4},{4,0},{8,12},{12,8},{16,20},{20,16},{24,28},{28,24},{1,5},{5... | collective-permute-start | bytes 786440 | tf_op jit(solution)/shard_map/ppermute | solution.py:50
  0.7 1.1 %copy-start = (bf16[1,128,3072]{2,1,0:T(8,128)(2,1)S(1)}, bf16[1,128,3072]{2,1,0:T(8,128)(2,1)}, u32[]{:S(2)}) copy-start(bf16[1,128,3072]{2,1,0:T(8,128)(2,1)} %param.7) | copy-start | bytes 2359300
  1.8 0.9 %copy-start.1 = (bf16[1,128,1024]{2,1,0:T(8,128)(2,1)S(1)}, bf16[1,128,1024]{2,1,0:T(8,128)(2,1)}, u32[]{:S(2)}) copy-start(bf16[1,128,1024]{2,1,0:T(8,128)(2,1)} %param.8) | copy-start | bytes 786436
  2.8 3.8 %copy-start.2 = (bf16[1,128,1024]{2,1,0:T(8,128)(2,1)S(1)}, bf16[1,128,1024]{2,1,0:T(8,128)(2,1)}, u32[]{:S(2)}) copy-start(bf16[1,128,1024]{2,1,0:T(8,128)(2,1)} %param.6) | copy-start | bytes 786436
  3.0 12.6 %collective-permute-start = (bf16[128,1024]{1,0:T(8,128)(2,1)S(1)}, bf16[128,1024]{1,0:T(8,128)(2,1)S(1)}, u32[]{:S(2)}, u32[]{:S(2)}) collective-permute-start(bf16[128,1024]{1,0:T(8,128)(2,1)S(1)} %get-tuple-element.21), channel_id=1, source_target_pairs={{0,1},{1,0},{2,3},{3,2},{4,5},{5,4},{6,7},{7,6},{8,9},{9,8},{10,11... | collective-permute-start | bytes 786440 | tf_op jit(solution)/shard_map/ppermute | solution.py:50
  4.7 18.2 %collective-permute-start.1 = (bf16[128,1024]{1,0:T(8,128)(2,1)S(1)}, bf16[128,1024]{1,0:T(8,128)(2,1)S(1)}, u32[]{:S(2)}, u32[]{:S(2)}) collective-permute-start(bf16[128,1024]{1,0:T(8,128)(2,1)S(1)} %get-tuple-element.22), channel_id=1, source_target_pairs={{0,2},{1,3},{2,0},{3,1},{4,6},{5,7},{6,4},{7,5},{8,10},{9,11},{10,... | collective-permute-start | bytes 786440 | tf_op jit(solution)/shard_map/ppermute | solution.py:50
  5.0 24.9 %collective-permute-start.2 = (bf16[128,1024]{1,0:T(8,128)(2,1)S(1)}, bf16[128,1024]{1,0:T(8,128)(2,1)S(1)}, u32[]{:S(2)}, u32[]{:S(2)}) collective-permute-start(bf16[128,1024]{1,0:T(8,128)(2,1)S(1)} %get-tuple-element.23), channel_id=1, source_target_pairs={{0,3},{1,2},{2,1},{3,0},{4,7},{5,6},{6,5},{7,4},{8,11},{9,10},{10,... | collective-permute-start | bytes 786440 | tf_op jit(solution)/shard_map/ppermute | solution.py:50
  6.6 2.6 %copy-start.3 = (bf16[128,768]{1,0:T(8,128)(2,1)S(1)}, bf16[128,768]{1,0:T(8,128)(2,1)}, u32[]{:S(2)}) copy-start(bf16[128,768]{1,0:T(8,128)(2,1)} %own_ref.1) | copy-start | bytes 589828
  6.7 23.3 %collective-permute-start.6 = (bf16[2,128,512]{2,1,0:T(8,128)(2,1)S(1)}, bf16[2,128,512]{2,1,0:T(8,128)(2,1)S(1)}, u32[]{:S(2)}, u32[]{:S(2)}) collective-permute-start(bf16[2,128,512]{2,1,0:T(8,128)(2,1)S(1)} %shard_map.79.refs_4_), channel_id=1, source_target_pairs={{0,1},{1,0},{2,3},{3,2},{4,5},{5,4},{6,7},{7,6},{8,9},{9,8},{10,11... | collective-permute-start | bytes 786440 | tf_op jit(solution)/shard_map/ppermute | solution.py:50
  9.2 1.4 %collective-permute-start.12 = (bf16[128,768]{1,0:T(8,128)(2,1)S(1)}, bf16[128,768]{1,0:T(8,128)(2,1)S(1)}, u32[]{:S(2)}, u32[]{:S(2)}) collective-permute-start(bf16[128,768]{1,0:T(8,128)(2,1)S(1)} %copy-done.3), channel_id=1, source_target_pairs={{0,4},{4,0},{8,12},{12,8},{16,20},{20,16},{24,28},{28,24},{1,5},{5... | collective-permute-start | bytes 589832 | tf_op jit(solution)/shard_map/ppermute | solution.py:50
  9.2 0.7 copy-start.4
  9.2 0.7 copy-start.5
  10.7 24.2 %collective-permute-start.15 = (bf16[256,768]{1,0:T(8,128)(2,1)S(1)}, bf16[256,768]{1,0:T(8,128)(2,1)S(1)}, u32[]{:S(2)}, u32[]{:S(2)}) collective-permute-start(bf16[256,768]{1,0:T(8,128)(2,1)S(1)} %shard_map.81.refs_2_), channel_id=1, source_target_pairs={{0,24},{4,28},{8,16},{12,20},{16,8},{20,12},{24,0},{28,4},{1,25},{... | collective-permute-start | bytes 1179656 | tf_op jit(solution)/shard_map/ppermute | solution.py:50
  15.7 29.0 %collective-permute-start.14 = (bf16[256,768]{1,0:T(8,128)(2,1)S(1)}, bf16[256,768]{1,0:T(8,128)(2,1)S(1)}, u32[]{:S(2)}, u32[]{:S(2)}) collective-permute-start(bf16[256,768]{1,0:T(8,128)(2,1)S(1)} %shard_map.81.refs_2_), channel_id=1, source_target_pairs={{0,16},{4,20},{8,24},{12,28},{16,0},{20,4},{24,8},{28,12},{1,17},{... | collective-permute-start | bytes 1179656 | tf_op jit(solution)/shard_map/ppermute | solution.py:50
  22.9 21.8 %collective-permute-start.13 = (bf16[256,768]{1,0:T(8,128)(2,1)S(1)}, bf16[256,768]{1,0:T(8,128)(2,1)S(1)}, u32[]{:S(2)}, u32[]{:S(2)}) collective-permute-start(bf16[256,768]{1,0:T(8,128)(2,1)S(1)} %shard_map.81.refs_2_), channel_id=1, source_target_pairs={{0,8},{4,12},{8,0},{12,4},{16,24},{20,28},{24,16},{28,20},{1,9},{5... | collective-permute-start | bytes 1179656 | tf_op jit(solution)/shard_map/ppermute | solution.py:50
  29.9 11.0 %collective-permute-start.7 = (bf16[2,128,512]{2,1,0:T(8,128)(2,1)S(1)}, bf16[2,128,512]{2,1,0:T(8,128)(2,1)S(1)}, u32[]{:S(2)}, u32[]{:S(2)}) collective-permute-start(bf16[2,128,512]{2,1,0:T(8,128)(2,1)S(1)} %shard_map.79.refs_4_), channel_id=1, source_target_pairs={{0,2},{1,3},{2,0},{3,1},{4,6},{5,7},{6,4},{7,5},{8,10},{9,11},{10,... | collective-permute-start | bytes 786440 | tf_op jit(solution)/shard_map/ppermute | solution.py:50
  34.8 13.3 %collective-permute-start.3 = (bf16[256,768]{1,0:T(8,128)(2,1)S(1)}, bf16[256,768]{1,0:T(8,128)(2,1)S(1)}, u32[]{:S(2)}, u32[]{:S(2)}) collective-permute-start(bf16[256,768]{1,0:T(8,128)(2,1)S(1)} %get-tuple-element.24.refs_0_), channel_id=1, source_target_pairs={{0,4},{4,0},{8,12},{12,8},{16,20},{20,16},{24,28},{28,24},{1,5},{5... | collective-permute-start | bytes 1179656 | tf_op jit(solution)/shard_map/ppermute | solution.py:50
  34.9 15.0 %collective-permute-start.4 = (bf16[256,768]{1,0:T(8,128)(2,1)S(1)}, bf16[256,768]{1,0:T(8,128)(2,1)S(1)}, u32[]{:S(2)}, u32[]{:S(2)}) collective-permute-start(bf16[256,768]{1,0:T(8,128)(2,1)S(1)} %get-tuple-element.25.refs_1_), channel_id=1, source_target_pairs={{0,4},{4,0},{8,12},{12,8},{16,20},{20,16},{24,28},{28,24},{1,5},{5... | collective-permute-start | bytes 1179656 | tf_op jit(solution)/shard_map/ppermute | solution.py:50
  41.0 14.9 %collective-permute-start.8 = (bf16[2,128,512]{2,1,0:T(8,128)(2,1)S(1)}, bf16[2,128,512]{2,1,0:T(8,128)(2,1)S(1)}, u32[]{:S(2)}, u32[]{:S(2)}) collective-permute-start(bf16[2,128,512]{2,1,0:T(8,128)(2,1)S(1)} %collective-permute-done.7.refs_6_), channel_id=1, source_target_pairs={{0,1},{1,0},{2,3},{3,2},{4,5},{5,4},{6,7},{7,6},{8,9},{9,8},{10,11... | collective-permute-start | bytes 786440 | tf_op jit(solution)/shard_map/ppermute | solution.py:50
  46.4 15.2 %collective-permute-start.16 = (bf16[128,1024]{1,0:T(8,128)(2,1)S(1)}, bf16[128,1024]{1,0:T(8,128)(2,1)S(1)}, u32[]{:S(2)}, u32[]{:S(2)}) collective-permute-start(bf16[128,1024]{1,0:T(8,128)(2,1)S(1)} %get-tuple-element.33), channel_id=1, source_target_pairs={{0,1},{1,0},{2,3},{3,2},{4,5},{5,4},{6,7},{7,6},{8,9},{9,8},{10,11... | collective-permute-start | bytes 786440 | tf_op jit(solution)/shard_map/ppermute | solution.py:50
  46.4 16.6 %collective-permute-start.17 = (bf16[128,1024]{1,0:T(8,128)(2,1)S(1)}, bf16[128,1024]{1,0:T(8,128)(2,1)S(1)}, u32[]{:S(2)}, u32[]{:S(2)}) collective-permute-start(bf16[128,1024]{1,0:T(8,128)(2,1)S(1)} %get-tuple-element.34), channel_id=1, source_target_pairs={{0,2},{1,3},{2,0},{3,1},{4,6},{5,7},{6,4},{7,5},{8,10},{9,11},{10,... | collective-permute-start | bytes 786440 | tf_op jit(solution)/shard_map/ppermute | solution.py:50
  48.1 23.5 %collective-permute-start.18 = (bf16[128,1024]{1,0:T(8,128)(2,1)S(1)}, bf16[128,1024]{1,0:T(8,128)(2,1)S(1)}, u32[]{:S(2)}, u32[]{:S(2)}) collective-permute-start(bf16[128,1024]{1,0:T(8,128)(2,1)S(1)} %get-tuple-element.35), channel_id=1, source_target_pairs={{0,3},{1,2},{2,1},{3,0},{4,7},{5,6},{6,5},{7,4},{8,11},{9,10},{10,... | collective-permute-start | bytes 786440 | tf_op jit(solution)/shard_map/ppermute | solution.py:50
  56.9 14.6 %collective-permute-start.9 = (bf16[128,768]{1,0:T(8,128)(2,1)S(1)}, bf16[128,768]{1,0:T(8,128)(2,1)S(1)}, u32[]{:S(2)}, u32[]{:S(2)}) collective-permute-start(bf16[128,768]{1,0:T(8,128)(2,1)S(1)} %get-tuple-element.28), channel_id=1, source_target_pairs={{0,8},{4,12},{8,0},{12,4},{16,24},{20,28},{24,16},{28,20},{1,9},{5... | collective-permute-start | bytes 589832 | tf_op jit(solution)/shard_map/ppermute | solution.py:50
  57.5 14.1 %collective-permute-start.10 = (bf16[128,768]{1,0:T(8,128)(2,1)S(1)}, bf16[128,768]{1,0:T(8,128)(2,1)S(1)}, u32[]{:S(2)}, u32[]{:S(2)}) collective-permute-start(bf16[128,768]{1,0:T(8,128)(2,1)S(1)} %get-tuple-element.29), channel_id=1, source_target_pairs={{0,16},{4,20},{8,24},{12,28},{16,0},{20,4},{24,8},{28,12},{1,17},{... | collective-permute-start | bytes 589832 | tf_op jit(solution)/shard_map/ppermute | solution.py:50
  61.5 10.1 %collective-permute-start.11 = (bf16[128,768]{1,0:T(8,128)(2,1)S(1)}, bf16[128,768]{1,0:T(8,128)(2,1)S(1)}, u32[]{:S(2)}, u32[]{:S(2)}) collective-permute-start(bf16[128,768]{1,0:T(8,128)(2,1)S(1)} %get-tuple-element.30), channel_id=1, source_target_pairs={{0,24},{4,28},{8,16},{12,20},{16,8},{20,12},{24,0},{28,4},{1,25},{... | collective-permute-start | bytes 589832 | tf_op jit(solution)/shard_map/ppermute | solution.py:50

commit v4 on v3

--- a/solution.py
+++ b/solution.py
@@ -227,35 +227,39 @@
             [s_ref[2 + i] for i in range(users)],
             refs[:ctx_count],
             refs[-1],
-            refs[ctx_count + 2 : -1],
+            refs[ctx_count + 1 : -1],
             heads,
             rows,
         )
-        size = whole // 2
-        for i in range(2):
+        size = whole // 1
+        for i in range(1):
             refs[ctx_count + i][...] = refs[-1][i * size : (i + 1) * size, :]
 
     grad_pre = call(
         main,
         [scalars],
         arrived,
-        [bf16(whole // 2, wide)] * 2,
+        [bf16(whole // 1, wide)] * 1,
         attention_scratch(heads, rows, ctx_count) + [pltpu.VMEM((whole, wide), jnp.bfloat16)],
         12 * product_flops,
     )
     grad_pre = list(grad_pre)
 
     def input_terms(s_ref, *refs):
-        grad_refs, pair_refs, terms, band = refs[:2], refs[2 : 2 + chips], refs[2 + chips : -1], refs[-1]
-        size = ctx_count // 2
-        for r in range(chips):
-            band[row_block((s_ref[1] >> 1) ^ r, 2 * w_rows), :] = pair_refs[r][...]
-        step = min(256, width)
-        for at in range(0, width, step):
-            for i in range(2):
-                product = dot(grad_refs[i][...], band[at : at + step, :], BY_COLS).astype(jnp.bfloat16)
-                for r in range(size):
-                    terms[i * size + r][:, at : at + step] = product[r * rows : (r + 1) * rows]
+        grad_refs, pair_refs, terms, band = refs[:1], refs[1 : 1 + chips], refs[1 + chips : -1], refs[-1]
+        size = ctx_count // 1
+        direct = 2 * w_rows % LANES == 0
+        step = 2 * w_rows if direct else min(256, width)
+        if not direct:
+            for r in range(chips):
+                band[row_block((s_ref[1] >> 1) ^ r, 2 * w_rows), :] = pair_refs[r][...]
+        grads = jnp.concatenate([grad[...] for grad in grad_refs], axis=0)
+        for n in range(width // step):
+            rhs = pair_refs[n][...] if direct else band[n * step : (n + 1) * step, :]
+            at = row_block((s_ref[1] >> 1) ^ n if direct else n, step)
+            product = dot(grads, rhs, BY_COLS).astype(jnp.bfloat16)
+            for r in range(ctx_count):
+                terms[r][:, at] = product[r * rows : (r + 1) * rows]
 
     terms = call(
         input_terms,
@@ -273,7 +277,7 @@
     mask = ctx_count // 2
     tokens[0] = tokens[0]
     near = swap(tokens[0], "ctx", 1)
-    tokens[0] = after(tokens[0], near, arrived)
+    tokens[0] = after(tokens[0], near, arrived[1], arrived[2])
     while mask > 1:
         for r in sorted(tokens):
             tokens[r ^ mask] = swap(tokens[r], "ctx", mask)
@@ -285,14 +289,14 @@
     grad_pair = [swap(part, "dp", 1) for part in grad_pre]
 
     def weight_terms(*refs):
-        token_refs = refs[2 * 2 : 2 * 2 + ctx_count]
-        outs, (held, grads) = refs[2 * 2 + ctx_count : -2], refs[-2:]
+        token_refs = refs[2 * 1 : 2 * 1 + ctx_count]
+        outs, (held, grads) = refs[2 * 1 + ctx_count : -2], refs[-2:]
         for r in range(ctx_count):
             for i in range(2):
                 at = i * whole + r * rows
                 held[at : at + rows, :] = token_refs[r][i]
-        size = whole // 2
-        for i in range(2 * 2):
+        size = whole // 1
+        for i in range(2 * 1):
             grads[i * size : (i + 1) * size, :] = refs[i][...]
         product = dot(held[...], grads[...], BY_ROWS)
         for r in range(chips):

time: 73.1 us -> 72 us (0.985); the launches traced: 72.6 us -> 70.7 us
  starting transfers between devices: 21.2 us -> 17.5 us
  waiting for transfers between devices: 38.9 us -> 40.8 us
    ppermute x19 -> x18, starting transfers between devices: 21.2 us -> 17.5 us  [swap(): return lax.ppermute(array, axis, [(i, i ^ mask) for i in range(count)])]
    ppermute x19 -> x18, waiting for transfers between devices: 38.9 us -> 40.8 us  [swap(): return lax.ppermute(array, axis, [(i, i ^ mask) for i in range(count)])]
  transfers between devices with their start and end apart: 19 -> 18, of which waited for: 8 -> 9; matrix products, arithmetic and copies ran while one was open for 0% -> 0% of each run, Pallas kernels for 11% -> 11%
where the time goes in v4:
time: 72 us; the launch traced here: 70.7 us
  waiting for transfers between devices  40.8 us (57%)
  starting transfers between devices  17.5 us (24%)
  Pallas kernels  8.77 us (12%)
  local copies, waits for them, and re-layouts  2.75 us (4%)
  between operations  0.74 us (1%)
    ppermute x18, waiting for transfers between devices, swap(): return lax.ppermute(array, axis, [(i, i ^ mask) for i in range(count)])  40.8 us
    ppermute x18, starting transfers between devices, swap(): return lax.ppermute(array, axis, [(i, i ^ mask) for i in range(count)])  17.5 us
    pallas_call x7, Pallas kernels, call(): pl.pallas_call(kernel, out_shape=list(outs), in_specs=[pl.BlockSpec(memor...  8.77 us
    unnamed x12, local copies, waits for them, and re-layouts  2.75 us
  transfers between devices with their start and end apart: 18, of which 9 were waited for; matrix products, arithmetic and copies ran while one was open for 0% of the time, Pallas kernels for 11%

profile of v4, /device:TPU:18, one launch (start us, length us, event | category | flops | bytes accessed | tf_op | source)
XLA Modules:
  0.0 70.7 jit_solution(14690246333777255437)
XLA Ops:
  0.6 0.1 collective-permute-start.4
  0.7 0.0 copy-start
  0.7 1.1 %copy-done = bf16[1,128,3072]{2,1,0:T(8,128)(2,1)S(1)} copy-done((bf16[1,128,3072]{2,1,0:T(8,128)(2,1)S(1)}, bf16[1,128,3072]{2,1,0:T(8,128)(2,1)}, u32[]{:S(2)}) %copy-start) | copy-done | bytes 786456
  1.8 0.9 %copy-done.1 = bf16[1,128,1024]{2,1,0:T(8,128)(2,1)S(1)} copy-done((bf16[1,128,1024]{2,1,0:T(8,128)(2,1)S(1)}, bf16[1,128,1024]{2,1,0:T(8,128)(2,1)}, u32[]{:S(2)}) %copy-start.1) | copy-done | bytes 262168
  2.8 0.2 shard_map.77
  3.0 1.6 %collective-permute-start = (bf16[128,1024]{1,0:T(8,128)(2,1)S(1)}, bf16[128,1024]{1,0:T(8,128)(2,1)S(1)}, u32[]{:S(2)}, u32[]{:S(2)}) collective-permute-start(bf16[128,1024]{1,0:T(8,128)(2,1)S(1)} %get-tuple-element.19), channel_id=1, source_target_pairs={{0,1},{1,0},{2,3},{3,2},{4,5},{5,4},{6,7},{7,6},{8,9},{9,8},{10,11... | collective-permute-start | bytes 786440 | tf_op jit(solution)/shard_map/ppermute | solution.py:50
  4.7 0.3 collective-permute-start.1
  5.0 0.0 collective-permute-done.4.other_ref
  5.0 0.1 shard_map.79.refs_2_
  5.1 0.5 collective-permute-start.5
  5.6 2.7 %collective-permute-start.2 = (bf16[128,1024]{1,0:T(8,128)(2,1)S(1)}, bf16[128,1024]{1,0:T(8,128)(2,1)S(1)}, u32[]{:S(2)}, u32[]{:S(2)}) collective-permute-start(bf16[128,1024]{1,0:T(8,128)(2,1)S(1)} %get-tuple-element.21), channel_id=1, source_target_pairs={{0,3},{1,2},{2,1},{3,0},{4,7},{5,6},{6,5},{7,4},{8,11},{9,10},{10,... | collective-permute-start | bytes 786440 | tf_op jit(solution)/shard_map/ppermute | solution.py:50
  8.3 0.0 collective-permute-start.11
  8.3 0.6 copy-done.4
  9.0 0.0 copy-done.5
  9.0 0.1 pad_add_fusion.s_ref
  9.1 0.7 collective-permute-done.11.other_ref
  9.8 1.6 %collective-permute-start.14 = (bf16[256,768]{1,0:T(8,128)(2,1)S(1)}, bf16[256,768]{1,0:T(8,128)(2,1)S(1)}, u32[]{:S(2)}, u32[]{:S(2)}) collective-permute-start(bf16[256,768]{1,0:T(8,128)(2,1)S(1)} %shard_map.81.refs_1_), channel_id=1, source_target_pairs={{0,24},{4,28},{8,16},{12,20},{16,8},{20,12},{24,0},{28,4},{1,25},{... | collective-permute-start | bytes 1179656 | tf_op jit(solution)/shard_map/ppermute | solution.py:50
  11.4 4.3 %collective-permute-done.refs_1_ = bf16[128,1024]{1,0:T(8,128)(2,1)S(1)} collective-permute-done((bf16[128,1024]{1,0:T(8,128)(2,1)S(1)}, bf16[128,1024]{1,0:T(8,128)(2,1)S(1)}, u32[]{:S(2)}, u32[]{:S(2)}) %collective-permute-start) | collective-permute-done | bytes 262176 | tf_op jit(solution)/shard_map/ppermute | solution.py:50
  15.7 1.5 %collective-permute-start.13 = (bf16[256,768]{1,0:T(8,128)(2,1)S(1)}, bf16[256,768]{1,0:T(8,128)(2,1)S(1)}, u32[]{:S(2)}, u32[]{:S(2)}) collective-permute-start(bf16[256,768]{1,0:T(8,128)(2,1)S(1)} %shard_map.81.refs_1_), channel_id=1, source_target_pairs={{0,16},{4,20},{8,24},{12,28},{16,0},{20,4},{24,8},{28,12},{1,17},{... | collective-permute-start | bytes 1179656 | tf_op jit(solution)/shard_map/ppermute | solution.py:50
  17.2 0.6 collective-permute-done.1.refs_2_
  17.8 0.5 collective-permute-start.12
  18.3 5.2 %collective-permute-done.5.refs_3_ = bf16[2,128,512]{2,1,0:T(8,128)(2,1)S(1)} collective-permute-done((bf16[2,128,512]{2,1,0:T(8,128)(2,1)S(1)}, bf16[2,128,512]{2,1,0:T(8,128)(2,1)S(1)}, u32[]{:S(2)}, u32[]{:S(2)}) %collective-permute-start.5) | collective-permute-done | bytes 262176 | tf_op jit(solution)/shard_map/ppermute | solution.py:50
  23.5 0.0 collective-permute-start.6
  23.5 12.7 %collective-permute-done.2.refs_3_ = bf16[128,1024]{1,0:T(8,128)(2,1)S(1)} collective-permute-done((bf16[128,1024]{1,0:T(8,128)(2,1)S(1)}, bf16[128,1024]{1,0:T(8,128)(2,1)S(1)}, u32[]{:S(2)}, u32[]{:S(2)}) %collective-permute-start.2) | collective-permute-done | bytes 262176 | tf_op jit(solution)/shard_map/ppermute | solution.py:50
  36.2 4.9 %shard_map.78.refs_0_ = bf16[512,768]{1,0:T(8,128)(2,1)S(1)} custom-call(s32[14]{0:T(128)S(1)} %pad_add_fusion.s_ref, bf16[128,1024]{1,0:T(8,128)(2,1)S(1)} %get-tuple-element.18.refs_0_, bf16[128,1024]{1,0:T(8,128)(2,1)S(1)} %collective-permute-done.refs_1_, bf16[128,1024]{1,0:T(8,128)(2,1)S(1)} %collective-permute-done.1.refs_2_, ...), custom_call_target="tpu_custom_call" | custom-call | flops 9663676416 | bytes 1835008 | tf_op jit(solution)/shard_map/pallas_call | solution.py:24
  41.1 0.1 collective-permute-start.3
  41.2 0.0 collective-permute-done.6.refs_4_
  41.2 1.4 %collective-permute-start.7 = (bf16[2,128,512]{2,1,0:T(8,128)(2,1)S(1)}, bf16[2,128,512]{2,1,0:T(8,128)(2,1)S(1)}, u32[]{:S(2)}, u32[]{:S(2)}) collective-permute-start(bf16[2,128,512]{2,1,0:T(8,128)(2,1)S(1)} %collective-permute-done.6.refs_4_), channel_id=1, source_target_pairs={{0,1},{1,0},{2,3},{3,2},{4,5},{5,4},{6,7},{7,6},{8,9},{9,8},{10,11... | collective-permute-start | bytes 786440 | tf_op jit(solution)/shard_map/ppermute | solution.py:50
  42.6 0.0 collective-permute-done.14.refs_4_
  42.6 0.0 collective-permute-done.13.refs_3_
  42.6 0.0 collective-permute-done.12.refs_2_
  42.6 1.6 %shard_map.82 = (bf16[128,1024]{1,0:T(8,128)(2,1)S(1)}, bf16[128,1024]{1,0:T(8,128)(2,1)S(1)}, bf16[128,1024]{1,0:T(8,128)(2,1)S(1)}, bf16[128,1024]{1,0:T(8,128)(2,1)S(1)}) custom-call(s32[14]{0:T(128)S(1)} %pad_add_fusion.s_ref, bf16[512,768]{1,0:T(8,128)(2,1)S(1)} %shard_map.78.refs_0_, bf16[256,768]{1,0:T(8,128)(2,1)S(1)} %shard_map.81.refs_1_, ...), custom_call_target="tpu_custom_call" | custom-call | flops 40265318400 | bytes 3407872 | tf_op jit(solution)/shard_map/pallas_call | solution.py:24
  44.2 0.7 %collective-permute-start.15 = (bf16[128,1024]{1,0:T(8,128)(2,1)S(1)}, bf16[128,1024]{1,0:T(8,128)(2,1)S(1)}, u32[]{:S(2)}, u32[]{:S(2)}) collective-permute-start(bf16[128,1024]{1,0:T(8,128)(2,1)S(1)} %get-tuple-element.29), channel_id=1, source_target_pairs={{0,1},{1,0},{2,3},{3,2},{4,5},{5,4},{6,7},{7,6},{8,9},{9,8},{10,11... | collective-permute-start | bytes 786440 | tf_op jit(solution)/shard_map/ppermute | solution.py:50
  44.9 1.2 %collective-permute-start.16 = (bf16[128,1024]{1,0:T(8,128)(2,1)S(1)}, bf16[128,1024]{1,0:T(8,128)(2,1)S(1)}, u32[]{:S(2)}, u32[]{:S(2)}) collective-permute-start(bf16[128,1024]{1,0:T(8,128)(2,1)S(1)} %get-tuple-element.30), channel_id=1, source_target_pairs={{0,2},{1,3},{2,0},{3,1},{4,6},{5,7},{6,4},{7,5},{8,10},{9,11},{10,... | collective-permute-start | bytes 786440 | tf_op jit(solution)/shard_map/ppermute | solution.py:50
  46.2 1.6 %collective-permute-start.17 = (bf16[128,1024]{1,0:T(8,128)(2,1)S(1)}, bf16[128,1024]{1,0:T(8,128)(2,1)S(1)}, u32[]{:S(2)}, u32[]{:S(2)}) collective-permute-start(bf16[128,1024]{1,0:T(8,128)(2,1)S(1)} %get-tuple-element.31), channel_id=1, source_target_pairs={{0,3},{1,2},{2,1},{3,0},{4,7},{5,6},{6,5},{7,4},{8,11},{9,10},{10,... | collective-permute-start | bytes 786440 | tf_op jit(solution)/shard_map/ppermute | solution.py:50
  47.7 7.0 %collective-permute-done.7.refs_5_ = bf16[2,128,512]{2,1,0:T(8,128)(2,1)S(1)} collective-permute-done((bf16[2,128,512]{2,1,0:T(8,128)(2,1)S(1)}, bf16[2,128,512]{2,1,0:T(8,128)(2,1)S(1)}, u32[]{:S(2)}, u32[]{:S(2)}) %collective-permute-start.7) | collective-permute-done | bytes 262176 | tf_op jit(solution)/shard_map/ppermute | solution.py:50
  54.7 0.0 collective-permute-done.3.refs_1_
  54.7 1.0 %shard_map.80 = (f32[128,768]{1,0:T(8,128)S(1)}, bf16[128,768]{1,0:T(8,128)(2,1)S(1)}, bf16[128,768]{1,0:T(8,128)(2,1)S(1)}, bf16[128,768]{1,0:T(8,128)(2,1)S(1)}) custom-call(bf16[512,768]{1,0:T(8,128)(2,1)S(1)} %shard_map.78.refs_0_, bf16[512,768]{1,0:T(8,128)(2,1)S(1)} %collective-permute-done.3.refs_1_, bf16[2,128,512]{2,1,0:T(8,128)(2,1)S(1)} %shard_map.79.refs_2_, ...), custom_call_target="tpu_custom_call" | custom-call | flops 805306368 | bytes 3604480 | tf_op jit(solution)/shard_map/pallas_call | solution.py:24
  55.8 0.6 collective-permute-start.8
  56.4 1.5 %collective-permute-start.9 = (bf16[128,768]{1,0:T(8,128)(2,1)S(1)}, bf16[128,768]{1,0:T(8,128)(2,1)S(1)}, u32[]{:S(2)}, u32[]{:S(2)}) collective-permute-start(bf16[128,768]{1,0:T(8,128)(2,1)S(1)} %get-tuple-element.25), channel_id=1, source_target_pairs={{0,16},{4,20},{8,24},{12,28},{16,0},{20,4},{24,8},{28,12},{1,17},{... | collective-permute-start | bytes 589832 | tf_op jit(solution)/shard_map/ppermute | solution.py:50
  57.9 1.0 %collective-permute-done.15.refs_4_ = bf16[128,1024]{1,0:T(8,128)(2,1)S(1)} collective-permute-done((bf16[128,1024]{1,0:T(8,128)(2,1)S(1)}, bf16[128,1024]{1,0:T(8,128)(2,1)S(1)}, u32[]{:S(2)}, u32[]{:S(2)}) %collective-permute-start.15) | collective-permute-done | bytes 262176 | tf_op jit(solution)/shard_map/ppermute | solution.py:50
  58.9 1.5 %collective-permute-start.10 = (bf16[128,768]{1,0:T(8,128)(2,1)S(1)}, bf16[128,768]{1,0:T(8,128)(2,1)S(1)}, u32[]{:S(2)}, u32[]{:S(2)}) collective-permute-start(bf16[128,768]{1,0:T(8,128)(2,1)S(1)} %get-tuple-element.26), channel_id=1, source_target_pairs={{0,24},{4,28},{8,16},{12,20},{16,8},{20,12},{24,0},{28,4},{1,25},{... | collective-permute-start | bytes 589832 | tf_op jit(solution)/shard_map/ppermute | solution.py:50
  60.4 0.6 collective-permute-done.16.refs_5_
  60.9 8.8 %collective-permute-done.17.refs_6_ = bf16[128,1024]{1,0:T(8,128)(2,1)S(1)} collective-permute-done((bf16[128,1024]{1,0:T(8,128)(2,1)S(1)}, bf16[128,1024]{1,0:T(8,128)(2,1)S(1)}, u32[]{:S(2)}, u32[]{:S(2)}) %collective-permute-start.17) | collective-permute-done | bytes 262176 | tf_op jit(solution)/shard_map/ppermute | solution.py:50
  69.7 0.0 collective-permute-done.8.refs_0_
  69.7 0.0 collective-permute-done.9.refs_1_
  69.7 0.0 collective-permute-done.10.refs_2_
  69.7 1.0 %shard_map.83 = (f32[128,768]{1,0:T(8,128)}, bf16[128,1024]{1,0:T(8,128)(2,1)}) custom-call(f32[128,768]{1,0:T(8,128)S(1)} %get-tuple-element.23.own_ref, bf16[128,768]{1,0:T(8,128)(2,1)S(1)} %collective-permute-done.8.refs_0_, bf16[128,768]{1,0:T(8,128)(2,1)S(1)} %collective-permute-done.9.refs_1_, bf16[128,768]{1,0:T(8,128)(2,1)S(1)} %collective-permute-done.10.refs_2_, ...), custom_call_target="tpu_custom_call" | custom-call | bytes 2686976 | tf_op jit(solution)/shard_map/pallas_call | solution.py:24
  (8 shorter events, 0.0 us)
Async XLA Ops:
  0.6 4.4 %collective-permute-start.4 = (bf16[128,1024]{1,0:T(8,128)(2,1)}, bf16[128,1024]{1,0:T(8,128)(2,1)S(1)}, u32[]{:S(2)}, u32[]{:S(2)}) collective-permute-start(bf16[128,1024]{1,0:T(8,128)(2,1)} %bitcast.10), channel_id=1, source_target_pairs={{0,4},{4,0},{8,12},{12,8},{16,20},{20,16},{24,28},{28,24},{1,5},{5... | collective-permute-start | bytes 786440 | tf_op jit(solution)/shard_map/ppermute | solution.py:50
  0.7 1.1 %copy-start = (bf16[1,128,3072]{2,1,0:T(8,128)(2,1)S(1)}, bf16[1,128,3072]{2,1,0:T(8,128)(2,1)}, u32[]{:S(2)}) copy-start(bf16[1,128,3072]{2,1,0:T(8,128)(2,1)} %param.7) | copy-start | bytes 2359300
  1.8 0.9 %copy-start.1 = (bf16[1,128,1024]{2,1,0:T(8,128)(2,1)S(1)}, bf16[1,128,1024]{2,1,0:T(8,128)(2,1)}, u32[]{:S(2)}) copy-start(bf16[1,128,1024]{2,1,0:T(8,128)(2,1)} %param.8) | copy-start | bytes 786436
  2.8 2.2 %copy-start.2 = (bf16[1,128,1024]{2,1,0:T(8,128)(2,1)S(1)}, bf16[1,128,1024]{2,1,0:T(8,128)(2,1)}, u32[]{:S(2)}) copy-start(bf16[1,128,1024]{2,1,0:T(8,128)(2,1)} %param.6) | copy-start | bytes 786436
  3.0 12.6 %collective-permute-start = (bf16[128,1024]{1,0:T(8,128)(2,1)S(1)}, bf16[128,1024]{1,0:T(8,128)(2,1)S(1)}, u32[]{:S(2)}, u32[]{:S(2)}) collective-permute-start(bf16[128,1024]{1,0:T(8,128)(2,1)S(1)} %get-tuple-element.19), channel_id=1, source_target_pairs={{0,1},{1,0},{2,3},{3,2},{4,5},{5,4},{6,7},{7,6},{8,9},{9,8},{10,11... | collective-permute-start | bytes 786440 | tf_op jit(solution)/shard_map/ppermute | solution.py:50
  4.7 13.1 %collective-permute-start.1 = (bf16[128,1024]{1,0:T(8,128)(2,1)S(1)}, bf16[128,1024]{1,0:T(8,128)(2,1)S(1)}, u32[]{:S(2)}, u32[]{:S(2)}) collective-permute-start(bf16[128,1024]{1,0:T(8,128)(2,1)S(1)} %get-tuple-element.20), channel_id=1, source_target_pairs={{0,2},{1,3},{2,0},{3,1},{4,6},{5,7},{6,4},{7,5},{8,10},{9,11},{10,... | collective-permute-start | bytes 786440 | tf_op jit(solution)/shard_map/ppermute | solution.py:50
  5.0 3.3 %copy-start.3 = (bf16[128,768]{1,0:T(8,128)(2,1)S(1)}, bf16[128,768]{1,0:T(8,128)(2,1)}, u32[]{:S(2)}) copy-start(bf16[128,768]{1,0:T(8,128)(2,1)} %own_ref.1) | copy-start | bytes 589828
  5.1 18.4 %collective-permute-start.5 = (bf16[2,128,512]{2,1,0:T(8,128)(2,1)S(1)}, bf16[2,128,512]{2,1,0:T(8,128)(2,1)S(1)}, u32[]{:S(2)}, u32[]{:S(2)}) collective-permute-start(bf16[2,128,512]{2,1,0:T(8,128)(2,1)S(1)} %shard_map.79.refs_2_), channel_id=1, source_target_pairs={{0,1},{1,0},{2,3},{3,2},{4,5},{5,4},{6,7},{7,6},{8,9},{9,8},{10,11... | collective-permute-start | bytes 786440 | tf_op jit(solution)/shard_map/ppermute | solution.py:50
  5.6 30.6 %collective-permute-start.2 = (bf16[128,1024]{1,0:T(8,128)(2,1)S(1)}, bf16[128,1024]{1,0:T(8,128)(2,1)S(1)}, u32[]{:S(2)}, u32[]{:S(2)}) collective-permute-start(bf16[128,1024]{1,0:T(8,128)(2,1)S(1)} %get-tuple-element.21), channel_id=1, source_target_pairs={{0,3},{1,2},{2,1},{3,0},{4,7},{5,6},{6,5},{7,4},{8,11},{9,10},{10,... | collective-permute-start | bytes 786440 | tf_op jit(solution)/shard_map/ppermute | solution.py:50
  8.3 1.4 %collective-permute-start.11 = (bf16[128,768]{1,0:T(8,128)(2,1)S(1)}, bf16[128,768]{1,0:T(8,128)(2,1)S(1)}, u32[]{:S(2)}, u32[]{:S(2)}) collective-permute-start(bf16[128,768]{1,0:T(8,128)(2,1)S(1)} %copy-done.3), channel_id=1, source_target_pairs={{0,4},{4,0},{8,12},{12,8},{16,20},{20,16},{24,28},{28,24},{1,5},{5... | collective-permute-start | bytes 589832 | tf_op jit(solution)/shard_map/ppermute | solution.py:50
  8.3 0.7 copy-start.4
  8.3 0.7 copy-start.5
  9.8 32.8 %collective-permute-start.14 = (bf16[256,768]{1,0:T(8,128)(2,1)S(1)}, bf16[256,768]{1,0:T(8,128)(2,1)S(1)}, u32[]{:S(2)}, u32[]{:S(2)}) collective-permute-start(bf16[256,768]{1,0:T(8,128)(2,1)S(1)} %shard_map.81.refs_1_), channel_id=1, source_target_pairs={{0,24},{4,28},{8,16},{12,20},{16,8},{20,12},{24,0},{28,4},{1,25},{... | collective-permute-start | bytes 1179656 | tf_op jit(solution)/shard_map/ppermute | solution.py:50
  15.7 26.9 %collective-permute-start.13 = (bf16[256,768]{1,0:T(8,128)(2,1)S(1)}, bf16[256,768]{1,0:T(8,128)(2,1)S(1)}, u32[]{:S(2)}, u32[]{:S(2)}) collective-permute-start(bf16[256,768]{1,0:T(8,128)(2,1)S(1)} %shard_map.81.refs_1_), channel_id=1, source_target_pairs={{0,16},{4,20},{8,24},{12,28},{16,0},{20,4},{24,8},{28,12},{1,17},{... | collective-permute-start | bytes 1179656 | tf_op jit(solution)/shard_map/ppermute | solution.py:50
  17.8 24.8 %collective-permute-start.12 = (bf16[256,768]{1,0:T(8,128)(2,1)S(1)}, bf16[256,768]{1,0:T(8,128)(2,1)S(1)}, u32[]{:S(2)}, u32[]{:S(2)}) collective-permute-start(bf16[256,768]{1,0:T(8,128)(2,1)S(1)} %shard_map.81.refs_1_), channel_id=1, source_target_pairs={{0,8},{4,12},{8,0},{12,4},{16,24},{20,28},{24,16},{28,20},{1,9},{5... | collective-permute-start | bytes 1179656 | tf_op jit(solution)/shard_map/ppermute | solution.py:50
  23.5 17.7 %collective-permute-start.6 = (bf16[2,128,512]{2,1,0:T(8,128)(2,1)S(1)}, bf16[2,128,512]{2,1,0:T(8,128)(2,1)S(1)}, u32[]{:S(2)}, u32[]{:S(2)}) collective-permute-start(bf16[2,128,512]{2,1,0:T(8,128)(2,1)S(1)} %shard_map.79.refs_2_), channel_id=1, source_target_pairs={{0,2},{1,3},{2,0},{3,1},{4,6},{5,7},{6,4},{7,5},{8,10},{9,11},{10,... | collective-permute-start | bytes 786440 | tf_op jit(solution)/shard_map/ppermute | solution.py:50
  41.1 13.7 %collective-permute-start.3 = (bf16[512,768]{1,0:T(8,128)(2,1)S(1)}, bf16[512,768]{1,0:T(8,128)(2,1)S(1)}, u32[]{:S(2)}, u32[]{:S(2)}) collective-permute-start(bf16[512,768]{1,0:T(8,128)(2,1)S(1)} %shard_map.78.refs_0_), channel_id=1, source_target_pairs={{0,4},{4,0},{8,12},{12,8},{16,20},{20,16},{24,28},{28,24},{1,5},{5... | collective-permute-start | bytes 2359304 | tf_op jit(solution)/shard_map/ppermute | solution.py:50
  41.2 13.6 %collective-permute-start.7 = (bf16[2,128,512]{2,1,0:T(8,128)(2,1)S(1)}, bf16[2,128,512]{2,1,0:T(8,128)(2,1)S(1)}, u32[]{:S(2)}, u32[]{:S(2)}) collective-permute-start(bf16[2,128,512]{2,1,0:T(8,128)(2,1)S(1)} %collective-permute-done.6.refs_4_), channel_id=1, source_target_pairs={{0,1},{1,0},{2,3},{3,2},{4,5},{5,4},{6,7},{7,6},{8,9},{9,8},{10,11... | collective-permute-start | bytes 786440 | tf_op jit(solution)/shard_map/ppermute | solution.py:50
  44.2 14.7 %collective-permute-start.15 = (bf16[128,1024]{1,0:T(8,128)(2,1)S(1)}, bf16[128,1024]{1,0:T(8,128)(2,1)S(1)}, u32[]{:S(2)}, u32[]{:S(2)}) collective-permute-start(bf16[128,1024]{1,0:T(8,128)(2,1)S(1)} %get-tuple-element.29), channel_id=1, source_target_pairs={{0,1},{1,0},{2,3},{3,2},{4,5},{5,4},{6,7},{7,6},{8,9},{9,8},{10,11... | collective-permute-start | bytes 786440 | tf_op jit(solution)/shard_map/ppermute | solution.py:50
  44.9 16.0 %collective-permute-start.16 = (bf16[128,1024]{1,0:T(8,128)(2,1)S(1)}, bf16[128,1024]{1,0:T(8,128)(2,1)S(1)}, u32[]{:S(2)}, u32[]{:S(2)}) collective-permute-start(bf16[128,1024]{1,0:T(8,128)(2,1)S(1)} %get-tuple-element.30), channel_id=1, source_target_pairs={{0,2},{1,3},{2,0},{3,1},{4,6},{5,7},{6,4},{7,5},{8,10},{9,11},{10,... | collective-permute-start | bytes 786440 | tf_op jit(solution)/shard_map/ppermute | solution.py:50
  46.2 23.5 %collective-permute-start.17 = (bf16[128,1024]{1,0:T(8,128)(2,1)S(1)}, bf16[128,1024]{1,0:T(8,128)(2,1)S(1)}, u32[]{:S(2)}, u32[]{:S(2)}) collective-permute-start(bf16[128,1024]{1,0:T(8,128)(2,1)S(1)} %get-tuple-element.31), channel_id=1, source_target_pairs={{0,3},{1,2},{2,1},{3,0},{4,7},{5,6},{6,5},{7,4},{8,11},{9,10},{10,... | collective-permute-start | bytes 786440 | tf_op jit(solution)/shard_map/ppermute | solution.py:50
  55.8 13.9 %collective-permute-start.8 = (bf16[128,768]{1,0:T(8,128)(2,1)S(1)}, bf16[128,768]{1,0:T(8,128)(2,1)S(1)}, u32[]{:S(2)}, u32[]{:S(2)}) collective-permute-start(bf16[128,768]{1,0:T(8,128)(2,1)S(1)} %get-tuple-element.24), channel_id=1, source_target_pairs={{0,8},{4,12},{8,0},{12,4},{16,24},{20,28},{24,16},{28,20},{1,9},{5... | collective-permute-start | bytes 589832 | tf_op jit(solution)/shard_map/ppermute | solution.py:50
  56.4 13.3 %collective-permute-start.9 = (bf16[128,768]{1,0:T(8,128)(2,1)S(1)}, bf16[128,768]{1,0:T(8,128)(2,1)S(1)}, u32[]{:S(2)}, u32[]{:S(2)}) collective-permute-start(bf16[128,768]{1,0:T(8,128)(2,1)S(1)} %get-tuple-element.25), channel_id=1, source_target_pairs={{0,16},{4,20},{8,24},{12,28},{16,0},{20,4},{24,8},{28,12},{1,17},{... | collective-permute-start | bytes 589832 | tf_op jit(solution)/shard_map/ppermute | solution.py:50
  58.9 10.9 %collective-permute-start.10 = (bf16[128,768]{1,0:T(8,128)(2,1)S(1)}, bf16[128,768]{1,0:T(8,128)(2,1)S(1)}, u32[]{:S(2)}, u32[]{:S(2)}) collective-permute-start(bf16[128,768]{1,0:T(8,128)(2,1)S(1)} %get-tuple-element.26), channel_id=1, source_target_pairs={{0,24},{4,28},{8,16},{12,20},{16,8},{20,12},{24,0},{28,4},{1,25},{... | collective-permute-start | bytes 589832 | tf_op jit(solution)/shard_map/ppermute | solution.py:50

commit v5 on v4

--- a/solution.py
+++ b/solution.py
@@ -276,7 +276,7 @@
     tokens = {0: half_columns(me_dp, layer_input[0], swap(layer_input[0], "dp", 1), dp_count)}
     mask = ctx_count // 2
     tokens[0] = tokens[0]
-    near = swap(tokens[0], "ctx", 1)
+    near = swap(after(tokens[0], pair), "ctx", 1)
     tokens[0] = after(tokens[0], near, arrived[1], arrived[2])
     while mask > 1:
         for r in sorted(tokens):

time: 72 us -> 72.2 us (level)
  local copies, waits for them, and re-layouts: 2.75 us -> 3.66 us
    unnamed x12, local copies, waits for them, and re-layouts: 2.75 us -> 3.66 us
  transfers between devices with their start and end apart: 18 -> 18, of which waited for: 9 -> 8; matrix products, arithmetic and copies ran while one was open for 0% -> 0% of each run, Pallas kernels for 11% -> 11%
where the time goes in v5:
time: 72.2 us; the launch traced here: 71.2 us
  waiting for transfers between devices  40.4 us (56%)
  starting transfers between devices  17.5 us (24%)
  Pallas kernels  8.76 us (12%)
  local copies, waits for them, and re-layouts  3.66 us (5%)
  between operations  0.73 us (1%)
    ppermute x18, waiting for transfers between devices, swap(): return lax.ppermute(array, axis, [(i, i ^ mask) for i in range(count)])  40.4 us
    ppermute x18, starting transfers between devices, swap(): return lax.ppermute(array, axis, [(i, i ^ mask) for i in range(count)])  17.5 us
    pallas_call x7, Pallas kernels, call(): pl.pallas_call(kernel, out_shape=list(outs), in_specs=[pl.BlockSpec(memor...  8.76 us
    unnamed x12, local copies, waits for them, and re-layouts  3.66 us
  transfers between devices with their start and end apart: 18, of which 8 were waited for; matrix products, arithmetic and copies ran while one was open for 0% of the time, Pallas kernels for 11%

profile of v5, /device:TPU:18, one launch (start us, length us, event | category | flops | bytes accessed | tf_op | source)
XLA Modules:
  0.0 71.2 jit_solution(1970780548473510053)
XLA Ops:
  0.6 0.1 collective-permute-start.4
  0.7 0.5 collective-permute-start.5
  1.2 1.1 %copy-done = bf16[1,128,3072]{2,1,0:T(8,128)(2,1)S(1)} copy-done((bf16[1,128,3072]{2,1,0:T(8,128)(2,1)S(1)}, bf16[1,128,3072]{2,1,0:T(8,128)(2,1)}, u32[]{:S(2)}) %copy-start) | copy-done | bytes 786456
  2.3 0.9 %copy-done.1 = bf16[1,128,1024]{2,1,0:T(8,128)(2,1)S(1)} copy-done((bf16[1,128,1024]{2,1,0:T(8,128)(2,1)S(1)}, bf16[1,128,1024]{2,1,0:T(8,128)(2,1)}, u32[]{:S(2)}) %copy-start.1) | copy-done | bytes 262168
  3.3 0.2 shard_map.77
  3.5 1.6 %collective-permute-start = (bf16[128,1024]{1,0:T(8,128)(2,1)S(1)}, bf16[128,1024]{1,0:T(8,128)(2,1)S(1)}, u32[]{:S(2)}, u32[]{:S(2)}) collective-permute-start(bf16[128,1024]{1,0:T(8,128)(2,1)S(1)} %get-tuple-element.20), channel_id=1, source_target_pairs={{0,1},{1,0},{2,3},{3,2},{4,5},{5,4},{6,7},{7,6},{8,9},{9,8},{10,11... | collective-permute-start | bytes 786440 | tf_op jit(solution)/shard_map/ppermute | solution.py:50
  5.2 0.3 collective-permute-start.1
  5.5 0.0 collective-permute-done.5.other_ref
  5.6 0.0 collective-permute-done.4.other_ref
  5.6 0.9 %copy-done.2 = bf16[1,128,1024]{2,1,0:T(8,128)(2,1)S(1)} copy-done((bf16[1,128,1024]{2,1,0:T(8,128)(2,1)S(1)}, bf16[1,128,1024]{2,1,0:T(8,128)(2,1)}, u32[]{:S(2)}) %copy-start.2) | copy-done | bytes 262168
  6.5 0.1 shard_map.79.refs_2_
  6.5 0.5 collective-permute-start.6
  7.1 2.7 %collective-permute-start.2 = (bf16[128,1024]{1,0:T(8,128)(2,1)S(1)}, bf16[128,1024]{1,0:T(8,128)(2,1)S(1)}, u32[]{:S(2)}, u32[]{:S(2)}) collective-permute-start(bf16[128,1024]{1,0:T(8,128)(2,1)S(1)} %get-tuple-element.22), channel_id=1, source_target_pairs={{0,3},{1,2},{2,1},{3,0},{4,7},{5,6},{6,5},{7,4},{8,11},{9,10},{10,... | collective-permute-start | bytes 786440 | tf_op jit(solution)/shard_map/ppermute | solution.py:50
  9.8 0.7 copy-done.4
  10.4 0.0 copy-done.5
  10.4 0.1 pad_add_fusion.s_ref
  10.5 0.5 collective-permute-start.12
  11.1 5.2 %collective-permute-done.refs_1_ = bf16[128,1024]{1,0:T(8,128)(2,1)S(1)} collective-permute-done((bf16[128,1024]{1,0:T(8,128)(2,1)S(1)}, bf16[128,1024]{1,0:T(8,128)(2,1)S(1)}, u32[]{:S(2)}, u32[]{:S(2)}) %collective-permute-start) | collective-permute-done | bytes 262176 | tf_op jit(solution)/shard_map/ppermute | solution.py:50
  16.2 1.5 %collective-permute-start.13 = (bf16[256,768]{1,0:T(8,128)(2,1)S(1)}, bf16[256,768]{1,0:T(8,128)(2,1)S(1)}, u32[]{:S(2)}, u32[]{:S(2)}) collective-permute-start(bf16[256,768]{1,0:T(8,128)(2,1)S(1)} %shard_map.80.refs_1_), channel_id=1, source_target_pairs={{0,16},{4,20},{8,24},{12,28},{16,0},{20,4},{24,8},{28,12},{1,17},{... | collective-permute-start | bytes 1179656 | tf_op jit(solution)/shard_map/ppermute | solution.py:50
  17.8 0.6 collective-permute-done.1.refs_2_
  18.3 1.5 %collective-permute-start.14 = (bf16[256,768]{1,0:T(8,128)(2,1)S(1)}, bf16[256,768]{1,0:T(8,128)(2,1)S(1)}, u32[]{:S(2)}, u32[]{:S(2)}) collective-permute-start(bf16[256,768]{1,0:T(8,128)(2,1)S(1)} %shard_map.80.refs_1_), channel_id=1, source_target_pairs={{0,24},{4,28},{8,16},{12,20},{16,8},{20,12},{24,0},{28,4},{1,25},{... | collective-permute-start | bytes 1179656 | tf_op jit(solution)/shard_map/ppermute | solution.py:50
  19.8 4.2 %collective-permute-done.6.refs_3_ = bf16[2,128,512]{2,1,0:T(8,128)(2,1)S(1)} collective-permute-done((bf16[2,128,512]{2,1,0:T(8,128)(2,1)S(1)}, bf16[2,128,512]{2,1,0:T(8,128)(2,1)S(1)}, u32[]{:S(2)}, u32[]{:S(2)}) %collective-permute-start.6) | collective-permute-done | bytes 262176 | tf_op jit(solution)/shard_map/ppermute | solution.py:50
  24.1 0.0 collective-permute-start.7
  24.1 12.7 %collective-permute-done.2.refs_3_ = bf16[128,1024]{1,0:T(8,128)(2,1)S(1)} collective-permute-done((bf16[128,1024]{1,0:T(8,128)(2,1)S(1)}, bf16[128,1024]{1,0:T(8,128)(2,1)S(1)}, u32[]{:S(2)}, u32[]{:S(2)}) %collective-permute-start.2) | collective-permute-done | bytes 262176 | tf_op jit(solution)/shard_map/ppermute | solution.py:50
  36.7 4.8 %shard_map.78.refs_0_ = bf16[512,768]{1,0:T(8,128)(2,1)S(1)} custom-call(s32[14]{0:T(128)S(1)} %pad_add_fusion.s_ref, bf16[128,1024]{1,0:T(8,128)(2,1)S(1)} %get-tuple-element.19.refs_0_, bf16[128,1024]{1,0:T(8,128)(2,1)S(1)} %collective-permute-done.refs_1_, bf16[128,1024]{1,0:T(8,128)(2,1)S(1)} %collective-permute-done.1.refs_2_, ...), custom_call_target="tpu_custom_call" | custom-call | flops 9663676416 | bytes 1835008 | tf_op jit(solution)/shard_map/pallas_call | solution.py:24
  41.6 0.1 collective-permute-start.3
  41.7 0.0 collective-permute-done.7.refs_4_
  41.7 1.0 %collective-permute-start.8 = (bf16[2,128,512]{2,1,0:T(8,128)(2,1)S(1)}, bf16[2,128,512]{2,1,0:T(8,128)(2,1)S(1)}, u32[]{:S(2)}, u32[]{:S(2)}) collective-permute-start(bf16[2,128,512]{2,1,0:T(8,128)(2,1)S(1)} %collective-permute-done.7.refs_4_), channel_id=1, source_target_pairs={{0,1},{1,0},{2,3},{3,2},{4,5},{5,4},{6,7},{7,6},{8,9},{9,8},{10,11... | collective-permute-start | bytes 786440 | tf_op jit(solution)/shard_map/ppermute | solution.py:50
  42.7 0.0 collective-permute-done.12.refs_2_
  42.7 0.0 collective-permute-done.13.refs_3_
  42.7 0.0 collective-permute-done.14.refs_4_
  42.7 1.6 %shard_map.82 = (bf16[128,1024]{1,0:T(8,128)(2,1)S(1)}, bf16[128,1024]{1,0:T(8,128)(2,1)S(1)}, bf16[128,1024]{1,0:T(8,128)(2,1)S(1)}, bf16[128,1024]{1,0:T(8,128)(2,1)S(1)}) custom-call(s32[14]{0:T(128)S(1)} %pad_add_fusion.s_ref, bf16[512,768]{1,0:T(8,128)(2,1)S(1)} %shard_map.78.refs_0_, bf16[256,768]{1,0:T(8,128)(2,1)S(1)} %shard_map.80.refs_1_, ...), custom_call_target="tpu_custom_call" | custom-call | flops 40265318400 | bytes 3407872 | tf_op jit(solution)/shard_map/pallas_call | solution.py:24
  44.3 1.2 %collective-permute-start.15 = (bf16[128,1024]{1,0:T(8,128)(2,1)S(1)}, bf16[128,1024]{1,0:T(8,128)(2,1)S(1)}, u32[]{:S(2)}, u32[]{:S(2)}) collective-permute-start(bf16[128,1024]{1,0:T(8,128)(2,1)S(1)} %get-tuple-element.31), channel_id=1, source_target_pairs={{0,1},{1,0},{2,3},{3,2},{4,5},{5,4},{6,7},{7,6},{8,9},{9,8},{10,11... | collective-permute-start | bytes 786440 | tf_op jit(solution)/shard_map/ppermute | solution.py:50
  45.4 0.8 %collective-permute-start.16 = (bf16[128,1024]{1,0:T(8,128)(2,1)S(1)}, bf16[128,1024]{1,0:T(8,128)(2,1)S(1)}, u32[]{:S(2)}, u32[]{:S(2)}) collective-permute-start(bf16[128,1024]{1,0:T(8,128)(2,1)S(1)} %get-tuple-element.32), channel_id=1, source_target_pairs={{0,2},{1,3},{2,0},{3,1},{4,6},{5,7},{6,4},{7,5},{8,10},{9,11},{10,... | collective-permute-start | bytes 786440 | tf_op jit(solution)/shard_map/ppermute | solution.py:50
  46.2 1.6 %collective-permute-start.17 = (bf16[128,1024]{1,0:T(8,128)(2,1)S(1)}, bf16[128,1024]{1,0:T(8,128)(2,1)S(1)}, u32[]{:S(2)}, u32[]{:S(2)}) collective-permute-start(bf16[128,1024]{1,0:T(8,128)(2,1)S(1)} %get-tuple-element.33), channel_id=1, source_target_pairs={{0,3},{1,2},{2,1},{3,0},{4,7},{5,6},{6,5},{7,4},{8,11},{9,10},{10,... | collective-permute-start | bytes 786440 | tf_op jit(solution)/shard_map/ppermute | solution.py:50
  47.8 0.0 collective-permute-done.3.refs_1_
  47.8 7.1 %collective-permute-done.8.refs_5_ = bf16[2,128,512]{2,1,0:T(8,128)(2,1)S(1)} collective-permute-done((bf16[2,128,512]{2,1,0:T(8,128)(2,1)S(1)}, bf16[2,128,512]{2,1,0:T(8,128)(2,1)S(1)}, u32[]{:S(2)}, u32[]{:S(2)}) %collective-permute-start.8) | collective-permute-done | bytes 262176 | tf_op jit(solution)/shard_map/ppermute | solution.py:50
  54.9 1.0 %shard_map.81 = (f32[128,768]{1,0:T(8,128)S(1)}, bf16[128,768]{1,0:T(8,128)(2,1)S(1)}, bf16[128,768]{1,0:T(8,128)(2,1)S(1)}, bf16[128,768]{1,0:T(8,128)(2,1)S(1)}) custom-call(bf16[512,768]{1,0:T(8,128)(2,1)S(1)} %shard_map.78.refs_0_, bf16[512,768]{1,0:T(8,128)(2,1)S(1)} %collective-permute-done.3.refs_1_, bf16[2,128,512]{2,1,0:T(8,128)(2,1)S(1)} %shard_map.79.refs_2_, ...), custom_call_target="tpu_custom_call" | custom-call | flops 805306368 | bytes 3604480 | tf_op jit(solution)/shard_map/pallas_call | solution.py:24
  55.9 0.6 collective-permute-start.9
  56.5 1.5 %collective-permute-start.10 = (bf16[128,768]{1,0:T(8,128)(2,1)S(1)}, bf16[128,768]{1,0:T(8,128)(2,1)S(1)}, u32[]{:S(2)}, u32[]{:S(2)}) collective-permute-start(bf16[128,768]{1,0:T(8,128)(2,1)S(1)} %get-tuple-element.28), channel_id=1, source_target_pairs={{0,16},{4,20},{8,24},{12,28},{16,0},{20,4},{24,8},{28,12},{1,17},{... | collective-permute-start | bytes 589832 | tf_op jit(solution)/shard_map/ppermute | solution.py:50
  58.0 1.4 %collective-permute-done.15.refs_4_ = bf16[128,1024]{1,0:T(8,128)(2,1)S(1)} collective-permute-done((bf16[128,1024]{1,0:T(8,128)(2,1)S(1)}, bf16[128,1024]{1,0:T(8,128)(2,1)S(1)}, u32[]{:S(2)}, u32[]{:S(2)}) %collective-permute-start.15) | collective-permute-done | bytes 262176 | tf_op jit(solution)/shard_map/ppermute | solution.py:50
  59.5 1.5 %collective-permute-start.11 = (bf16[128,768]{1,0:T(8,128)(2,1)S(1)}, bf16[128,768]{1,0:T(8,128)(2,1)S(1)}, u32[]{:S(2)}, u32[]{:S(2)}) collective-permute-start(bf16[128,768]{1,0:T(8,128)(2,1)S(1)} %get-tuple-element.29), channel_id=1, source_target_pairs={{0,24},{4,28},{8,16},{12,20},{16,8},{20,12},{24,0},{28,4},{1,25},{... | collective-permute-start | bytes 589832 | tf_op jit(solution)/shard_map/ppermute | solution.py:50
  61.0 0.2 collective-permute-done.16.refs_5_
  61.2 9.0 %collective-permute-done.17.refs_6_ = bf16[128,1024]{1,0:T(8,128)(2,1)S(1)} collective-permute-done((bf16[128,1024]{1,0:T(8,128)(2,1)S(1)}, bf16[128,1024]{1,0:T(8,128)(2,1)S(1)}, u32[]{:S(2)}, u32[]{:S(2)}) %collective-permute-start.17) | collective-permute-done | bytes 262176 | tf_op jit(solution)/shard_map/ppermute | solution.py:50
  70.2 0.0 collective-permute-done.9.refs_0_
  70.2 0.0 collective-permute-done.10.refs_1_
  70.2 0.0 collective-permute-done.11.refs_2_
  70.2 1.0 %shard_map.83 = (f32[128,768]{1,0:T(8,128)}, bf16[128,1024]{1,0:T(8,128)(2,1)}) custom-call(f32[128,768]{1,0:T(8,128)S(1)} %get-tuple-element.26.own_ref, bf16[128,768]{1,0:T(8,128)(2,1)S(1)} %collective-permute-done.9.refs_0_, bf16[128,768]{1,0:T(8,128)(2,1)S(1)} %collective-permute-done.10.refs_1_, bf16[128,768]{1,0:T(8,128)(2,1)S(1)} %collective-permute-done.11.refs_2_, ...), custom_call_target="tpu_custom_call" | custom-call | bytes 2686976 | tf_op jit(solution)/shard_map/pallas_call | solution.py:24
  (8 shorter events, 0.0 us)
Async XLA Ops:
  0.6 4.9 %collective-permute-start.4 = (bf16[128,1024]{1,0:T(8,128)(2,1)}, bf16[128,1024]{1,0:T(8,128)(2,1)S(1)}, u32[]{:S(2)}, u32[]{:S(2)}) collective-permute-start(bf16[128,1024]{1,0:T(8,128)(2,1)} %bitcast.10), channel_id=1, source_target_pairs={{0,4},{4,0},{8,12},{12,8},{16,20},{20,16},{24,28},{28,24},{1,5},{5... | collective-permute-start | bytes 786440 | tf_op jit(solution)/shard_map/ppermute | solution.py:50
  0.7 4.8 %collective-permute-start.5 = (bf16[128,768]{1,0:T(8,128)(2,1)}, bf16[128,768]{1,0:T(8,128)(2,1)S(1)}, u32[]{:S(2)}, u32[]{:S(2)}) collective-permute-start(bf16[128,768]{1,0:T(8,128)(2,1)} %own_ref.1), channel_id=1, source_target_pairs={{0,4},{4,0},{8,12},{12,8},{16,20},{20,16},{24,28},{28,24},{1,5},{5... | collective-permute-start | bytes 589832 | tf_op jit(solution)/shard_map/ppermute | solution.py:50
  1.2 1.1 %copy-start = (bf16[1,128,3072]{2,1,0:T(8,128)(2,1)S(1)}, bf16[1,128,3072]{2,1,0:T(8,128)(2,1)}, u32[]{:S(2)}) copy-start(bf16[1,128,3072]{2,1,0:T(8,128)(2,1)} %param.7) | copy-start | bytes 2359300
  2.3 0.9 %copy-start.1 = (bf16[1,128,1024]{2,1,0:T(8,128)(2,1)S(1)}, bf16[1,128,1024]{2,1,0:T(8,128)(2,1)}, u32[]{:S(2)}) copy-start(bf16[1,128,1024]{2,1,0:T(8,128)(2,1)} %param.8) | copy-start | bytes 786436
  3.3 2.2 %copy-start.3 = (bf16[128,768]{1,0:T(8,128)(2,1)S(1)}, bf16[128,768]{1,0:T(8,128)(2,1)}, u32[]{:S(2)}) copy-start(bf16[128,768]{1,0:T(8,128)(2,1)} %own_ref.1) | copy-start | bytes 589828
  3.5 12.7 %collective-permute-start = (bf16[128,1024]{1,0:T(8,128)(2,1)S(1)}, bf16[128,1024]{1,0:T(8,128)(2,1)S(1)}, u32[]{:S(2)}, u32[]{:S(2)}) collective-permute-start(bf16[128,1024]{1,0:T(8,128)(2,1)S(1)} %get-tuple-element.20), channel_id=1, source_target_pairs={{0,1},{1,0},{2,3},{3,2},{4,5},{5,4},{6,7},{7,6},{8,9},{9,8},{10,11... | collective-permute-start | bytes 786440 | tf_op jit(solution)/shard_map/ppermute | solution.py:50
  5.2 13.1 %collective-permute-start.1 = (bf16[128,1024]{1,0:T(8,128)(2,1)S(1)}, bf16[128,1024]{1,0:T(8,128)(2,1)S(1)}, u32[]{:S(2)}, u32[]{:S(2)}) collective-permute-start(bf16[128,1024]{1,0:T(8,128)(2,1)S(1)} %get-tuple-element.21), channel_id=1, source_target_pairs={{0,2},{1,3},{2,0},{3,1},{4,6},{5,7},{6,4},{7,5},{8,10},{9,11},{10,... | collective-permute-start | bytes 786440 | tf_op jit(solution)/shard_map/ppermute | solution.py:50
  5.5 1.0 %copy-start.2 = (bf16[1,128,1024]{2,1,0:T(8,128)(2,1)S(1)}, bf16[1,128,1024]{2,1,0:T(8,128)(2,1)}, u32[]{:S(2)}) copy-start(bf16[1,128,1024]{2,1,0:T(8,128)(2,1)} %param.6) | copy-start | bytes 786436
  6.5 17.5 %collective-permute-start.6 = (bf16[2,128,512]{2,1,0:T(8,128)(2,1)S(1)}, bf16[2,128,512]{2,1,0:T(8,128)(2,1)S(1)}, u32[]{:S(2)}, u32[]{:S(2)}) collective-permute-start(bf16[2,128,512]{2,1,0:T(8,128)(2,1)S(1)} %shard_map.79.refs_2_), channel_id=1, source_target_pairs={{0,1},{1,0},{2,3},{3,2},{4,5},{5,4},{6,7},{7,6},{8,9},{9,8},{10,11... | collective-permute-start | bytes 786440 | tf_op jit(solution)/shard_map/ppermute | solution.py:50
  7.1 29.7 %collective-permute-start.2 = (bf16[128,1024]{1,0:T(8,128)(2,1)S(1)}, bf16[128,1024]{1,0:T(8,128)(2,1)S(1)}, u32[]{:S(2)}, u32[]{:S(2)}) collective-permute-start(bf16[128,1024]{1,0:T(8,128)(2,1)S(1)} %get-tuple-element.22), channel_id=1, source_target_pairs={{0,3},{1,2},{2,1},{3,0},{4,7},{5,6},{6,5},{7,4},{8,11},{9,10},{10,... | collective-permute-start | bytes 786440 | tf_op jit(solution)/shard_map/ppermute | solution.py:50
  9.8 0.7 copy-start.4
  9.8 0.7 copy-start.5
  10.5 32.2 %collective-permute-start.12 = (bf16[256,768]{1,0:T(8,128)(2,1)S(1)}, bf16[256,768]{1,0:T(8,128)(2,1)S(1)}, u32[]{:S(2)}, u32[]{:S(2)}) collective-permute-start(bf16[256,768]{1,0:T(8,128)(2,1)S(1)} %shard_map.80.refs_1_), channel_id=1, source_target_pairs={{0,8},{4,12},{8,0},{12,4},{16,24},{20,28},{24,16},{28,20},{1,9},{5... | collective-permute-start | bytes 1179656 | tf_op jit(solution)/shard_map/ppermute | solution.py:50
  16.2 26.4 %collective-permute-start.13 = (bf16[256,768]{1,0:T(8,128)(2,1)S(1)}, bf16[256,768]{1,0:T(8,128)(2,1)S(1)}, u32[]{:S(2)}, u32[]{:S(2)}) collective-permute-start(bf16[256,768]{1,0:T(8,128)(2,1)S(1)} %shard_map.80.refs_1_), channel_id=1, source_target_pairs={{0,16},{4,20},{8,24},{12,28},{16,0},{20,4},{24,8},{28,12},{1,17},{... | collective-permute-start | bytes 1179656 | tf_op jit(solution)/shard_map/ppermute | solution.py:50
  18.3 24.4 %collective-permute-start.14 = (bf16[256,768]{1,0:T(8,128)(2,1)S(1)}, bf16[256,768]{1,0:T(8,128)(2,1)S(1)}, u32[]{:S(2)}, u32[]{:S(2)}) collective-permute-start(bf16[256,768]{1,0:T(8,128)(2,1)S(1)} %shard_map.80.refs_1_), channel_id=1, source_target_pairs={{0,24},{4,28},{8,16},{12,20},{16,8},{20,12},{24,0},{28,4},{1,25},{... | collective-permute-start | bytes 1179656 | tf_op jit(solution)/shard_map/ppermute | solution.py:50
  24.1 17.6 %collective-permute-start.7 = (bf16[2,128,512]{2,1,0:T(8,128)(2,1)S(1)}, bf16[2,128,512]{2,1,0:T(8,128)(2,1)S(1)}, u32[]{:S(2)}, u32[]{:S(2)}) collective-permute-start(bf16[2,128,512]{2,1,0:T(8,128)(2,1)S(1)} %shard_map.79.refs_2_), channel_id=1, source_target_pairs={{0,2},{1,3},{2,0},{3,1},{4,6},{5,7},{6,4},{7,5},{8,10},{9,11},{10,... | collective-permute-start | bytes 786440 | tf_op jit(solution)/shard_map/ppermute | solution.py:50
  41.6 6.2 %collective-permute-start.3 = (bf16[512,768]{1,0:T(8,128)(2,1)S(1)}, bf16[512,768]{1,0:T(8,128)(2,1)S(1)}, u32[]{:S(2)}, u32[]{:S(2)}) collective-permute-start(bf16[512,768]{1,0:T(8,128)(2,1)S(1)} %shard_map.78.refs_0_), channel_id=1, source_target_pairs={{0,4},{4,0},{8,12},{12,8},{16,20},{20,16},{24,28},{28,24},{1,5},{5... | collective-permute-start | bytes 2359304 | tf_op jit(solution)/shard_map/ppermute | solution.py:50
  41.7 13.2 %collective-permute-start.8 = (bf16[2,128,512]{2,1,0:T(8,128)(2,1)S(1)}, bf16[2,128,512]{2,1,0:T(8,128)(2,1)S(1)}, u32[]{:S(2)}, u32[]{:S(2)}) collective-permute-start(bf16[2,128,512]{2,1,0:T(8,128)(2,1)S(1)} %collective-permute-done.7.refs_4_), channel_id=1, source_target_pairs={{0,1},{1,0},{2,3},{3,2},{4,5},{5,4},{6,7},{7,6},{8,9},{9,8},{10,11... | collective-permute-start | bytes 786440 | tf_op jit(solution)/shard_map/ppermute | solution.py:50
  44.3 15.2 %collective-permute-start.15 = (bf16[128,1024]{1,0:T(8,128)(2,1)S(1)}, bf16[128,1024]{1,0:T(8,128)(2,1)S(1)}, u32[]{:S(2)}, u32[]{:S(2)}) collective-permute-start(bf16[128,1024]{1,0:T(8,128)(2,1)S(1)} %get-tuple-element.31), channel_id=1, source_target_pairs={{0,1},{1,0},{2,3},{3,2},{4,5},{5,4},{6,7},{7,6},{8,9},{9,8},{10,11... | collective-permute-start | bytes 786440 | tf_op jit(solution)/shard_map/ppermute | solution.py:50
  45.4 15.8 %collective-permute-start.16 = (bf16[128,1024]{1,0:T(8,128)(2,1)S(1)}, bf16[128,1024]{1,0:T(8,128)(2,1)S(1)}, u32[]{:S(2)}, u32[]{:S(2)}) collective-permute-start(bf16[128,1024]{1,0:T(8,128)(2,1)S(1)} %get-tuple-element.32), channel_id=1, source_target_pairs={{0,2},{1,3},{2,0},{3,1},{4,6},{5,7},{6,4},{7,5},{8,10},{9,11},{10,... | collective-permute-start | bytes 786440 | tf_op jit(solution)/shard_map/ppermute | solution.py:50
  46.2 24.0 %collective-permute-start.17 = (bf16[128,1024]{1,0:T(8,128)(2,1)S(1)}, bf16[128,1024]{1,0:T(8,128)(2,1)S(1)}, u32[]{:S(2)}, u32[]{:S(2)}) collective-permute-start(bf16[128,1024]{1,0:T(8,128)(2,1)S(1)} %get-tuple-element.33), channel_id=1, source_target_pairs={{0,3},{1,2},{2,1},{3,0},{4,7},{5,6},{6,5},{7,4},{8,11},{9,10},{10,... | collective-permute-start | bytes 786440 | tf_op jit(solution)/shard_map/ppermute | solution.py:50
  55.9 14.3 %collective-permute-start.9 = (bf16[128,768]{1,0:T(8,128)(2,1)S(1)}, bf16[128,768]{1,0:T(8,128)(2,1)S(1)}, u32[]{:S(2)}, u32[]{:S(2)}) collective-permute-start(bf16[128,768]{1,0:T(8,128)(2,1)S(1)} %get-tuple-element.27), channel_id=1, source_target_pairs={{0,8},{4,12},{8,0},{12,4},{16,24},{20,28},{24,16},{28,20},{1,9},{5... | collective-permute-start | bytes 589832 | tf_op jit(solution)/shard_map/ppermute | solution.py:50
  56.5 13.7 %collective-permute-start.10 = (bf16[128,768]{1,0:T(8,128)(2,1)S(1)}, bf16[128,768]{1,0:T(8,128)(2,1)S(1)}, u32[]{:S(2)}, u32[]{:S(2)}) collective-permute-start(bf16[128,768]{1,0:T(8,128)(2,1)S(1)} %get-tuple-element.28), channel_id=1, source_target_pairs={{0,16},{4,20},{8,24},{12,28},{16,0},{20,4},{24,8},{28,12},{1,17},{... | collective-permute-start | bytes 589832 | tf_op jit(solution)/shard_map/ppermute | solution.py:50
  59.5 10.8 %collective-permute-start.11 = (bf16[128,768]{1,0:T(8,128)(2,1)S(1)}, bf16[128,768]{1,0:T(8,128)(2,1)S(1)}, u32[]{:S(2)}, u32[]{:S(2)}) collective-permute-start(bf16[128,768]{1,0:T(8,128)(2,1)S(1)} %get-tuple-element.29), channel_id=1, source_target_pairs={{0,24},{4,28},{8,16},{12,20},{16,8},{20,12},{24,0},{28,4},{1,25},{... | collective-permute-start | bytes 589832 | tf_op jit(solution)/shard_map/ppermute | solution.py:50
